TPU v7x, 32 devices: a whole 2x2x4 slice. The times are simulated.
32 devices in a mesh: row: 4 (over y, core), col: 8 (over z, x).
Axes of the slice: x: 2, y: 2, z: 4, core: 2. Of those that a mesh axis runs over, the one named last changes fastest.
Arguments:
- start_block: bfloat16 [4096, 128], P(('row', 'col')), may hold values from -6 to 6
- matrix_tiles: bfloat16 [4, 4, 8, 2, 128, 128], P('row', None, 'col')
- tile_columns: int32 [4, 4, 8, 2], P('row', None, 'col'), may hold values from 0 to 7
- history: bfloat16 [4096, 512], P(('row', 'col'))
Outputs:
- new_block: float32 [4096, 128], P(('row', 'col'))
- coeffs: float32 [512, 128], replicated
All inputs are finite; a program needn't handle non-finite values.
Results may differ from a plain program's by a relative error of at most 0.0029.
Values may be sent and summed in bfloat16 or wider, within the bound.
No kernel may reach another device: no remote copies, remote signals or barrier semaphores. Data moves between devices by JAX's collectives and lax.ppermute only.
A program may use at most 64 MiB of HBM per device.

v0:
```python
import jax
import jax.numpy as jnp
from jax import lax
from jax.sharding import PartitionSpec as P


def apply_matrix(pieces, matrix_tiles, tile_columns):
    gathered = lax.all_gather(pieces, "col", axis=0, tiled=True)
    tile_order = matrix_tiles.shape[-1]
    block_width = gathered.shape[1]
    column_count = gathered.shape[0] // tile_order
    blocks = gathered.reshape(column_count, tile_order, block_width)
    picked = blocks[tile_columns[0, :, 0, :]]
    local_tiles = matrix_tiles[0, :, 0]
    partial_value = jnp.einsum(
        "rsij,rsjk->rik", local_tiles, picked, preferred_element_type=jnp.float32
    )
    partial_value = partial_value.reshape(partial_value.shape[0] * tile_order, block_width)
    return lax.psum_scatter(partial_value, "row", scatter_dimension=0, tiled=True)


def per_device(start_block, matrix_tiles, tile_columns, history):
    history_wide = history.astype(jnp.float32)
    start_wide = start_block.astype(jnp.float32)
    first_power = apply_matrix(start_block, matrix_tiles, tile_columns).astype(jnp.bfloat16)
    second_power = apply_matrix(first_power, matrix_tiles, tile_columns)
    filtered = 2.0 * second_power - start_wide
    coeffs = lax.psum(
        jnp.dot(history_wide.T, filtered, precision=lax.Precision.HIGHEST), ("row", "col")
    )
    cleaned = filtered - jnp.dot(history_wide, coeffs, precision=lax.Precision.HIGHEST)
    squares = lax.psum(jnp.sum(cleaned * cleaned, axis=0), ("row", "col"))
    row_total = cleaned.shape[0] * lax.axis_size("row") * lax.axis_size("col")
    lengths = jnp.sqrt(squares / row_total + 1e-05)
    return (cleaned / lengths[None, :], coeffs)


def solution(mesh):
    in_specs = (
        P(("row", "col"), None),
        P("row", None, "col", None, None, None),
        P("row", None, "col", None),
        P(("row", "col"), None),
    )
    out_specs = (P(("row", "col"), None), P())
    return jax.shard_map(
        per_device, mesh=mesh, in_specs=in_specs, out_specs=out_specs, check_vma=False
    )
```

profile of v0, /device:TPU:0, one launch (start us, length us, event | category | flops | bytes accessed | tf_op | source)
XLA Modules:
  0.0 296.7 jit_solution(16707992108680796220)
XLA Ops:
  7.2 0.0 copy-start
  7.2 0.0 reduce-scatter.3.cloned.1.call-start
  7.2 0.7 compare_select_fusion
  7.9 0.1 copy.8
  8.0 0.1 reshape.51
  8.1 32.7 %all_gather.6 = bf16[1024,128]{1,0:T(8,128)(2,1)S(1)} all-gather(bf16[128,128]{1,0:T(8,128)(2,1)} %param.4), channel_id=1, replica_groups=mesh['row'=4,'col'=8] {'col'}, dimensions={0}, use_global_device_ids=true | all-gather | bytes 294912 | tf_op jit(solution)/shard_map/all_gather | solution.py:8
  40.9 0.6 gather_fusion
  41.5 0.0 copy-done
  41.5 0.9 fusion.1
  42.4 0.0 reduce-scatter.3.cloned.1.call-update
  42.4 0.0 reduce-scatter.5.cloned.1.call-start
  42.5 21.1 %reduce-scatter.3.cloned.1.call-done = f32[128,128]{1,0:T(8,128)} async-done(((f32[512,128]{1,0:T(8,128)}), f32[128,128]{1,0:T(8,128)}) %reduce-scatter.3.cloned.1.call-update) | async-done | bytes 65552 | tf_op jit(solution)/shard_map/reduce_scatter | solution.py:19
  63.6 0.8 convert_element_type.7
  64.4 30.8 %all_gather.7 = bf16[1024,128]{1,0:T(8,128)(2,1)S(1)} all-gather(bf16[128,128]{1,0:T(8,128)(2,1)S(1)} %convert_element_type.7), channel_id=1, replica_groups=mesh['row'=4,'col'=8] {'col'}, dimensions={0}, use_global_device_ids=true | all-gather | bytes 294912 | tf_op jit(solution)/shard_map/all_gather | solution.py:8
  95.2 0.6 gather_fusion.1
  95.8 0.9 fusion.3
  96.7 0.0 copy-start.2
  96.7 0.0 copy-start.3
  96.7 0.0 reduce-scatter.5.cloned.1.call-update
  96.8 0.0 all-reduce.2.cloned.1.call-start
  96.8 20.2 %reduce-scatter.5.cloned.1.call-done = f32[128,128]{1,0:T(8,128)} async-done(((f32[512,128]{1,0:T(8,128)}), f32[128,128]{1,0:T(8,128)}) %reduce-scatter.5.cloned.1.call-update) | async-done | bytes 65552 | tf_op jit(solution)/shard_map/reduce_scatter | solution.py:19
  117.0 0.0 copy-done.2
  117.0 0.0 copy-done.3
  117.0 1.9 convolution_bitcast_fusion
  118.9 0.0 all-reduce.2.cloned.1.call-update
  118.9 129.2 %all-reduce.2.cloned.1.call-done = f32[512,128]{0,1:T(8,128)} async-done(((f32[512,128]{0,1:T(8,128)}), f32[512,128]{0,1:T(8,128)}) %all-reduce.2.cloned.1.call-update) | async-done | bytes 262160 | tf_op jit(solution)/shard_map/psum | solution.py:28
  248.1 0.0 copy-done.4
  248.1 1.3 multiply_reduce_fusion
  249.4 39.2 %psum.15 = f32[128]{0:T(128)S(1)} all-reduce(f32[128]{0:T(128)S(1)} %get-tuple-element.6), channel_id=1, replica_groups=mesh['row'=4,'col'=8] {'row','col'}, use_global_device_ids=true, to_apply=%region_4.0 | all-reduce | flops 128 | bytes 1024 | tf_op jit(solution)/shard_map/psum | solution.py:32
  288.7 0.6 broadcast_divide_fusion
  289.3 0.0 copy-done.1
  289.3 0.8 copy.9
  (4 shorter events, 0.0 us)
Async XLA Ops:
  7.2 34.3 %copy-start = (bf16[1,4,1,2,128,128]{5,4,3,2,1,0:T(8,128)(2,1)S(1)}, bf16[1,4,1,2,128,128]{5,4,3,2,1,0:T(8,128)(2,1)}, u32[]{:S(2)}) copy-start(bf16[1,4,1,2,128,128]{5,4,3,2,1,0:T(8,128)(2,1)} %param.5) | copy-start | bytes 786436
  7.2 56.4 %reduce-scatter.3.cloned.1.call-start = ((), (), s32[]{:S(2)}) async-start(), calls=%async_computation.2 | async-start | bytes 327680 | tf_op jit(solution)/shard_map/reduce_scatter | solution.py:19
  42.4 74.6 %reduce-scatter.5.cloned.1.call-start = ((), (), s32[]{:S(2)}) async-start(), calls=%async_computation.3 | async-start | bytes 327680 | tf_op jit(solution)/shard_map/reduce_scatter | solution.py:19
  96.7 20.3 %copy-start.2 = (bf16[128,512]{1,0:T(8,128)(2,1)S(1)}, bf16[128,512]{1,0:T(8,128)(2,1)}, u32[]{:S(2)}) copy-start(bf16[128,512]{1,0:T(8,128)(2,1)} %param.7) | copy-start | bytes 393220
  96.7 20.3 %copy-start.3 = (bf16[128,128]{1,0:T(8,128)(2,1)S(1)}, bf16[128,128]{1,0:T(8,128)(2,1)}, u32[]{:S(2)}) copy-start(bf16[128,128]{1,0:T(8,128)(2,1)} %param.4) | copy-start | bytes 98308
  96.8 151.3 %all-reduce.2.cloned.1.call-start = ((), (), s32[]{:S(2)}) async-start(), calls=%async_computation.4 | async-start | bytes 524288 | tf_op jit(solution)/shard_map/psum | solution.py:28
  118.9 129.2 %copy-start.4 = (f32[128,128]{1,0:T(8,128)S(1)}, f32[128,128]{1,0:T(8,128)}, u32[]{:S(2)}) copy-start(f32[128,128]{1,0:T(8,128)} %reduce-scatter.5.cloned.1.call-done) | copy-start | bytes 196612
  248.1 41.2 %copy-start.1 = (f32[512,128]{0,1:T(8,128)S(1)}, f32[512,128]{0,1:T(8,128)}, u32[]{:S(2)}) copy-start(f32[512,128]{0,1:T(8,128)} %all-reduce.2.cloned.1.call-done) | copy-start | bytes 786436
Sparse Core Ops, SparseCore 0:
  42.5 21.0 reduce-scatter.2
  96.9 20.0 reduce-scatter.4
  123.1 124.9 all-reduce.1
where the time goes:
time: 297 us
  waiting for transfers between devices  171 us (58%)
  blocking collectives  103 us (35%)
  between operations  13.8 us (5%)
  matrix products  5.02 us (2%)
    psum x1, waiting for transfers between devices, per_device(): lax.psum(jnp.dot(history_wide.T, filtered, precision=lax.Precision.HIGHES...  129 us
    all_gather x2, blocking collectives, apply_matrix(): gathered = lax.all_gather(pieces, 'col', axis=0, tiled=True)  63.5 us
    reduce_scatter x2, waiting for transfers between devices, apply_matrix(): lax.psum_scatter(partial_value, 'row', scatter_dimension=0, tiled=True)  41.3 us
    psum x1, blocking collectives, per_device(): squares = lax.psum(jnp.sum(cleaned * cleaned, axis=0), ('row', 'col'))  39.2 us
  transfers between devices with their start and end apart: 3, of which 3 were waited for; matrix products, arithmetic and copies ran while one was open for 0% of the time, Pallas kernels for 0%

commit v1 on v0

v1 whole, which is shorter than its diff:
```python
import functools

import jax
import jax.numpy as jnp
from jax import lax
from jax.experimental import pallas as pl
from jax.experimental.pallas import tpu as pltpu
from jax.sharding import PartitionSpec as P

F32 = jnp.float32
BF16 = jnp.bfloat16
PAD = 16
VMEM = pl.BlockSpec(memory_space=pltpu.VMEM)
SMEM = pl.BlockSpec(memory_space=pltpu.SMEM)


def nbytes(tree):
    return sum(a.size * a.dtype.itemsize for a in jax.tree.leaves(tree))


def call(kernel, out, args, n_smem, out_specs=None):
    single = jax.tree.structure(out) == jax.tree.structure(0)
    if out_specs is None:
        out_specs = VMEM if single else jax.tree.map(lambda _: VMEM, out)
    room = 2 * (nbytes(args) + nbytes(out)) + 8 * 2**20
    return pl.pallas_call(
        kernel,
        out_shape=out,
        in_specs=[SMEM] * n_smem + [VMEM] * (len(args) - n_smem),
        out_specs=out_specs,
        compiler_params=pltpu.CompilerParams(vmem_limit_bytes=min(room, 56 * 2**20)),
    )(*args)


def nt(a, b):
    return lax.dot_general(a, b, (((1,), (1,)), ((), ())), preferred_element_type=F32)


def pieces(value):
    high = value.astype(BF16)
    rest = value - high.astype(F32)
    middle = rest.astype(BF16)
    low = (rest - middle.astype(F32)).astype(BF16)
    return jnp.concatenate([high, middle, low], axis=0)


def joined(stacked):
    third = stacked.shape[0] // 3
    return (stacked[2 * third :] + stacked[third : 2 * third]) + stacked[:third]


def prepare(columns_ref, start_ref, tiles_ref, parts_ref, packed_ref):
    n_row, n_col, width, _ = parts_ref.shape
    turned = start_ref[...].astype(F32).T
    for r in range(n_row):
        part = turned[r * width : (r + 1) * width].astype(BF16)
        for c in range(n_col):
            parts_ref[r, c] = part
    rows = tiles_ref.shape[0]
    packed_ref[:rows] = tiles_ref[...]
    lane = lax.broadcasted_iota(jnp.int32, (PAD, packed_ref.shape[1]), 1)
    numbers = jnp.zeros(lane.shape, jnp.int32)
    for i in range(columns_ref.shape[0]):
        numbers = jnp.where(lane == i, columns_ref[i], numbers)
    packed_ref[rows:] = numbers.astype(F32).astype(BF16)


def multiply(me_row, n_row, slots, order, columns, segment, tiles, p):
    total = None
    for q in range(n_row):
        block = me_row ^ q
        for s in range(slots):
            picked = segment(block, columns(q, p * slots + s))
            start = (p * slots + s) * order
            if not isinstance(start, int):
                start = pl.multiple_of(start, order)
            term = nt(picked, tiles[q][pl.ds(start, order), :])
            total = term if total is None else total + term
    return total


def each(count, body):
    if count <= 4:
        for i in range(count):
            body(i)
    else:
        pl.loop(0, count)(body)


def first(n_row, groups, slots, me_ref, parts_ref, *refs):
    tiles, (copies_ref, columns_ref) = refs[:n_row], refs[n_row:]
    order = parts_ref.shape[-1]
    rows = groups * slots * order
    lane = lax.broadcasted_iota(jnp.int32, (PAD, order), 1)
    for q in range(n_row):
        numbers = tiles[q][rows:, :].astype(F32).astype(jnp.int32)
        for i in range(groups * slots):
            columns_ref[q, i] = jnp.max(jnp.where(lane == i, numbers, 0))

    def row(p):
        total = multiply(
            me_ref[0], n_row, slots, order, lambda q, i: columns_ref[q, i],
            lambda b, c: parts_ref[b, c], tiles, p,
        )
        value = total.astype(BF16)
        for c in range(copies_ref.shape[0]):
            copies_ref[c, p] = value

    each(groups, row)


def second(n_row, groups, slots, me_ref, columns_ref, parts_ref, vectors_ref, *refs):
    tiles, history, (filtered_ref, coeffs_ref) = refs[:n_row], refs[n_row : 2 * n_row], refs[2 * n_row :]
    order = parts_ref.shape[-1]

    def row(p):
        total = multiply(
            me_ref[0], n_row, slots, order, lambda q, i: columns_ref[q, i],
            lambda b, c: vectors_ref[c, b], tiles, p,
        )
        filtered_ref[p] = 2.0 * total - parts_ref[p, me_ref[1]].astype(F32)

    each(groups, row)
    total = None
    for q in range(n_row):
        split = pieces(filtered_ref[me_ref[0] ^ q])
        term = joined(jnp.dot(split, history[q][...], preferred_element_type=F32))
        total = term if total is None else total + term
    coeffs_ref[...] = total


def clean(n_row, me_ref, coeffs_ref, filtered_ref, *refs):
    history, outs, squares_ref = refs[:n_row], refs[n_row : 2 * n_row], refs[2 * n_row]
    width, order = filtered_ref.shape[1:]
    stored = coeffs_ref.shape[1]
    coeffs = coeffs_ref[...]
    split = pieces(coeffs)
    squares = jnp.zeros((width, order), F32)
    for q in range(n_row):
        cleaned = filtered_ref[me_ref[0] ^ q] - joined(nt(split, history[q][...]))
        squares = squares + cleaned * cleaned
        outs[q][:, :stored] = coeffs
        outs[q][:, stored:] = cleaned
    sums = jnp.sum(squares.T, axis=0, keepdims=True)
    line = jnp.concatenate([sums] * n_row, axis=1)
    lane = lax.broadcasted_iota(jnp.int32, line.shape, 1)
    mine = (lane >= me_ref[0] * width) & (lane < (me_ref[0] + 1) * width)
    line = jnp.where(mine, line, 0.0)
    squares_ref[...] = jnp.broadcast_to(line[:, None, :], squares_ref.shape)


def finish(n_row, total_rows, me_ref, squares_ref, *refs):
    slabs, (block_ref, out_ref, whole_ref) = refs[:n_row], refs[n_row:]
    width = slabs[0].shape[0]
    stored = out_ref.shape[0]
    for q in range(n_row):
        r = me_ref[0] ^ q
        whole_ref[pl.ds(pl.multiple_of(r * width, width), width), :] = slabs[q][...]
    sums = jnp.sum(squares_ref[...], axis=0)[:1]
    lengths = jnp.sqrt(sums / total_rows + 1e-05)
    out_ref[...] = whole_ref[:, :stored].T
    block_ref[...] = whole_ref[:, stored:].T / lengths


def exchanged(value, axis, q):
    return lax.ppermute(value, axis, [(i, i ^ q) for i in range(lax.axis_size(axis))])


def per_device(start_block, matrix_tiles, tile_columns, history):
    n_row, n_col = lax.axis_size("row"), lax.axis_size("col")
    me_row, me_col = lax.axis_index("row"), lax.axis_index("col")
    me = jnp.stack([me_row, me_col]).astype(jnp.int32)
    _, groups, _, slots, order, _ = matrix_tiles.shape
    n_vectors = start_block.shape[1]
    stored = history.shape[1]
    width = n_vectors // n_row
    rows = groups * slots * order
    both = ("row", "col")

    parts, packed = call(
        prepare,
        (
            jax.ShapeDtypeStruct((n_row, n_col, width, order), BF16),
            jax.ShapeDtypeStruct((rows + PAD, order), BF16),
        ),
        (tile_columns.reshape(-1), start_block, matrix_tiles.reshape(rows, order)),
        1,
    )
    tiles = [packed] + [exchanged(packed, "row", q) for q in range(1, n_row)]
    parts = lax.all_to_all(
        parts.reshape(n_row * n_col, width, order), both, 0, 0
    ).reshape(n_row, n_col, width, order)
    histories = [history] + [exchanged(history, "row", q) for q in range(1, n_row)]

    copies, columns = call(
        functools.partial(first, n_row, groups, slots),
        (
            jax.ShapeDtypeStruct((n_col, groups, width, order), BF16),
            jax.ShapeDtypeStruct((n_row, groups * slots), jnp.int32),
        ),
        (me, parts, *tiles),
        1,
        (VMEM, SMEM),
    )
    vectors = lax.all_to_all(copies, "col", 0, 0)
    filtered, coeffs = call(
        functools.partial(second, n_row, groups, slots),
        (
            jax.ShapeDtypeStruct((groups, width, order), F32),
            jax.ShapeDtypeStruct((width, stored), F32),
        ),
        (me, columns, parts, vectors, *tiles, *histories),
        2,
    )
    step = 1
    while step < n_col:
        coeffs = coeffs + exchanged(coeffs, "col", step)
        step *= 2
    *slabs, squares = call(
        functools.partial(clean, n_row),
        [jax.ShapeDtypeStruct((width, stored + order), F32) for _ in range(n_row)]
        + [jax.ShapeDtypeStruct((n_row * n_col, 1, n_vectors), F32)],
        (me, coeffs, filtered, *histories),
        1,
    )
    slabs = [slabs[0]] + [exchanged(slabs[q], "row", q) for q in range(1, n_row)]
    squares = lax.all_to_all(squares, both, 0, 0)
    total_rows = order * n_row * n_col
    out = (
        jax.ShapeDtypeStruct((order, n_vectors), F32),
        jax.ShapeDtypeStruct((stored, n_vectors), F32),
    )
    args = (me, squares, *slabs)
    return pl.pallas_call(
        functools.partial(finish, n_row, total_rows),
        out_shape=out,
        in_specs=[SMEM] + [VMEM] * (len(args) - 1),
        out_specs=(VMEM, VMEM),
        scratch_shapes=[pltpu.VMEM((n_vectors, stored + order), F32)],
        compiler_params=pltpu.CompilerParams(vmem_limit_bytes=2 * nbytes(args) + 16 * 2**20),
    )(*args)


def solution(mesh):
    in_specs = (
        P(("row", "col"), None),
        P("row", None, "col", None, None, None),
        P("row", None, "col", None),
        P(("row", "col"), None),
    )
    out_specs = (P(("row", "col"), None), P())
    return jax.shard_map(
        per_device, mesh=mesh, in_specs=in_specs, out_specs=out_specs, check_vma=False
    )
```

time: 297 us -> 78.2 us (0.26)
  waiting for transfers between devices: 171 us -> 31.8 us
  blocking collectives: 103 us -> 11.3 us
  starting transfers between devices: 0.12 us -> 23.9 us
  between operations: 13.8 us -> 0.7 us
  Pallas kernels: 0 us -> 7.43 us
  matrix products: 5.02 us -> 0 us
    psum x1 -> x0, waiting for transfers between devices: 129 us -> none  [per_device(): lax.psum(jnp.dot(history_wide.T, filtered, precision=lax.Precision.HIGHES...]
    all_gather x2 -> x0, blocking collectives: 63.5 us -> none  [apply_matrix(): gathered = lax.all_gather(pieces, 'col', axis=0, tiled=True)]
    reduce_scatter x2 -> x0, waiting for transfers between devices: 41.3 us -> none  [apply_matrix(): lax.psum_scatter(partial_value, 'row', scatter_dimension=0, tiled=True)]
    psum x1 -> x0, blocking collectives: 39.2 us -> none  [per_device(): squares = lax.psum(jnp.sum(cleaned * cleaned, axis=0), ('row', 'col'))]
    ppermute x0 -> x12, waiting for transfers between devices: none -> 31 us  [exchanged(): lax.ppermute(value, axis, [(i, i ^ q) for i in range(lax.axis_size(axis))])]
    all_to_all x0 -> x2, starting transfers between devices: none -> 13.1 us  [the longest x1 7.3 us: per_device(): lax.all_to_all(parts.reshape(n_row * n_col, width, order), both, 0, 0)]
    all_to_all x0 -> x1, blocking collectives: none -> 11.3 us  [per_device(): squares = lax.all_to_all(squares, both, 0, 0)]
    ppermute x0 -> x12, starting transfers between devices: none -> 10.8 us  [exchanged(): lax.ppermute(value, axis, [(i, i ^ q) for i in range(lax.axis_size(axis))])]
  transfers between devices with their start and end apart: 3 -> 14, of which waited for: 3 -> 8; matrix products, arithmetic and copies ran while one was open for 0% -> 0% of each run, Pallas kernels for 0% -> 0%
where the time goes in v1:
time: 78.2 us; the launch traced here: 77.8 us
  waiting for transfers between devices  31.8 us (41%)
  starting transfers between devices  23.9 us (31%)
  blocking collectives  11.3 us (14%)
  Pallas kernels  7.43 us (10%)
  local copies, waits for them, and re-layouts  2.57 us (3%)
    ppermute x12, waiting for transfers between devices, exchanged(): lax.ppermute(value, axis, [(i, i ^ q) for i in range(lax.axis_size(axis))])  31 us
    all_to_all x1, blocking collectives, per_device(): squares = lax.all_to_all(squares, both, 0, 0)  11.3 us
    ppermute x12, starting transfers between devices, exchanged(): lax.ppermute(value, axis, [(i, i ^ q) for i in range(lax.axis_size(axis))])  10.8 us
    all_to_all x1, starting transfers between devices, per_device(): lax.all_to_all(parts.reshape(n_row * n_col, width, order), both, 0, 0)  7.3 us
    pallas_call x4, Pallas kernels, call(): pl.pallas_call(kernel, out_shape=out, in_specs=[SMEM] * n_smem + [VMEM] *...  5.99 us
    all_to_all x1, starting transfers between devices, per_device(): vectors = lax.all_to_all(copies, 'col', 0, 0)  5.78 us
    unnamed x7, local copies, waits for them, and re-layouts  2.48 us
  transfers between devices with their start and end apart: 14, of which 8 were waited for; matrix products, arithmetic and copies ran while one was open for 0% of the time, Pallas kernels for 0%

profile of v1, /device:TPU:0, one launch (start us, length us, event | category | flops | bytes accessed | tf_op | source)
XLA Modules:
  0.0 77.8 jit_solution(13404426636476933823)
XLA Ops:
  0.6 0.8 copy.7
  1.4 0.1 reshape.16.columns_ref
  1.5 0.9 %copy-done.1 = bf16[1,4,1,2,128,128]{5,4,3,2,1,0:T(8,128)(2,1)S(1)} copy-done((bf16[1,4,1,2,128,128]{5,4,3,2,1,0:T(8,128)(2,1)S(1)}, bf16[1,4,1,2,128,128]{5,4,3,2,1,0:T(8,128)(2,1)}, u32[]{:S(2)}) %copy-start.1) | copy-done | bytes 262168
  2.4 0.8 copy-done.2
  3.2 1.3 %shard_map.59 = (bf16[4,8,32,128]{3,2,1,0:T(8,128)(2,1)}, bf16[1040,128]{1,0:T(8,128)(2,1)S(1)}) custom-call(s32[8]{0:T(128)S(1)} %reshape.16.columns_ref, bf16[128,128]{1,0:T(8,128)(2,1)S(1)} %copy-done.2, bf16[1024,128]{1,0:T(8,128)(2,1)S(1)} %bitcast.9), custom_call_target="tpu_custom_call" | custom-call | tf_op jit(solution)/shard_map/pallas_call | solution.py:26
  4.5 7.3 %all-to-all-start = ((bf16[32,32,128]{2,1,0:T(8,128)(2,1)}), bf16[32,32,128]{2,1,0:T(8,128)(2,1)S(1)}, u32[]{:S(2)}, u32[]{:S(2)}) async-start(bf16[32,32,128]{2,1,0:T(8,128)(2,1)} %bitcast.3), calls=%async_computation | async-start | bytes 524288 | tf_op jit(solution)/shard_map/all_to_all | solution.py:190
  11.8 0.3 collective-permute-start
  12.2 1.7 %collective-permute-start.1 = (bf16[1040,128]{1,0:T(8,128)(2,1)S(1)}, bf16[1040,128]{1,0:T(8,128)(2,1)S(1)}, u32[]{:S(2)}, u32[]{:S(2)}) collective-permute-start(bf16[1040,128]{1,0:T(8,128)(2,1)S(1)} %get-tuple-element.14.refs_0_), channel_id=1, source_target_pairs={{0,16},{8,24},{16,0},{24,8},{1,17},{9,25},{17,1},{25,9},{2,18},{10... | collective-permute-start | bytes 798728 | tf_op jit(solution)/shard_map/ppermute | solution.py:166
  13.8 0.1 pad_add_fusion.me_ref
  13.9 9.9 %collective-permute-done.1.refs_2_ = bf16[1040,128]{1,0:T(8,128)(2,1)S(1)} collective-permute-done((bf16[1040,128]{1,0:T(8,128)(2,1)S(1)}, bf16[1040,128]{1,0:T(8,128)(2,1)S(1)}, u32[]{:S(2)}, u32[]{:S(2)}) %collective-permute-start.1) | collective-permute-done | bytes 266272 | tf_op jit(solution)/shard_map/ppermute | solution.py:166
  23.8 4.8 %collective-permute-done.2.refs_3_ = bf16[1040,128]{1,0:T(8,128)(2,1)S(1)} collective-permute-done((bf16[1040,128]{1,0:T(8,128)(2,1)S(1)}, bf16[1040,128]{1,0:T(8,128)(2,1)S(1)}, u32[]{:S(2)}, u32[]{:S(2)}) %collective-permute-start.2) | collective-permute-done | bytes 266272 | tf_op jit(solution)/shard_map/ppermute | solution.py:166
  28.6 2.2 %shard_map.60 = (bf16[8,4,32,128]{3,2,1,0:T(8,128)(2,1)}, s32[4,8]{1,0:T(4,128)S(1)}) custom-call(s32[2]{0:T(128)S(1)} %pad_add_fusion.me_ref, bf16[4,8,32,128]{3,2,1,0:T(8,128)(2,1)S(1)} %bitcast.7, bf16[1040,128]{1,0:T(8,128)(2,1)S(1)} %get-tuple-element.14.refs_0_, bf16[1040,128]{1,0:T(8,128)(2,1)S(1)} %collective-permute-done.refs_1_, ...), custom_call_target="tpu_custom_call" | custom-call | tf_op jit(solution)/shard_map/pallas_call | solution.py:26
  30.8 0.0 copy-start
  30.8 5.8 %all-to-all-start.1 = ((bf16[8,4,32,128]{3,2,1,0:T(8,128)(2,1)}), bf16[8,4,32,128]{3,2,1,0:T(8,128)(2,1)S(1)}, u32[]{:S(2)}, u32[]{:S(2)}) async-start(bf16[8,4,32,128]{3,2,1,0:T(8,128)(2,1)} %get-tuple-element.16), calls=%async_computation.1 | async-start | bytes 524288 | tf_op jit(solution)/shard_map/all_to_all | solution.py:205
  36.6 0.1 collective-permute-start.3
  36.7 0.8 %collective-permute-start.4 = (bf16[128,512]{1,0:T(8,128)(2,1)S(1)}, bf16[128,512]{1,0:T(8,128)(2,1)S(1)}, u32[]{:S(2)}, u32[]{:S(2)}) collective-permute-start(bf16[128,512]{1,0:T(8,128)(2,1)S(1)} %copy-done), channel_id=1, source_target_pairs={{0,16},{8,24},{16,0},{24,8},{1,17},{9,25},{17,1},{25,9},{2,18},{10... | collective-permute-start | bytes 393224 | tf_op jit(solution)/shard_map/ppermute | solution.py:166
  37.5 1.0 %collective-permute-start.5 = (bf16[128,512]{1,0:T(8,128)(2,1)S(1)}, bf16[128,512]{1,0:T(8,128)(2,1)S(1)}, u32[]{:S(2)}, u32[]{:S(2)}) collective-permute-start(bf16[128,512]{1,0:T(8,128)(2,1)S(1)} %copy-done), channel_id=1, source_target_pairs={{0,24},{8,16},{16,8},{24,0},{1,25},{9,17},{17,9},{25,1},{2,26},{10... | collective-permute-start | bytes 393224 | tf_op jit(solution)/shard_map/ppermute | solution.py:166
  38.5 4.5 %collective-permute-done.4.refs_6_.refs_2_ = bf16[128,512]{1,0:T(8,128)(2,1)S(1)} collective-permute-done((bf16[128,512]{1,0:T(8,128)(2,1)S(1)}, bf16[128,512]{1,0:T(8,128)(2,1)S(1)}, u32[]{:S(2)}, u32[]{:S(2)}) %collective-permute-start.4) | collective-permute-done | bytes 131104 | tf_op jit(solution)/shard_map/ppermute | solution.py:166
  43.0 1.9 %collective-permute-done.5.refs_7_.refs_3_ = bf16[128,512]{1,0:T(8,128)(2,1)S(1)} collective-permute-done((bf16[128,512]{1,0:T(8,128)(2,1)S(1)}, bf16[128,512]{1,0:T(8,128)(2,1)S(1)}, u32[]{:S(2)}, u32[]{:S(2)}) %collective-permute-start.5) | collective-permute-done | bytes 131104 | tf_op jit(solution)/shard_map/ppermute | solution.py:166
  45.0 0.8 %all-to-all-done.1.vectors_ref = bf16[8,4,32,128]{3,2,1,0:T(8,128)(2,1)S(1)} async-done(((bf16[8,4,32,128]{3,2,1,0:T(8,128)(2,1)}), bf16[8,4,32,128]{3,2,1,0:T(8,128)(2,1)S(1)}, u32[]{:S(2)}, u32[]{:S(2)}) %all-to-all-start.1) | async-done | bytes 262176 | tf_op jit(solution)/shard_map/all_to_all | solution.py:205
  45.8 1.4 %shard_map.61 = (f32[4,32,128]{2,1,0:T(8,128)S(1)}, f32[32,512]{1,0:T(8,128)S(1)}) custom-call(s32[2]{0:T(128)S(1)} %pad_add_fusion.me_ref, s32[4,8]{1,0:T(4,128)S(1)} %get-tuple-element.15.columns_ref, bf16[4,8,32,128]{3,2,1,0:T(8,128)(2,1)S(1)} %bitcast.8, bf16[8,4,32,128]{3,2,1,0:T(8,128)(2,1)S(1)} %all-to-all-done.1.vectors_ref, ...), custom_call_target="tpu_custom_call" | custom-call | tf_op jit(solution)/shard_map/pallas_call | solution.py:26
  47.2 1.5 %collective-permute-start.6 = (f32[32,512]{1,0:T(8,128)S(1)}, f32[32,512]{1,0:T(8,128)S(1)}, u32[]{:S(2)}, u32[]{:S(2)}) collective-permute-start(f32[32,512]{1,0:T(8,128)S(1)} %get-tuple-element.17), channel_id=1, source_target_pairs={{0,1},{1,0},{2,3},{3,2},{4,5},{5,4},{6,7},{7,6},{8,9},{9,8},{10,11... | collective-permute-start | bytes 196616 | tf_op jit(solution)/shard_map/ppermute | solution.py:166
  48.7 2.9 %collective-permute-done.6 = f32[32,512]{1,0:T(8,128)S(1)} collective-permute-done((f32[32,512]{1,0:T(8,128)S(1)}, f32[32,512]{1,0:T(8,128)S(1)}, u32[]{:S(2)}, u32[]{:S(2)}) %collective-permute-start.6) | collective-permute-done | bytes 65568 | tf_op jit(solution)/shard_map/ppermute | solution.py:166
  51.6 1.2 %collective-permute-start.7 = (f32[32,512]{1,0:T(8,128)S(1)}, f32[32,512]{1,0:T(8,128)S(1)}, u32[]{:S(2)}, u32[]{:S(2)}) collective-permute-start(f32[32,512]{1,0:T(8,128)S(1)} %add.9), channel_id=1, source_target_pairs={{0,2},{1,3},{2,0},{3,1},{4,6},{5,7},{6,4},{7,5},{8,10},{9,11},{10,... | collective-permute-start | bytes 196616 | tf_op jit(solution)/shard_map/ppermute | solution.py:166
  52.7 3.2 %collective-permute-done.7 = f32[32,512]{1,0:T(8,128)S(1)} collective-permute-done((f32[32,512]{1,0:T(8,128)S(1)}, f32[32,512]{1,0:T(8,128)S(1)}, u32[]{:S(2)}, u32[]{:S(2)}) %collective-permute-start.7) | collective-permute-done | bytes 65568 | tf_op jit(solution)/shard_map/ppermute | solution.py:166
  55.9 2.1 %collective-permute-start.8 = (f32[32,512]{1,0:T(8,128)S(1)}, f32[32,512]{1,0:T(8,128)S(1)}, u32[]{:S(2)}, u32[]{:S(2)}) collective-permute-start(f32[32,512]{1,0:T(8,128)S(1)} %add.10), channel_id=1, source_target_pairs={{0,4},{1,5},{2,6},{3,7},{4,0},{5,1},{6,2},{7,3},{8,12},{9,13},{10,... | collective-permute-start | bytes 196616 | tf_op jit(solution)/shard_map/ppermute | solution.py:166
  58.0 3.9 %collective-permute-done.8 = f32[32,512]{1,0:T(8,128)S(1)} collective-permute-done((f32[32,512]{1,0:T(8,128)S(1)}, f32[32,512]{1,0:T(8,128)S(1)}, u32[]{:S(2)}, u32[]{:S(2)}) %collective-permute-start.8) | collective-permute-done | bytes 65568 | tf_op jit(solution)/shard_map/ppermute | solution.py:166
  61.8 1.0 %shard_map.62 = (f32[32,640]{1,0:T(8,128)S(1)}, f32[32,640]{1,0:T(8,128)S(1)}, f32[32,640]{1,0:T(8,128)S(1)}, f32[32,640]{1,0:T(8,128)S(1)}, f32[32,1,128]{2,1,0:T(1,128)S(1)}) custom-call(s32[2]{0:T(128)S(1)} %pad_add_fusion.me_ref, f32[32,512]{1,0:T(8,128)S(1)} %add.11.coeffs_ref, f32[4,32,128]{2,1,0:T(8,128)S(1)} %get-tuple-element.18.filtered_ref, ...), custom_call_target="tpu_custom_call" | custom-call | tf_op jit(solution)/shard_map/pallas_call | solution.py:26
  62.9 0.8 %collective-permute-start.10 = (f32[32,640]{1,0:T(8,128)S(1)}, f32[32,640]{1,0:T(8,128)S(1)}, u32[]{:S(2)}, u32[]{:S(2)}) collective-permute-start(f32[32,640]{1,0:T(8,128)S(1)} %get-tuple-element.22), channel_id=1, source_target_pairs={{0,16},{8,24},{16,0},{24,8},{1,17},{9,25},{17,1},{25,9},{2,18},{10... | collective-permute-start | bytes 245768 | tf_op jit(solution)/shard_map/ppermute | solution.py:166
  63.7 1.4 %collective-permute-start.9 = (f32[32,640]{1,0:T(8,128)S(1)}, f32[32,640]{1,0:T(8,128)S(1)}, u32[]{:S(2)}, u32[]{:S(2)}) collective-permute-start(f32[32,640]{1,0:T(8,128)S(1)} %get-tuple-element.21), channel_id=1, source_target_pairs={{0,8},{8,0},{16,24},{24,16},{1,9},{9,1},{17,25},{25,17},{2,10},{10... | collective-permute-start | bytes 245768 | tf_op jit(solution)/shard_map/ppermute | solution.py:166
  65.1 11.3 %all_to_all.15.squares_ref = f32[32,1,128]{2,1,0:T(1,128)S(1)} all-to-all(f32[32,1,128]{2,1,0:T(1,128)S(1)} %get-tuple-element.19), channel_id=1, replica_groups=mesh['row'=4,'col'=8] {'row','col'}, dimensions={0} | all-to-all | bytes 32768 | tf_op jit(solution)/shard_map/all_to_all | solution.py:227
  76.4 1.4 %shard_map.63 = (f32[128,128]{1,0:T(8,128)}, f32[512,128]{1,0:T(8,128)}) custom-call(s32[2]{0:T(128)S(1)} %pad_add_fusion.me_ref, f32[32,1,128]{2,1,0:T(1,128)S(1)} %all_to_all.15.squares_ref, f32[32,640]{1,0:T(8,128)S(1)} %get-tuple-element.20.refs_0_, f32[32,640]{1,0:T(8,128)S(1)} %collective-permute-done.9.refs_1_, ...), custom_call_target="tpu_custom_call" | custom-call | tf_op jit(solution)/shard_map/pallas_call | solution.py:234
  (14 shorter events, 0.1 us)
Async XLA Ops:
  1.5 1.0 %copy-start.1 = (bf16[1,4,1,2,128,128]{5,4,3,2,1,0:T(8,128)(2,1)S(1)}, bf16[1,4,1,2,128,128]{5,4,3,2,1,0:T(8,128)(2,1)}, u32[]{:S(2)}) copy-start(bf16[1,4,1,2,128,128]{5,4,3,2,1,0:T(8,128)(2,1)} %param.5) | copy-start | bytes 786436
  2.4 0.8 copy-start.2
  4.5 24.1 %all-to-all-start = ((bf16[32,32,128]{2,1,0:T(8,128)(2,1)}), bf16[32,32,128]{2,1,0:T(8,128)(2,1)S(1)}, u32[]{:S(2)}, u32[]{:S(2)}) async-start(bf16[32,32,128]{2,1,0:T(8,128)(2,1)} %bitcast.3), calls=%async_computation | async-start | bytes 524288 | tf_op jit(solution)/shard_map/all_to_all | solution.py:190
  11.8 2.1 %collective-permute-start = (bf16[1040,128]{1,0:T(8,128)(2,1)S(1)}, bf16[1040,128]{1,0:T(8,128)(2,1)S(1)}, u32[]{:S(2)}, u32[]{:S(2)}) collective-permute-start(bf16[1040,128]{1,0:T(8,128)(2,1)S(1)} %get-tuple-element.14.refs_0_), channel_id=1, source_target_pairs={{0,8},{8,0},{16,24},{24,16},{1,9},{9,1},{17,25},{25,17},{2,10},{10... | collective-permute-start | bytes 798728 | tf_op jit(solution)/shard_map/ppermute | solution.py:166
  12.2 11.7 %collective-permute-start.1 = (bf16[1040,128]{1,0:T(8,128)(2,1)S(1)}, bf16[1040,128]{1,0:T(8,128)(2,1)S(1)}, u32[]{:S(2)}, u32[]{:S(2)}) collective-permute-start(bf16[1040,128]{1,0:T(8,128)(2,1)S(1)} %get-tuple-element.14.refs_0_), channel_id=1, source_target_pairs={{0,16},{8,24},{16,0},{24,8},{1,17},{9,25},{17,1},{25,9},{2,18},{10... | collective-permute-start | bytes 798728 | tf_op jit(solution)/shard_map/ppermute | solution.py:166
  13.8 14.8 %collective-permute-start.2 = (bf16[1040,128]{1,0:T(8,128)(2,1)S(1)}, bf16[1040,128]{1,0:T(8,128)(2,1)S(1)}, u32[]{:S(2)}, u32[]{:S(2)}) collective-permute-start(bf16[1040,128]{1,0:T(8,128)(2,1)S(1)} %get-tuple-element.14.refs_0_), channel_id=1, source_target_pairs={{0,24},{8,16},{16,8},{24,0},{1,25},{9,17},{17,9},{25,1},{2,26},{10... | collective-permute-start | bytes 798728 | tf_op jit(solution)/shard_map/ppermute | solution.py:166
  30.8 5.8 %copy-start = (bf16[128,512]{1,0:T(8,128)(2,1)S(1)}, bf16[128,512]{1,0:T(8,128)(2,1)}, u32[]{:S(2)}) copy-start(bf16[128,512]{1,0:T(8,128)(2,1)} %refs_0_.1) | copy-start | bytes 393220
  30.8 15.0 %all-to-all-start.1 = ((bf16[8,4,32,128]{3,2,1,0:T(8,128)(2,1)}), bf16[8,4,32,128]{3,2,1,0:T(8,128)(2,1)S(1)}, u32[]{:S(2)}, u32[]{:S(2)}) async-start(bf16[8,4,32,128]{3,2,1,0:T(8,128)(2,1)} %get-tuple-element.16), calls=%async_computation.1 | async-start | bytes 524288 | tf_op jit(solution)/shard_map/all_to_all | solution.py:205
  36.6 1.9 %collective-permute-start.3 = (bf16[128,512]{1,0:T(8,128)(2,1)S(1)}, bf16[128,512]{1,0:T(8,128)(2,1)S(1)}, u32[]{:S(2)}, u32[]{:S(2)}) collective-permute-start(bf16[128,512]{1,0:T(8,128)(2,1)S(1)} %copy-done), channel_id=1, source_target_pairs={{0,8},{8,0},{16,24},{24,16},{1,9},{9,1},{17,25},{25,17},{2,10},{10... | collective-permute-start | bytes 393224 | tf_op jit(solution)/shard_map/ppermute | solution.py:166
  36.7 6.4 %collective-permute-start.4 = (bf16[128,512]{1,0:T(8,128)(2,1)S(1)}, bf16[128,512]{1,0:T(8,128)(2,1)S(1)}, u32[]{:S(2)}, u32[]{:S(2)}) collective-permute-start(bf16[128,512]{1,0:T(8,128)(2,1)S(1)} %copy-done), channel_id=1, source_target_pairs={{0,16},{8,24},{16,0},{24,8},{1,17},{9,25},{17,1},{25,9},{2,18},{10... | collective-permute-start | bytes 393224 | tf_op jit(solution)/shard_map/ppermute | solution.py:166
  37.5 7.4 %collective-permute-start.5 = (bf16[128,512]{1,0:T(8,128)(2,1)S(1)}, bf16[128,512]{1,0:T(8,128)(2,1)S(1)}, u32[]{:S(2)}, u32[]{:S(2)}) collective-permute-start(bf16[128,512]{1,0:T(8,128)(2,1)S(1)} %copy-done), channel_id=1, source_target_pairs={{0,24},{8,16},{16,8},{24,0},{1,25},{9,17},{17,9},{25,1},{2,26},{10... | collective-permute-start | bytes 393224 | tf_op jit(solution)/shard_map/ppermute | solution.py:166
  47.2 4.3 %collective-permute-start.6 = (f32[32,512]{1,0:T(8,128)S(1)}, f32[32,512]{1,0:T(8,128)S(1)}, u32[]{:S(2)}, u32[]{:S(2)}) collective-permute-start(f32[32,512]{1,0:T(8,128)S(1)} %get-tuple-element.17), channel_id=1, source_target_pairs={{0,1},{1,0},{2,3},{3,2},{4,5},{5,4},{6,7},{7,6},{8,9},{9,8},{10,11... | collective-permute-start | bytes 196616 | tf_op jit(solution)/shard_map/ppermute | solution.py:166
  51.6 4.3 %collective-permute-start.7 = (f32[32,512]{1,0:T(8,128)S(1)}, f32[32,512]{1,0:T(8,128)S(1)}, u32[]{:S(2)}, u32[]{:S(2)}) collective-permute-start(f32[32,512]{1,0:T(8,128)S(1)} %add.9), channel_id=1, source_target_pairs={{0,2},{1,3},{2,0},{3,1},{4,6},{5,7},{6,4},{7,5},{8,10},{9,11},{10,... | collective-permute-start | bytes 196616 | tf_op jit(solution)/shard_map/ppermute | solution.py:166
  55.9 5.9 %collective-permute-start.8 = (f32[32,512]{1,0:T(8,128)S(1)}, f32[32,512]{1,0:T(8,128)S(1)}, u32[]{:S(2)}, u32[]{:S(2)}) collective-permute-start(f32[32,512]{1,0:T(8,128)S(1)} %add.10), channel_id=1, source_target_pairs={{0,4},{1,5},{2,6},{3,7},{4,0},{5,1},{6,2},{7,3},{8,12},{9,13},{10,... | collective-permute-start | bytes 196616 | tf_op jit(solution)/shard_map/ppermute | solution.py:166
  62.9 13.5 %collective-permute-start.10 = (f32[32,640]{1,0:T(8,128)S(1)}, f32[32,640]{1,0:T(8,128)S(1)}, u32[]{:S(2)}, u32[]{:S(2)}) collective-permute-start(f32[32,640]{1,0:T(8,128)S(1)} %get-tuple-element.22), channel_id=1, source_target_pairs={{0,16},{8,24},{16,0},{24,8},{1,17},{9,25},{17,1},{25,9},{2,18},{10... | collective-permute-start | bytes 245768 | tf_op jit(solution)/shard_map/ppermute | solution.py:166
  63.7 12.7 %collective-permute-start.11 = (f32[32,640]{1,0:T(8,128)S(1)}, f32[32,640]{1,0:T(8,128)S(1)}, u32[]{:S(2)}, u32[]{:S(2)}) collective-permute-start(f32[32,640]{1,0:T(8,128)S(1)} %get-tuple-element.23), channel_id=1, source_target_pairs={{0,24},{8,16},{16,8},{24,0},{1,25},{9,17},{17,9},{25,1},{2,26},{10... | collective-permute-start | bytes 245768 | tf_op jit(solution)/shard_map/ppermute | solution.py:166
  63.7 12.7 %collective-permute-start.9 = (f32[32,640]{1,0:T(8,128)S(1)}, f32[32,640]{1,0:T(8,128)S(1)}, u32[]{:S(2)}, u32[]{:S(2)}) collective-permute-start(f32[32,640]{1,0:T(8,128)S(1)} %get-tuple-element.21), channel_id=1, source_target_pairs={{0,8},{8,0},{16,24},{24,16},{1,9},{9,1},{17,25},{25,17},{2,10},{10... | collective-permute-start | bytes 245768 | tf_op jit(solution)/shard_map/ppermute | solution.py:166

commit v2 on v1

--- a/solution.py
+++ b/solution.py
@@ -9,7 +9,6 @@
 
 F32 = jnp.float32
 BF16 = jnp.bfloat16
-PAD = 16
 VMEM = pl.BlockSpec(memory_space=pltpu.VMEM)
 SMEM = pl.BlockSpec(memory_space=pltpu.SMEM)
 
@@ -49,20 +48,13 @@
     return (stacked[2 * third :] + stacked[third : 2 * third]) + stacked[:third]
 
 
-def prepare(columns_ref, start_ref, tiles_ref, parts_ref, packed_ref):
+def prepare(start_ref, parts_ref):
     n_row, n_col, width, _ = parts_ref.shape
     turned = start_ref[...].astype(F32).T
     for r in range(n_row):
         part = turned[r * width : (r + 1) * width].astype(BF16)
         for c in range(n_col):
             parts_ref[r, c] = part
-    rows = tiles_ref.shape[0]
-    packed_ref[:rows] = tiles_ref[...]
-    lane = lax.broadcasted_iota(jnp.int32, (PAD, packed_ref.shape[1]), 1)
-    numbers = jnp.zeros(lane.shape, jnp.int32)
-    for i in range(columns_ref.shape[0]):
-        numbers = jnp.where(lane == i, columns_ref[i], numbers)
-    packed_ref[rows:] = numbers.astype(F32).astype(BF16)
 
 
 def multiply(me_row, n_row, slots, order, columns, segment, tiles, p):
@@ -87,15 +79,9 @@
         pl.loop(0, count)(body)
 
 
-def first(n_row, groups, slots, me_ref, parts_ref, *refs):
-    tiles, (copies_ref, columns_ref) = refs[:n_row], refs[n_row:]
+def first(n_row, groups, slots, me_ref, columns_ref, parts_ref, *refs):
+    tiles, copies_ref = refs[:n_row], refs[n_row]
     order = parts_ref.shape[-1]
-    rows = groups * slots * order
-    lane = lax.broadcasted_iota(jnp.int32, (PAD, order), 1)
-    for q in range(n_row):
-        numbers = tiles[q][rows:, :].astype(F32).astype(jnp.int32)
-        for i in range(groups * slots):
-            columns_ref[q, i] = jnp.max(jnp.where(lane == i, numbers, 0))
 
     def row(p):
         total = multiply(
@@ -162,6 +148,16 @@
     block_ref[...] = whole_ref[:, stored:].T / lengths
 
 
+def from_rows(value):
+    n_row = lax.axis_size("row")
+    found = {0: value}
+    bit = n_row // 2
+    while bit:
+        found |= {q | bit: exchanged(found[q], "row", bit) for q in list(found)}
+        bit //= 2
+    return [found[q] for q in range(n_row)]
+
+
 def exchanged(value, axis, q):
     return lax.ppermute(value, axis, [(i, i ^ q) for i in range(lax.axis_size(axis))])
 
@@ -177,30 +173,21 @@
     rows = groups * slots * order
     both = ("row", "col")
 
-    parts, packed = call(
-        prepare,
-        (
-            jax.ShapeDtypeStruct((n_row, n_col, width, order), BF16),
-            jax.ShapeDtypeStruct((rows + PAD, order), BF16),
-        ),
-        (tile_columns.reshape(-1), start_block, matrix_tiles.reshape(rows, order)),
-        1,
-    )
-    tiles = [packed] + [exchanged(packed, "row", q) for q in range(1, n_row)]
+    tiles = from_rows(matrix_tiles.reshape(rows, order))
+    parts = call(
+        prepare, jax.ShapeDtypeStruct((n_row, n_col, width, order), BF16), (start_block,), 0
+    )
     parts = lax.all_to_all(
         parts.reshape(n_row * n_col, width, order), both, 0, 0
     ).reshape(n_row, n_col, width, order)
-    histories = [history] + [exchanged(history, "row", q) for q in range(1, n_row)]
-
-    copies, columns = call(
+    histories = from_rows(history)
+    columns = jnp.stack(from_rows(tile_columns.reshape(-1)))
+
+    copies = call(
         functools.partial(first, n_row, groups, slots),
-        (
-            jax.ShapeDtypeStruct((n_col, groups, width, order), BF16),
-            jax.ShapeDtypeStruct((n_row, groups * slots), jnp.int32),
-        ),
-        (me, parts, *tiles),
-        1,
-        (VMEM, SMEM),
+        jax.ShapeDtypeStruct((n_col, groups, width, order), BF16),
+        (me, columns, parts, *tiles),
+        2,
     )
     vectors = lax.all_to_all(copies, "col", 0, 0)
     filtered, coeffs = call(

time: 78.2 us -> 65.9 us (0.84)
  starting transfers between devices: 23.9 us -> 19.9 us
  waiting for transfers between devices: 31.8 us -> 28.1 us
  blocking collectives: 11.3 us -> 9.05 us
  local copies, waits for them, and re-layouts: 2.57 us -> 1.03 us
    ppermute x12 -> x15, waiting for transfers between devices: 31 us -> 20.5 us  [exchanged(): lax.ppermute(value, axis, [(i, i ^ q) for i in range(lax.axis_size(axis))])]
    all_to_all x1, waiting for transfers between devices: 0.01 us -> 5.19 us  [per_device(): lax.all_to_all(parts.reshape(n_row * n_col, width, order), both, 0, 0)]
    all_to_all x1, starting transfers between devices: 7.3 us -> 4.89 us  [per_device(): lax.all_to_all(parts.reshape(n_row * n_col, width, order), both, 0, 0)]
    all_to_all x1, starting transfers between devices: 5.78 us -> 3.54 us  [per_device(): vectors = lax.all_to_all(copies, 'col', 0, 0)]
    all_to_all x1, blocking collectives: 11.3 us -> 9.05 us  [per_device(): squares = lax.all_to_all(squares, both, 0, 0)]
    all_to_all x1, waiting for transfers between devices: 0.85 us -> 2.47 us  [per_device(): vectors = lax.all_to_all(copies, 'col', 0, 0)]
    unnamed x7 -> x9, local copies, waits for them, and re-layouts: 2.48 us -> 0.86 us
    ppermute x12 -> x15, starting transfers between devices: 10.8 us -> 11.4 us  [exchanged(): lax.ppermute(value, axis, [(i, i ^ q) for i in range(lax.axis_size(axis))])]
  transfers between devices with their start and end apart: 14 -> 17, of which waited for: 8 -> 9; matrix products, arithmetic and copies ran while one was open for 0% -> 1% of each run, Pallas kernels for 0% -> 1%
where the time goes in v2:
time: 65.9 us; the launch traced here: 65.6 us
  waiting for transfers between devices  28.1 us (43%)
  starting transfers between devices  19.9 us (30%)
  blocking collectives  9.05 us (14%)
  Pallas kernels  6.65 us (10%)
  local copies, waits for them, and re-layouts  1.03 us (2%)
  between operations  0.72 us (1%)
    ppermute x15, waiting for transfers between devices, exchanged(): lax.ppermute(value, axis, [(i, i ^ q) for i in range(lax.axis_size(axis))])  20.5 us
    ppermute x15, starting transfers between devices, exchanged(): lax.ppermute(value, axis, [(i, i ^ q) for i in range(lax.axis_size(axis))])  11.4 us
    all_to_all x1, blocking collectives, per_device(): squares = lax.all_to_all(squares, both, 0, 0)  9.05 us
    pallas_call x4, Pallas kernels, call(): pl.pallas_call(kernel, out_shape=out, in_specs=[SMEM] * n_smem + [VMEM] *...  5.2 us
    all_to_all x1, waiting for transfers between devices, per_device(): lax.all_to_all(parts.reshape(n_row * n_col, width, order), both, 0, 0)  5.19 us
    all_to_all x1, starting transfers between devices, per_device(): lax.all_to_all(parts.reshape(n_row * n_col, width, order), both, 0, 0)  4.89 us
    all_to_all x1, starting transfers between devices, per_device(): vectors = lax.all_to_all(copies, 'col', 0, 0)  3.54 us
    all_to_all x1, waiting for transfers between devices, per_device(): vectors = lax.all_to_all(copies, 'col', 0, 0)  2.47 us
  transfers between devices with their start and end apart: 17, of which 9 were waited for; matrix products, arithmetic and copies ran while one was open for 1% of the time, Pallas kernels for 1%

profile of v2, /device:TPU:0, one launch (start us, length us, event | category | flops | bytes accessed | tf_op | source)
XLA Modules:
  0.0 65.6 jit_solution(1576486989966926820)
XLA Ops:
  0.6 3.0 %collective-permute-start.4 = (bf16[1024,128]{1,0:T(8,128)(2,1)}, bf16[1024,128]{1,0:T(8,128)(2,1)S(1)}, u32[]{:S(2)}, u32[]{:S(2)}) collective-permute-start(bf16[1024,128]{1,0:T(8,128)(2,1)} %bitcast.14), channel_id=1, source_target_pairs={{0,16},{8,24},{16,0},{24,8},{1,17},{9,25},{17,1},{25,9},{2,18},{10... | collective-permute-start | bytes 786440 | tf_op jit(solution)/shard_map/ppermute | solution.py:162
  3.7 0.8 %copy-done.2 = bf16[128,128]{1,0:T(8,128)(2,1)S(1)} copy-done((bf16[128,128]{1,0:T(8,128)(2,1)S(1)}, bf16[128,128]{1,0:T(8,128)(2,1)}, u32[]{:S(2)}) %copy-start.2) | copy-done | bytes 32792
  4.4 0.8 %shard_map.59 = bf16[4,8,32,128]{3,2,1,0:T(8,128)(2,1)} custom-call(bf16[128,128]{1,0:T(8,128)(2,1)S(1)} %copy-done.2), custom_call_target="tpu_custom_call" | custom-call | tf_op jit(solution)/shard_map/pallas_call | solution.py:25
  5.2 4.9 %all-to-all-start = ((bf16[32,32,128]{2,1,0:T(8,128)(2,1)}), bf16[32,32,128]{2,1,0:T(8,128)(2,1)S(1)}, u32[]{:S(2)}, u32[]{:S(2)}) async-start(bf16[32,32,128]{2,1,0:T(8,128)(2,1)} %bitcast.5), calls=%async_computation | async-start | bytes 524288 | tf_op jit(solution)/shard_map/all_to_all | solution.py:180
  10.1 0.3 collective-permute-start.3
  10.5 0.3 collective-permute-start.5
  10.7 0.1 copy.8
  10.8 0.1 reshape.16
  10.9 1.8 %collective-permute-start.1 = (s32[8]{0:T(128)S(1)}, s32[8]{0:T(128)S(1)}, u32[]{:S(2)}, u32[]{:S(2)}) collective-permute-start(s32[8]{0:T(128)S(1)} %reshape.16), channel_id=1, source_target_pairs={{0,16},{8,24},{16,0},{24,8},{1,17},{9,25},{17,1},{25,9},{2,18},{10... | collective-permute-start | bytes 104 | tf_op jit(solution)/shard_map/ppermute | solution.py:162
  12.7 0.1 stack_reshape.3
  12.8 1.6 %collective-permute-done.1 = s32[8]{0:T(128)S(1)} collective-permute-done((s32[8]{0:T(128)S(1)}, s32[8]{0:T(128)S(1)}, u32[]{:S(2)}, u32[]{:S(2)}) %collective-permute-start.1) | collective-permute-done | bytes 64 | tf_op jit(solution)/shard_map/ppermute | solution.py:162
  14.5 1.1 %collective-permute-done.2 = s32[8]{0:T(128)S(1)} collective-permute-done((s32[8]{0:T(128)S(1)}, s32[8]{0:T(128)S(1)}, u32[]{:S(2)}, u32[]{:S(2)}) %collective-permute-start.2) | collective-permute-done | bytes 64 | tf_op jit(solution)/shard_map/ppermute | solution.py:162
  15.6 5.2 %all-to-all-done = bf16[32,32,128]{2,1,0:T(8,128)(2,1)S(1)} async-done(((bf16[32,32,128]{2,1,0:T(8,128)(2,1)}), bf16[32,32,128]{2,1,0:T(8,128)(2,1)S(1)}, u32[]{:S(2)}, u32[]{:S(2)}) %all-to-all-start) | async-done | bytes 262176 | tf_op jit(solution)/shard_map/all_to_all | solution.py:180
  20.8 1.9 %shard_map.60 = bf16[8,4,32,128]{3,2,1,0:T(8,128)(2,1)} custom-call(s32[2]{0:T(128)S(1)} %pad_add_fusion.1.me_ref, s32[4,8]{1,0:T(4,128)S(1)} %pad_add_fusion.columns_ref, bf16[4,8,32,128]{3,2,1,0:T(8,128)(2,1)S(1)} %bitcast.12, bf16[1024,128]{1,0:T(8,128)(2,1)S(1)} %bitcast.16, bf16[1024,128]{1,0:T(8,128)(2,1)S(1)} %collective-permute-done.3.refs_1_, ...), custom_call_target="tpu_custom_call" | custom-call | tf_op jit(solution)/shard_map/pallas_call | solution.py:25
  22.7 3.5 %all-to-all-start.1 = ((bf16[8,4,32,128]{3,2,1,0:T(8,128)(2,1)}), bf16[8,4,32,128]{3,2,1,0:T(8,128)(2,1)S(1)}, u32[]{:S(2)}, u32[]{:S(2)}) async-start(bf16[8,4,32,128]{3,2,1,0:T(8,128)(2,1)} %shard_map.60), calls=%async_computation.1 | async-start | bytes 524288 | tf_op jit(solution)/shard_map/all_to_all | solution.py:192
  26.3 0.6 collective-permute-start.7
  26.9 0.1 collective-permute-start.6
  27.0 4.5 %collective-permute-done.7.refs_6_.refs_2_ = bf16[128,512]{1,0:T(8,128)(2,1)S(1)} collective-permute-done((bf16[128,512]{1,0:T(8,128)(2,1)S(1)}, bf16[128,512]{1,0:T(8,128)(2,1)S(1)}, u32[]{:S(2)}, u32[]{:S(2)}) %collective-permute-start.7) | collective-permute-done | bytes 131104 | tf_op jit(solution)/shard_map/ppermute | solution.py:162
  31.5 1.3 %collective-permute-done.8.refs_7_.refs_3_ = bf16[128,512]{1,0:T(8,128)(2,1)S(1)} collective-permute-done((bf16[128,512]{1,0:T(8,128)(2,1)S(1)}, bf16[128,512]{1,0:T(8,128)(2,1)S(1)}, u32[]{:S(2)}, u32[]{:S(2)}) %collective-permute-start.8) | collective-permute-done | bytes 131104 | tf_op jit(solution)/shard_map/ppermute | solution.py:162
  32.9 2.5 %all-to-all-done.1.vectors_ref = bf16[8,4,32,128]{3,2,1,0:T(8,128)(2,1)S(1)} async-done(((bf16[8,4,32,128]{3,2,1,0:T(8,128)(2,1)}), bf16[8,4,32,128]{3,2,1,0:T(8,128)(2,1)S(1)}, u32[]{:S(2)}, u32[]{:S(2)}) %all-to-all-start.1) | async-done | bytes 262176 | tf_op jit(solution)/shard_map/all_to_all | solution.py:192
  35.3 1.4 %shard_map.61 = (f32[4,32,128]{2,1,0:T(8,128)S(1)}, f32[32,512]{1,0:T(8,128)S(1)}) custom-call(s32[2]{0:T(128)S(1)} %pad_add_fusion.1.me_ref, s32[4,8]{1,0:T(4,128)S(1)} %pad_add_fusion.columns_ref, bf16[4,8,32,128]{3,2,1,0:T(8,128)(2,1)S(1)} %bitcast.13, bf16[8,4,32,128]{3,2,1,0:T(8,128)(2,1)S(1)} %all-to-all-done.1.vectors_ref, ...), custom_call_target="tpu_custom_call" | custom-call | tf_op jit(solution)/shard_map/pallas_call | solution.py:25
  36.8 1.4 %collective-permute-start.9 = (f32[32,512]{1,0:T(8,128)S(1)}, f32[32,512]{1,0:T(8,128)S(1)}, u32[]{:S(2)}, u32[]{:S(2)}) collective-permute-start(f32[32,512]{1,0:T(8,128)S(1)} %get-tuple-element.9), channel_id=1, source_target_pairs={{0,1},{1,0},{2,3},{3,2},{4,5},{5,4},{6,7},{7,6},{8,9},{9,8},{10,11... | collective-permute-start | bytes 196616 | tf_op jit(solution)/shard_map/ppermute | solution.py:162
  38.2 2.9 %collective-permute-done.9 = f32[32,512]{1,0:T(8,128)S(1)} collective-permute-done((f32[32,512]{1,0:T(8,128)S(1)}, f32[32,512]{1,0:T(8,128)S(1)}, u32[]{:S(2)}, u32[]{:S(2)}) %collective-permute-start.9) | collective-permute-done | bytes 65568 | tf_op jit(solution)/shard_map/ppermute | solution.py:162
  41.1 1.1 %collective-permute-start.10 = (f32[32,512]{1,0:T(8,128)S(1)}, f32[32,512]{1,0:T(8,128)S(1)}, u32[]{:S(2)}, u32[]{:S(2)}) collective-permute-start(f32[32,512]{1,0:T(8,128)S(1)} %add.9), channel_id=1, source_target_pairs={{0,2},{1,3},{2,0},{3,1},{4,6},{5,7},{6,4},{7,5},{8,10},{9,11},{10,... | collective-permute-start | bytes 196616 | tf_op jit(solution)/shard_map/ppermute | solution.py:162
  42.2 3.9 %collective-permute-done.10 = f32[32,512]{1,0:T(8,128)S(1)} collective-permute-done((f32[32,512]{1,0:T(8,128)S(1)}, f32[32,512]{1,0:T(8,128)S(1)}, u32[]{:S(2)}, u32[]{:S(2)}) %collective-permute-start.10) | collective-permute-done | bytes 65568 | tf_op jit(solution)/shard_map/ppermute | solution.py:162
  46.1 0.8 %collective-permute-start.11 = (f32[32,512]{1,0:T(8,128)S(1)}, f32[32,512]{1,0:T(8,128)S(1)}, u32[]{:S(2)}, u32[]{:S(2)}) collective-permute-start(f32[32,512]{1,0:T(8,128)S(1)} %add.10), channel_id=1, source_target_pairs={{0,4},{1,5},{2,6},{3,7},{4,0},{5,1},{6,2},{7,3},{8,12},{9,13},{10,... | collective-permute-start | bytes 196616 | tf_op jit(solution)/shard_map/ppermute | solution.py:162
  46.9 5.1 %collective-permute-done.11 = f32[32,512]{1,0:T(8,128)S(1)} collective-permute-done((f32[32,512]{1,0:T(8,128)S(1)}, f32[32,512]{1,0:T(8,128)S(1)}, u32[]{:S(2)}, u32[]{:S(2)}) %collective-permute-start.11) | collective-permute-done | bytes 65568 | tf_op jit(solution)/shard_map/ppermute | solution.py:162
  52.1 1.0 %shard_map.62 = (f32[32,640]{1,0:T(8,128)S(1)}, f32[32,640]{1,0:T(8,128)S(1)}, f32[32,640]{1,0:T(8,128)S(1)}, f32[32,640]{1,0:T(8,128)S(1)}, f32[32,1,128]{2,1,0:T(1,128)S(1)}) custom-call(s32[2]{0:T(128)S(1)} %pad_add_fusion.1.me_ref, f32[32,512]{1,0:T(8,128)S(1)} %add.11.coeffs_ref, f32[4,32,128]{2,1,0:T(8,128)S(1)} %get-tuple-element.10.filtered_ref, ...), custom_call_target="tpu_custom_call" | custom-call | tf_op jit(solution)/shard_map/pallas_call | solution.py:25
  53.2 0.6 collective-permute-start.13
  53.8 1.3 %collective-permute-start.14 = (f32[32,640]{1,0:T(8,128)S(1)}, f32[32,640]{1,0:T(8,128)S(1)}, u32[]{:S(2)}, u32[]{:S(2)}) collective-permute-start(f32[32,640]{1,0:T(8,128)S(1)} %get-tuple-element.15), channel_id=1, source_target_pairs={{0,24},{8,16},{16,8},{24,0},{1,25},{9,17},{17,9},{25,1},{2,26},{10... | collective-permute-start | bytes 245768 | tf_op jit(solution)/shard_map/ppermute | solution.py:162
  55.0 9.1 %all_to_all.15.squares_ref = f32[32,1,128]{2,1,0:T(1,128)S(1)} all-to-all(f32[32,1,128]{2,1,0:T(1,128)S(1)} %get-tuple-element.11), channel_id=1, replica_groups=mesh['row'=4,'col'=8] {'row','col'}, dimensions={0} | all-to-all | bytes 32768 | tf_op jit(solution)/shard_map/all_to_all | solution.py:214
  64.1 1.4 %shard_map.63 = (f32[128,128]{1,0:T(8,128)}, f32[512,128]{1,0:T(8,128)}) custom-call(s32[2]{0:T(128)S(1)} %pad_add_fusion.1.me_ref, f32[32,1,128]{2,1,0:T(1,128)S(1)} %all_to_all.15.squares_ref, f32[32,640]{1,0:T(8,128)S(1)} %get-tuple-element.12.refs_0_, f32[32,640]{1,0:T(8,128)S(1)} %collective-permute-done.12.refs_1_, ...), custom_call_target="tpu_custom_call" | custom-call | tf_op jit(solution)/shard_map/pallas_call | solution.py:221
  (24 shorter events, 0.2 us)
Async XLA Ops:
  0.6 9.8 %collective-permute-start.4 = (bf16[1024,128]{1,0:T(8,128)(2,1)}, bf16[1024,128]{1,0:T(8,128)(2,1)S(1)}, u32[]{:S(2)}, u32[]{:S(2)}) collective-permute-start(bf16[1024,128]{1,0:T(8,128)(2,1)} %bitcast.14), channel_id=1, source_target_pairs={{0,16},{8,24},{16,0},{24,8},{1,17},{9,25},{17,1},{25,9},{2,18},{10... | collective-permute-start | bytes 786440 | tf_op jit(solution)/shard_map/ppermute | solution.py:162
  3.7 0.8 %copy-start.2 = (bf16[128,128]{1,0:T(8,128)(2,1)S(1)}, bf16[128,128]{1,0:T(8,128)(2,1)}, u32[]{:S(2)}) copy-start(bf16[128,128]{1,0:T(8,128)(2,1)} %start_ref.1) | copy-start | bytes 98308
  5.2 4.9 %copy-start = (bf16[1,4,1,2,128,128]{5,4,3,2,1,0:T(8,128)(2,1)S(1)}, bf16[1,4,1,2,128,128]{5,4,3,2,1,0:T(8,128)(2,1)}, u32[]{:S(2)}) copy-start(bf16[1,4,1,2,128,128]{5,4,3,2,1,0:T(8,128)(2,1)} %param.5) | copy-start | bytes 786436
  5.2 5.5 %copy-start.3 = (s32[1,4,1,2]{1,3,2,0:T(2,128)S(1)}, s32[1,4,1,2]{1,3,2,0:T(2,128)}, u32[]{:S(2)}) copy-start(s32[1,4,1,2]{1,3,2,0:T(2,128)} %param.6) | copy-start | bytes 100
  5.2 15.5 %all-to-all-start = ((bf16[32,32,128]{2,1,0:T(8,128)(2,1)}), bf16[32,32,128]{2,1,0:T(8,128)(2,1)S(1)}, u32[]{:S(2)}, u32[]{:S(2)}) async-start(bf16[32,32,128]{2,1,0:T(8,128)(2,1)} %bitcast.5), calls=%async_computation | async-start | bytes 524288 | tf_op jit(solution)/shard_map/all_to_all | solution.py:180
  10.1 5.4 %collective-permute-start.3 = (bf16[1024,128]{1,0:T(8,128)(2,1)S(1)}, bf16[1024,128]{1,0:T(8,128)(2,1)S(1)}, u32[]{:S(2)}, u32[]{:S(2)}) collective-permute-start(bf16[1024,128]{1,0:T(8,128)(2,1)S(1)} %bitcast.15), channel_id=1, source_target_pairs={{0,8},{8,0},{16,24},{24,16},{1,9},{9,1},{17,25},{25,17},{2,10},{10... | collective-permute-start | bytes 786440 | tf_op jit(solution)/shard_map/ppermute | solution.py:162
  10.5 10.3 %collective-permute-start.5 = (bf16[1024,128]{1,0:T(8,128)(2,1)S(1)}, bf16[1024,128]{1,0:T(8,128)(2,1)S(1)}, u32[]{:S(2)}, u32[]{:S(2)}) collective-permute-start(bf16[1024,128]{1,0:T(8,128)(2,1)S(1)} %collective-permute-done.4.refs_2_), channel_id=1, source_target_pairs={{0,8},{8,0},{16,24},{24,16},{1,9},{9,1},{17,25},{25,17},{2,10},{10... | collective-permute-start | bytes 786440 | tf_op jit(solution)/shard_map/ppermute | solution.py:162
  10.9 3.5 %collective-permute-start.1 = (s32[8]{0:T(128)S(1)}, s32[8]{0:T(128)S(1)}, u32[]{:S(2)}, u32[]{:S(2)}) collective-permute-start(s32[8]{0:T(128)S(1)} %reshape.16), channel_id=1, source_target_pairs={{0,16},{8,24},{16,0},{24,8},{1,17},{9,25},{17,1},{25,9},{2,18},{10... | collective-permute-start | bytes 104 | tf_op jit(solution)/shard_map/ppermute | solution.py:162
  12.7 1.8 %collective-permute-start = (s32[8]{0:T(128)S(1)}, s32[8]{0:T(128)S(1)}, u32[]{:S(2)}, u32[]{:S(2)}) collective-permute-start(s32[8]{0:T(128)S(1)} %reshape.16), channel_id=1, source_target_pairs={{0,8},{8,0},{16,24},{24,16},{1,9},{9,1},{17,25},{25,17},{2,10},{10... | collective-permute-start | bytes 104 | tf_op jit(solution)/shard_map/ppermute | solution.py:162
  14.4 1.1 %collective-permute-start.2 = (s32[8]{0:T(128)S(1)}, s32[8]{0:T(128)S(1)}, u32[]{:S(2)}, u32[]{:S(2)}) collective-permute-start(s32[8]{0:T(128)S(1)} %collective-permute-done.1), channel_id=1, source_target_pairs={{0,8},{8,0},{16,24},{24,16},{1,9},{9,1},{17,25},{25,17},{2,10},{10... | collective-permute-start | bytes 104 | tf_op jit(solution)/shard_map/ppermute | solution.py:162
  22.7 3.6 %copy-start.1 = (bf16[128,512]{1,0:T(8,128)(2,1)S(1)}, bf16[128,512]{1,0:T(8,128)(2,1)}, u32[]{:S(2)}) copy-start(bf16[128,512]{1,0:T(8,128)(2,1)} %refs_0_.1) | copy-start | bytes 393220
  22.7 12.6 %all-to-all-start.1 = ((bf16[8,4,32,128]{3,2,1,0:T(8,128)(2,1)}), bf16[8,4,32,128]{3,2,1,0:T(8,128)(2,1)S(1)}, u32[]{:S(2)}, u32[]{:S(2)}) async-start(bf16[8,4,32,128]{3,2,1,0:T(8,128)(2,1)} %shard_map.60), calls=%async_computation.1 | async-start | bytes 524288 | tf_op jit(solution)/shard_map/all_to_all | solution.py:192
  26.3 5.2 %collective-permute-start.7 = (bf16[128,512]{1,0:T(8,128)(2,1)S(1)}, bf16[128,512]{1,0:T(8,128)(2,1)S(1)}, u32[]{:S(2)}, u32[]{:S(2)}) collective-permute-start(bf16[128,512]{1,0:T(8,128)(2,1)S(1)} %copy-done.1), channel_id=1, source_target_pairs={{0,16},{8,24},{16,0},{24,8},{1,17},{9,25},{17,1},{25,9},{2,18},{10... | collective-permute-start | bytes 393224 | tf_op jit(solution)/shard_map/ppermute | solution.py:162
  26.9 4.6 %collective-permute-start.6 = (bf16[128,512]{1,0:T(8,128)(2,1)S(1)}, bf16[128,512]{1,0:T(8,128)(2,1)S(1)}, u32[]{:S(2)}, u32[]{:S(2)}) collective-permute-start(bf16[128,512]{1,0:T(8,128)(2,1)S(1)} %copy-done.1), channel_id=1, source_target_pairs={{0,8},{8,0},{16,24},{24,16},{1,9},{9,1},{17,25},{25,17},{2,10},{10... | collective-permute-start | bytes 393224 | tf_op jit(solution)/shard_map/ppermute | solution.py:162
  31.5 1.3 %collective-permute-start.8 = (bf16[128,512]{1,0:T(8,128)(2,1)S(1)}, bf16[128,512]{1,0:T(8,128)(2,1)S(1)}, u32[]{:S(2)}, u32[]{:S(2)}) collective-permute-start(bf16[128,512]{1,0:T(8,128)(2,1)S(1)} %collective-permute-done.7.refs_6_.refs_2_), channel_id=1, source_target_pairs={{0,8},{8,0},{16,24},{24,16},{1,9},{9,1},{17,25},{25,17},{2,10},{10... | collective-permute-start | bytes 393224 | tf_op jit(solution)/shard_map/ppermute | solution.py:162
  36.8 4.3 %collective-permute-start.9 = (f32[32,512]{1,0:T(8,128)S(1)}, f32[32,512]{1,0:T(8,128)S(1)}, u32[]{:S(2)}, u32[]{:S(2)}) collective-permute-start(f32[32,512]{1,0:T(8,128)S(1)} %get-tuple-element.9), channel_id=1, source_target_pairs={{0,1},{1,0},{2,3},{3,2},{4,5},{5,4},{6,7},{7,6},{8,9},{9,8},{10,11... | collective-permute-start | bytes 196616 | tf_op jit(solution)/shard_map/ppermute | solution.py:162
  41.1 5.0 %collective-permute-start.10 = (f32[32,512]{1,0:T(8,128)S(1)}, f32[32,512]{1,0:T(8,128)S(1)}, u32[]{:S(2)}, u32[]{:S(2)}) collective-permute-start(f32[32,512]{1,0:T(8,128)S(1)} %add.9), channel_id=1, source_target_pairs={{0,2},{1,3},{2,0},{3,1},{4,6},{5,7},{6,4},{7,5},{8,10},{9,11},{10,... | collective-permute-start | bytes 196616 | tf_op jit(solution)/shard_map/ppermute | solution.py:162
  46.1 5.9 %collective-permute-start.11 = (f32[32,512]{1,0:T(8,128)S(1)}, f32[32,512]{1,0:T(8,128)S(1)}, u32[]{:S(2)}, u32[]{:S(2)}) collective-permute-start(f32[32,512]{1,0:T(8,128)S(1)} %add.10), channel_id=1, source_target_pairs={{0,4},{1,5},{2,6},{3,7},{4,0},{5,1},{6,2},{7,3},{8,12},{9,13},{10,... | collective-permute-start | bytes 196616 | tf_op jit(solution)/shard_map/ppermute | solution.py:162
  53.1 11.0 %collective-permute-start.12 = (f32[32,640]{1,0:T(8,128)S(1)}, f32[32,640]{1,0:T(8,128)S(1)}, u32[]{:S(2)}, u32[]{:S(2)}) collective-permute-start(f32[32,640]{1,0:T(8,128)S(1)} %get-tuple-element.13), channel_id=1, source_target_pairs={{0,8},{8,0},{16,24},{24,16},{1,9},{9,1},{17,25},{25,17},{2,10},{10... | collective-permute-start | bytes 245768 | tf_op jit(solution)/shard_map/ppermute | solution.py:162
  53.2 10.9 %collective-permute-start.13 = (f32[32,640]{1,0:T(8,128)S(1)}, f32[32,640]{1,0:T(8,128)S(1)}, u32[]{:S(2)}, u32[]{:S(2)}) collective-permute-start(f32[32,640]{1,0:T(8,128)S(1)} %get-tuple-element.14), channel_id=1, source_target_pairs={{0,16},{8,24},{16,0},{24,8},{1,17},{9,25},{17,1},{25,9},{2,18},{10... | collective-permute-start | bytes 245768 | tf_op jit(solution)/shard_map/ppermute | solution.py:162
  53.8 10.3 %collective-permute-start.14 = (f32[32,640]{1,0:T(8,128)S(1)}, f32[32,640]{1,0:T(8,128)S(1)}, u32[]{:S(2)}, u32[]{:S(2)}) collective-permute-start(f32[32,640]{1,0:T(8,128)S(1)} %get-tuple-element.15), channel_id=1, source_target_pairs={{0,24},{8,16},{16,8},{24,0},{1,25},{9,17},{17,9},{25,1},{2,26},{10... | collective-permute-start | bytes 245768 | tf_op jit(solution)/shard_map/ppermute | solution.py:162

commit v3 on v0

v3 whole, which is shorter than its diff:
```python
import functools

import jax
import jax.numpy as jnp
from jax import lax
from jax.experimental import pallas as pl
from jax.experimental.pallas import tpu as pltpu
from jax.sharding import PartitionSpec as P

F32 = jnp.float32
BF16 = jnp.bfloat16
PAD = 16
LINES = 8
VMEM = pl.BlockSpec(memory_space=pltpu.VMEM)
BOTH = ("row", "col")


def nbytes(tree):
    return sum(a.size * a.dtype.itemsize for a in jax.tree.leaves(tree))


def call(kernel, out, args, scratch=()):
    held = [jax.ShapeDtypeStruct(shape, kind) for shape, kind in scratch]
    room = 2 * (nbytes(args) + nbytes(out) + nbytes(held)) + 8 * 2**20
    return pl.pallas_call(
        kernel,
        out_shape=out,
        in_specs=[VMEM] * len(args),
        out_specs=jax.tree.map(lambda _: VMEM, out),
        scratch_shapes=[pltpu.VMEM(shape, kind) for shape, kind in scratch],
        compiler_params=pltpu.CompilerParams(vmem_limit_bytes=min(room, 56 * 2**20)),
    )(*args)


def position(lanes):
    row, col = lax.axis_index("row"), lax.axis_index("col")
    return row >> 1, row & 1, col >> (lanes - 1), col & (lanes - 1)


def place(entry, core):
    (even_q, even_u), (odd_q, odd_u) = entry
    return jnp.where(core == 0, even_q, odd_q), jnp.where(core == 0, even_u, odd_u)


def nt(a, b):
    return lax.dot_general(a, b, (((1,), (1,)), ((), ())), preferred_element_type=F32)


def pieces(value):
    high = value.astype(BF16)
    rest = value - high.astype(F32)
    middle = rest.astype(BF16)
    low = (rest - middle.astype(F32)).astype(BF16)
    return jnp.concatenate([high, middle, low], axis=0)


def joined(stacked):
    third = stacked.shape[0] // 3
    return (stacked[2 * third :] + stacked[third : 2 * third]) + stacked[:third]


def each(count, body):
    if count <= 4:
        for i in range(count):
            body(i)
    else:
        pl.loop(0, count)(body)


def prepare(lanes, width, columns_ref, start_ref, parts_ref):
    n_block, n_col, rows, order = parts_ref.shape
    groups, slots = columns_ref.shape
    lane = lax.broadcasted_iota(jnp.int32, (PAD, order), 1)
    numbers = jnp.zeros(lane.shape, jnp.int32)
    for p in range(groups):
        for s in range(slots):
            numbers = jnp.where(lane == p * slots + s, columns_ref[p, s], numbers)
    numbers = numbers.astype(F32).astype(BF16)
    turned = start_ref[...].astype(F32).T
    for r in range(n_block):
        for u in range(lanes):
            first_row = (r * lanes + u) * width
            part = turned[first_row : first_row + width].astype(BF16)
            for c in range(u, n_col, lanes):
                parts_ref[r, c, :width] = part
                parts_ref[r, c, rows - PAD :] = numbers


def multiply(near, lanes, slots, columns_ref, segment, tiles, sums_ref):
    groups, order = sums_ref.shape[1], sums_ref.shape[3]
    block, core, _, _ = position(lanes)
    for i, tile_ref in tiles:
        q, u = place(near[i], core)

        def row(p):
            total = None
            for s in range(slots):
                start = (p * slots + s) * order
                if not isinstance(start, int):
                    start = pl.multiple_of(start, order)
                picked = segment(block ^ q, columns_ref[i, p * slots + s, 0])
                term = nt(picked, tile_ref[pl.ds(start, order), :])
                total = term if total is None else total + term
            sums_ref[u, p] += total

        each(groups, row)


def first(near, early, lanes, slots, parts_ref, *refs):
    tiles, (sums_ref, columns_ref, start_ref) = refs[:early], refs[early:]
    _, groups, width, order = sums_ref.shape
    block, core, me_z, me_lane = position(lanes)
    rows = parts_ref.shape[2]
    for i, entry in enumerate(near):
        q, u = place(entry, core)
        numbers = parts_ref[block ^ q, me_z * lanes + (me_lane ^ u), rows - PAD :]
        columns_ref[i] = numbers.astype(F32)[:LINES].T.astype(jnp.int32)
    for u in range(lanes):
        for r in range(parts_ref.shape[0]):
            start_ref[u, r] = parts_ref[r, me_z * lanes + (me_lane ^ u), :width]
    sums_ref[...] = jnp.zeros_like(sums_ref)
    multiply(
        near, lanes, slots, columns_ref, lambda b, c: parts_ref[b, c, :width],
        list(enumerate(tiles)), sums_ref,
    )


def rest(near, early, slots, columns_ref, parts_ref, before_ref, *refs):
    tiles, (keep_ref, give_ref, sums_ref) = refs[: len(near) - early], refs[len(near) - early :]
    lanes, n_block, width, _ = keep_ref.shape
    _, core, _, _ = position(lanes)
    sums_ref[...] = before_ref[...]
    multiply(
        near, lanes, slots, columns_ref, lambda b, c: parts_ref[b, c, :width],
        list(enumerate(tiles, early)), sums_ref,
    )
    for u in range(lanes):
        for r in range(n_block):
            keep_ref[u, r] = sums_ref[u, 2 * r + core]
            give_ref[u, r] = sums_ref[u, 2 * r + (1 - core)]


def second(near, slots, n_vectors, columns_ref, start_ref, *refs):
    count = len(near)
    vectors, tiles, refs = refs[:n_vectors], refs[n_vectors : n_vectors + count], refs[n_vectors + count :]
    keep_ref, give_ref, sums_ref = refs[:3]
    lanes, n_block, _, _ = keep_ref.shape
    _, core, me_z, me_lane = position(lanes)
    if n_vectors > 1:
        all_ref = refs[3]
        for k in range(n_vectors):
            all_ref[me_z ^ k] = vectors[k][...]
    else:
        all_ref = vectors[0]

    def segment(b, c):
        return all_ref[c >> (lanes - 1), (c & (lanes - 1)) ^ me_lane, b]

    sums_ref[...] = jnp.zeros_like(sums_ref)
    multiply(near, lanes, slots, columns_ref, segment, list(enumerate(tiles)), sums_ref)
    for u in range(lanes):
        for r in range(n_block):
            keep_ref[u, r] = 2.0 * sums_ref[u, 2 * r + core] - start_ref[u, r].astype(F32)
            give_ref[u, r] = 2.0 * sums_ref[u, 2 * r + (1 - core)]


def project(near, keep_ref, given_ref, *refs):
    history, (filtered_ref, coeffs_keep_ref, coeffs_give_ref) = refs[: len(near)], refs[len(near) :]
    lanes = keep_ref.shape[0]
    block, core, _, _ = position(lanes)
    filtered_ref[...] = keep_ref[...] + given_ref[...]
    total = None
    for i, entry in enumerate(near):
        q, u = place(entry, core)
        split = pieces(filtered_ref[u, block ^ q])
        term = joined(jnp.dot(split, history[i][...], preferred_element_type=F32))
        total = term if total is None else total + term
    half = total.shape[1] // 2
    low, high = total[:, :half], total[:, half:]
    coeffs_keep_ref[...] = jnp.where(core == 0, low, high)
    coeffs_give_ref[...] = jnp.where(core == 0, high, low)


def clean(near, mine_ref, mate_ref, filtered_ref, *refs):
    count = len(near)
    history, outs, squares_ref = refs[:count], refs[count : 2 * count], refs[2 * count]
    lanes, _, width, order = filtered_ref.shape
    block, core, _, me_lane = position(lanes)
    mine, mate = mine_ref[...], mate_ref[...]
    coeffs = jnp.concatenate(
        [jnp.where(core == 0, mine, mate), jnp.where(core == 0, mate, mine)], axis=1
    )
    stored = coeffs.shape[1]
    split = pieces(coeffs)
    squares = jnp.zeros((width, order), F32)
    for i, entry in enumerate(near):
        q, u = place(entry, core)
        cleaned = filtered_ref[u, block ^ q] - joined(nt(split, history[i][...]))
        squares = squares + cleaned * cleaned
        outs[i][:, :stored] = coeffs
        outs[i][:, stored:] = cleaned
    sums = jnp.sum(squares.T, axis=0, keepdims=True)
    n_vectors = squares_ref.shape[2]
    line = jnp.concatenate([sums] * (n_vectors // width), axis=1)
    lane = lax.broadcasted_iota(jnp.int32, line.shape, 1)
    begin = (block * lanes + me_lane) * width
    line = jnp.where((lane >= begin) & (lane < begin + width), line, 0.0)
    squares_ref[...] = jnp.broadcast_to(line[:, None, :], squares_ref.shape)


def finish(near, lanes, total_rows, squares_ref, *refs):
    slabs, (block_ref, out_ref, whole_ref) = refs[:-3], refs[-3:]
    width = slabs[0].shape[0]
    stored = out_ref.shape[0]
    block, core, _, me_lane = position(lanes)
    for slab, entry in zip(slabs, near):
        q, u = place(entry, core)
        start = ((block ^ q) * lanes + (me_lane ^ u)) * width
        whole_ref[pl.ds(pl.multiple_of(start, width), width), :] = slab[...]
    sums = jnp.sum(squares_ref[...], axis=0)[:1]
    lengths = jnp.sqrt(sums / total_rows + 1e-05)
    out_ref[...] = whole_ref[:, :stored].T
    block_ref[...] = whole_ref[:, stored:].T / lengths


def neighbours(n_block, lanes):
    found = [((0, 0), (0, 0))]
    bit = n_block // 2
    if lanes == 2:
        found.append(((0, 1), (bit, 0)) if bit else ((0, 1), (0, 1)))
    if lanes == 2 and bit:
        found += [((bit, 0), (0, 1)), ((bit, 1), (bit, 1))]
        bit //= 2
    while bit:
        found += [((a ^ bit, u), (b ^ bit, v)) for (a, u), (b, v) in found]
        bit //= 2
    return found


def crossed(value, entry):
    n_row, n_col = lax.axis_size("row"), lax.axis_size("col")
    pairs = []
    for r in range(n_row):
        q, u = entry[r % 2]
        pairs += [(r * n_col + c, (r ^ (2 * q)) * n_col + (c ^ u)) for c in range(n_col)]
    return lax.ppermute(value, BOTH, pairs)


def spread(found, near):
    while len(found) < len(near):
        found = found + [crossed(a, near[len(found)]) for a in found]
    return found


def swapped(value, q, u):
    n_row, n_col = lax.axis_size("row"), lax.axis_size("col")
    pairs = [(r * n_col + c, (r ^ q) * n_col + (c ^ u)) for r in range(n_row) for c in range(n_col)]
    return lax.ppermute(value, BOTH, pairs)


def per_device(start_block, matrix_tiles, tile_columns, history):
    n_row, n_col = lax.axis_size("row"), lax.axis_size("col")
    _, groups, _, slots, order, _ = matrix_tiles.shape
    n_vectors = start_block.shape[1]
    stored = history.shape[1]
    rows = groups * slots * order
    n_block = n_row // 2
    lanes = 2 if n_col % 2 == 0 else 1
    width = n_vectors // (n_block * lanes)
    members = n_col // lanes
    few = members <= 4
    near = neighbours(n_block, lanes)
    count = len(near)
    early = count - count // 4

    def over_members(value):
        return [value] + [swapped(value, 0, k * lanes) for k in range(1, members)]

    def mate(value):
        return swapped(value, 1, 0)

    plane = lanes == 2 and n_block > 1
    tiles = [matrix_tiles.reshape(rows, order)]
    if plane:
        tiles += lax.optimization_barrier([crossed(tiles[0], entry) for entry in near[1:3]])
        tiles.append(crossed(tiles[1], near[2]))
    tiles = spread(tiles, near)
    tall = -(-width // PAD) * PAD + PAD
    parts = call(
        functools.partial(prepare, lanes, width),
        jax.ShapeDtypeStruct((n_block, n_col, tall, order), BF16),
        (tile_columns.reshape(groups, slots), start_block),
    )
    cores = [
        [(2 * r + core) * n_col + c for r in range(n_block) for c in range(n_col)] for core in range(2)
    ]
    parts = lax.all_to_all(
        parts.reshape(n_block * n_col, tall, order), BOTH, 0, 0, axis_index_groups=cores
    ).reshape(n_block, n_col, tall, order)
    own = [history]
    if plane:
        history, tiles[2] = lax.optimization_barrier((history, tiles[2]))
        own += [crossed(history, entry) for entry in near[1:3]]

    piece = (lanes, n_block, width, order)
    sums = ((lanes, groups, width, order), F32)
    before, columns, start = call(
        functools.partial(first, near, early, lanes, slots),
        [
            jax.ShapeDtypeStruct(sums[0], F32),
            jax.ShapeDtypeStruct((count, order, LINES), jnp.int32),
            jax.ShapeDtypeStruct(piece, BF16),
        ],
        (parts, *tiles[:early]),
    )
    if plane:
        tiles[early], *own = lax.optimization_barrier((tiles[early], *own))
    keep, give = call(
        functools.partial(rest, near, early, slots),
        [jax.ShapeDtypeStruct(piece, F32)] * 2,
        (columns, parts, before, *tiles[early:]),
        [sums],
    )
    if plane:
        keep, own[1] = lax.optimization_barrier((keep, own[1]))
        own.append(crossed(own[1], near[2]))
    own = spread(own, near)
    mine = (keep + mate(give)).astype(BF16)
    if few:
        vectors = over_members(mine)
    else:
        alike = [list(range(u, n_col, lanes)) for u in range(lanes)]
        vectors = [
            lax.all_to_all(
                jnp.broadcast_to(mine, (members,) + piece), "col", 0, 0, axis_index_groups=alike
            )
        ]
    keep, give = call(
        functools.partial(second, near, slots, len(vectors)),
        [jax.ShapeDtypeStruct(piece, F32)] * 2,
        (columns, start, *vectors, *tiles),
        [sums] + ([((members,) + piece, BF16)] if few else []),
    )
    filtered, coeffs, coeffs_give = call(
        functools.partial(project, near),
        [jax.ShapeDtypeStruct(piece, F32)] + [jax.ShapeDtypeStruct((width, stored // 2), F32)] * 2,
        (keep, mate(give), *own),
    )
    coeffs = coeffs + mate(coeffs_give)
    if members == 4:
        zero, one, two, three = over_members(coeffs)
        coeffs = (zero + one) + (two + three)
    else:
        step = lanes
        while step < n_col:
            coeffs = coeffs + swapped(coeffs, 0, step)
            step *= 2
    slab = jax.ShapeDtypeStruct((width, stored + order), F32)
    copies = 1
    while nbytes(slab) > n_row * n_col * copies * n_vectors * 4:
        copies *= 2
    *slabs, squares = call(
        functools.partial(clean, near),
        [slab] * count + [jax.ShapeDtypeStruct((n_row * n_col, copies, n_vectors), F32)],
        (coeffs, mate(coeffs), filtered, *own),
    )
    slabs = [slabs[0]] + [crossed(a, entry) for a, entry in zip(slabs[1:], near[1:])]
    squares = lax.all_to_all(squares, BOTH, 0, 0)
    return call(
        functools.partial(finish, near, lanes, order * n_row * n_col),
        (
            jax.ShapeDtypeStruct((order, n_vectors), F32),
            jax.ShapeDtypeStruct((stored, n_vectors), F32),
        ),
        (squares, *slabs),
        [((n_vectors, stored + order), F32)],
    )


def solution(mesh):
    in_specs = (
        P(("row", "col"), None),
        P("row", None, "col", None, None, None),
        P("row", None, "col", None),
        P(("row", "col"), None),
    )
    out_specs = (P(("row", "col"), None), P())
    return jax.shard_map(
        per_device, mesh=mesh, in_specs=in_specs, out_specs=out_specs, check_vma=False
    )
```

time: 297 us -> 58.6 us (0.20)
  waiting for transfers between devices: 171 us -> 20.6 us
  blocking collectives: 103 us -> 0 us
  starting transfers between devices: 0.12 us -> 31.4 us
  between operations: 13.8 us -> 0.74 us
  matrix products: 5.02 us -> 0 us
  Pallas kernels: 0 us -> 4.68 us
    psum x1 -> x0, waiting for transfers between devices: 129 us -> none  [per_device(): lax.psum(jnp.dot(history_wide.T, filtered, precision=lax.Precision.HIGHES...]
    all_gather x2 -> x0, blocking collectives: 63.5 us -> none  [apply_matrix(): gathered = lax.all_gather(pieces, 'col', axis=0, tiled=True)]
    reduce_scatter x2 -> x0, waiting for transfers between devices: 41.3 us -> none  [apply_matrix(): lax.psum_scatter(partial_value, 'row', scatter_dimension=0, tiled=True)]
    psum x1 -> x0, blocking collectives: 39.2 us -> none  [per_device(): squares = lax.psum(jnp.sum(cleaned * cleaned, axis=0), ('row', 'col'))]
    ppermute x0 -> x19, starting transfers between devices: none -> 22.6 us  [the longest x9 13.4 us: crossed(): return lax.ppermute(value, BOTH, pairs)]
    ppermute x0 -> x19, waiting for transfers between devices: none -> 16.5 us  [the longest x10 9.19 us: swapped(): return lax.ppermute(value, BOTH, pairs)]
    all_to_all x0 -> x2, starting transfers between devices: none -> 8.73 us  [the longest x1 5.11 us: per_device(): lax.all_to_all(parts.reshape(n_block * n_col, tall, order), BOTH, 0, 0, a...]
    dot_general x4 -> x0, matrix products: 5.02 us -> none  [the longest x1 1.86 us: per_device(): jnp.dot(history_wide.T, filtered, precision=lax.Precision.HIGHEST)]
  transfers between devices with their start and end apart: 3 -> 21, of which waited for: 3 -> 13; matrix products, arithmetic and copies ran while one was open for 0% -> 0% of each run, Pallas kernels for 0% -> 4%
where the time goes in v3:
time: 58.6 us; the launch traced here: 58.3 us
  starting transfers between devices  31.4 us (54%)
  waiting for transfers between devices  20.6 us (35%)
  Pallas kernels  4.68 us (8%)
  local copies, waits for them, and re-layouts  0.86 us (1%)
  between operations  0.74 us (1%)
    ppermute x9, starting transfers between devices, crossed(): return lax.ppermute(value, BOTH, pairs)  13.4 us
    ppermute x10, starting transfers between devices, swapped(): return lax.ppermute(value, BOTH, pairs)  9.21 us
    ppermute x10, waiting for transfers between devices, swapped(): return lax.ppermute(value, BOTH, pairs)  9.19 us
    ppermute x9, waiting for transfers between devices, crossed(): return lax.ppermute(value, BOTH, pairs)  7.34 us
    all_to_all x1, starting transfers between devices, per_device(): lax.all_to_all(parts.reshape(n_block * n_col, tall, order), BOTH, 0, 0, a...  5.11 us
    pallas_call x7, Pallas kernels, call(): pl.pallas_call(kernel, out_shape=out, in_specs=[VMEM] * len(args), out_sp...  4.68 us
    all_to_all x1, waiting for transfers between devices, per_device(): lax.all_to_all(parts.reshape(n_block * n_col, tall, order), BOTH, 0, 0, a...  4.08 us
    all_to_all x1, starting transfers between devices, per_device(): squares = lax.all_to_all(squares, BOTH, 0, 0)  3.62 us
  transfers between devices with their start and end apart: 21, of which 13 were waited for; matrix products, arithmetic and copies ran while one was open for 0% of the time, Pallas kernels for 4%

profile of v3, /device:TPU:0, one launch (start us, length us, event | category | flops | bytes accessed | tf_op | source)
XLA Modules:
  0.0 58.3 jit_solution(6096763377523637129)
XLA Ops:
  0.6 3.0 %collective-permute-start.1 = (bf16[1024,128]{1,0:T(8,128)(2,1)}, bf16[1024,128]{1,0:T(8,128)(2,1)S(1)}, u32[]{:S(2)}, u32[]{:S(2)}) collective-permute-start(bf16[1024,128]{1,0:T(8,128)(2,1)} %bitcast.6), channel_id=1, source_target_pairs={{0,16},{1,17},{2,18},{3,19},{4,20},{5,21},{6,22},{7,23},{8,9},{9,8... | collective-permute-start | bytes 786440 | tf_op jit(solution)/shard_map/ppermute | solution.py:246
  3.7 1.5 %collective-permute-start = (bf16[1024,128]{1,0:T(8,128)(2,1)}, bf16[1024,128]{1,0:T(8,128)(2,1)S(1)}, u32[]{:S(2)}, u32[]{:S(2)}) collective-permute-start(bf16[1024,128]{1,0:T(8,128)(2,1)} %bitcast.7), channel_id=1, source_target_pairs={{0,1},{1,0},{2,3},{3,2},{4,5},{5,4},{6,7},{7,6},{8,24},{9,25},{10,... | collective-permute-start | bytes 786440 | tf_op jit(solution)/shard_map/ppermute | solution.py:246
  5.3 0.8 %copy-done.2 = bf16[128,128]{1,0:T(8,128)(2,1)S(1)} copy-done((bf16[128,128]{1,0:T(8,128)(2,1)S(1)}, bf16[128,128]{1,0:T(8,128)(2,1)}, u32[]{:S(2)}) %copy-start.2) | copy-done | bytes 32792
  6.0 0.8 %shard_map.59 = bf16[2,8,48,128]{3,2,1,0:T(8,128)(2,1)} custom-call(s32[4,2]{1,0:T(4,128)S(1)} %copy.6.columns_ref, bf16[128,128]{1,0:T(8,128)(2,1)S(1)} %copy-done.2), custom_call_target="tpu_custom_call" | custom-call | tf_op jit(solution)/shard_map/pallas_call | solution.py:25
  6.8 5.1 %all-to-all-start = ((bf16[16,48,128]{2,1,0:T(8,128)(2,1)}), bf16[16,48,128]{2,1,0:T(8,128)(2,1)S(1)}, u32[]{:S(2)}, u32[]{:S(2)}) async-start(bf16[16,48,128]{2,1,0:T(8,128)(2,1)} %bitcast.1), calls=%async_computation | async-start | bytes 393216 | tf_op jit(solution)/shard_map/all_to_all | solution.py:297
  12.0 2.0 %collective-permute-start.2 = (bf16[1024,128]{1,0:T(8,128)(2,1)S(1)}, bf16[1024,128]{1,0:T(8,128)(2,1)S(1)}, u32[]{:S(2)}, u32[]{:S(2)}) collective-permute-start(bf16[1024,128]{1,0:T(8,128)(2,1)S(1)} %collective-permute-done.refs_1_.refs_5_), channel_id=1, source_target_pairs={{0,16},{1,17},{2,18},{3,19},{4,20},{5,21},{6,22},{7,23},{8,9},{9,8... | collective-permute-start | bytes 786440 | tf_op jit(solution)/shard_map/ppermute | solution.py:246
  14.1 1.9 %collective-permute-start.3 = (bf16[128,512]{1,0:T(8,128)(2,1)S(1)}, bf16[128,512]{1,0:T(8,128)(2,1)S(1)}, u32[]{:S(2)}, u32[]{:S(2)}) collective-permute-start(bf16[128,512]{1,0:T(8,128)(2,1)S(1)} %copy-done.1), channel_id=1, source_target_pairs={{0,1},{1,0},{2,3},{3,2},{4,5},{5,4},{6,7},{7,6},{8,24},{9,25},{10,... | collective-permute-start | bytes 393224 | tf_op jit(solution)/shard_map/ppermute | solution.py:246
  16.0 4.1 %all-to-all-done = bf16[16,48,128]{2,1,0:T(8,128)(2,1)S(1)} async-done(((bf16[16,48,128]{2,1,0:T(8,128)(2,1)}), bf16[16,48,128]{2,1,0:T(8,128)(2,1)S(1)}, u32[]{:S(2)}, u32[]{:S(2)}) %all-to-all-start) | async-done | bytes 196640 | tf_op jit(solution)/shard_map/all_to_all | solution.py:297
  20.1 0.6 %shard_map.60 = (f32[2,4,32,128]{3,2,1,0:T(8,128)S(1)}, s32[4,128,8]{2,1,0:T(8,128)S(1)}, bf16[2,2,32,128]{3,2,1,0:T(8,128)(2,1)S(1)}) custom-call(bf16[2,8,48,128]{3,2,1,0:T(8,128)(2,1)S(1)} %bitcast.4, bf16[1024,128]{1,0:T(8,128)(2,1)S(1)} %bitcast.8, bf16[1024,128]{1,0:T(8,128)(2,1)S(1)} %collective-permute-done.refs_1_.refs_5_, ...), custom_call_target="tpu_custom_call" | custom-call | tf_op jit(solution)/shard_map/pallas_call | solution.py:25
  20.7 2.1 %collective-permute-done.4.refs_2_ = bf16[128,512]{1,0:T(8,128)(2,1)S(1)} collective-permute-done((bf16[128,512]{1,0:T(8,128)(2,1)S(1)}, bf16[128,512]{1,0:T(8,128)(2,1)S(1)}, u32[]{:S(2)}, u32[]{:S(2)}) %collective-permute-start.4) | collective-permute-done | bytes 131104 | tf_op jit(solution)/shard_map/ppermute | solution.py:246
  23.0 1.3 %collective-permute-start.10 = (bf16[128,512]{1,0:T(8,128)(2,1)S(1)}, bf16[128,512]{1,0:T(8,128)(2,1)S(1)}, u32[]{:S(2)}, u32[]{:S(2)}) collective-permute-start(bf16[128,512]{1,0:T(8,128)(2,1)S(1)} %collective-permute-done.3.refs_1_), channel_id=1, source_target_pairs={{0,16},{1,17},{2,18},{3,19},{4,20},{5,21},{6,22},{7,23},{8,9},{9,8... | collective-permute-start | bytes 393224 | tf_op jit(solution)/shard_map/ppermute | solution.py:246
  24.4 3.1 %collective-permute-start.8 = (bf16[2,2,32,128]{3,2,1,0:T(8,128)(2,1)S(1)}, bf16[2,2,32,128]{3,2,1,0:T(8,128)(2,1)S(1)}, u32[]{:S(2)}, u32[]{:S(2)}) collective-permute-start(bf16[2,2,32,128]{3,2,1,0:T(8,128)(2,1)S(1)} %add_convert_fusion.refs_0_), channel_id=1, source_target_pairs={{0,6},{1,7},{2,4},{3,5},{4,2},{5,3},{6,0},{7,1},{8,14},{9,15},{10,... | collective-permute-start | bytes 98312 | tf_op jit(solution)/shard_map/ppermute | solution.py:258
  27.5 1.4 %collective-permute-start.6 = (bf16[2,2,32,128]{3,2,1,0:T(8,128)(2,1)S(1)}, bf16[2,2,32,128]{3,2,1,0:T(8,128)(2,1)S(1)}, u32[]{:S(2)}, u32[]{:S(2)}) collective-permute-start(bf16[2,2,32,128]{3,2,1,0:T(8,128)(2,1)S(1)} %add_convert_fusion.refs_0_), channel_id=1, source_target_pairs={{0,2},{1,3},{2,0},{3,1},{4,6},{5,7},{6,4},{7,5},{8,10},{9,11},{10,... | collective-permute-start | bytes 98312 | tf_op jit(solution)/shard_map/ppermute | solution.py:258
  28.8 1.4 %collective-permute-done.8.refs_3_ = bf16[2,2,32,128]{3,2,1,0:T(8,128)(2,1)S(1)} collective-permute-done((bf16[2,2,32,128]{3,2,1,0:T(8,128)(2,1)S(1)}, bf16[2,2,32,128]{3,2,1,0:T(8,128)(2,1)S(1)}, u32[]{:S(2)}, u32[]{:S(2)}) %collective-permute-start.8) | collective-permute-done | bytes 32800 | tf_op jit(solution)/shard_map/ppermute | solution.py:258
  30.3 2.0 %collective-permute-done.7.refs_2_ = bf16[2,2,32,128]{3,2,1,0:T(8,128)(2,1)S(1)} collective-permute-done((bf16[2,2,32,128]{3,2,1,0:T(8,128)(2,1)S(1)}, bf16[2,2,32,128]{3,2,1,0:T(8,128)(2,1)S(1)}, u32[]{:S(2)}, u32[]{:S(2)}) %collective-permute-start.7) | collective-permute-done | bytes 32800 | tf_op jit(solution)/shard_map/ppermute | solution.py:258
  32.3 0.7 %shard_map.62 = (f32[2,2,32,128]{3,2,1,0:T(8,128)S(1)}, f32[2,2,32,128]{3,2,1,0:T(8,128)S(1)}) custom-call(s32[4,128,8]{2,1,0:T(8,128)S(1)} %get-tuple-element.30.columns_ref, bf16[2,2,32,128]{3,2,1,0:T(8,128)(2,1)S(1)} %get-tuple-element.31.start_ref, bf16[2,2,32,128]{3,2,1,0:T(8,128)(2,1)S(1)} %add_convert_fusion.refs_0_, ...), custom_call_target="tpu_custom_call" | custom-call | tf_op jit(solution)/shard_map/pallas_call | solution.py:25
  33.1 1.2 %collective-permute-done.9.given_ref = f32[2,2,32,128]{3,2,1,0:T(8,128)S(1)} collective-permute-done((f32[2,2,32,128]{3,2,1,0:T(8,128)S(1)}, f32[2,2,32,128]{3,2,1,0:T(8,128)S(1)}, u32[]{:S(2)}, u32[]{:S(2)}) %collective-permute-start.9) | collective-permute-done | bytes 65568 | tf_op jit(solution)/shard_map/ppermute | solution.py:258
  34.7 1.1 %collective-permute-done.11 = f32[32,256]{1,0:T(8,128)S(1)} collective-permute-done((f32[32,256]{1,0:T(8,128)S(1)}, f32[32,256]{1,0:T(8,128)S(1)}, u32[]{:S(2)}, u32[]{:S(2)}) %collective-permute-start.11) | collective-permute-done | bytes 32800 | tf_op jit(solution)/shard_map/ppermute | solution.py:258
  35.8 1.5 %collective-permute-start.14 = (f32[32,256]{1,0:T(8,128)S(1)}, f32[32,256]{1,0:T(8,128)S(1)}, u32[]{:S(2)}, u32[]{:S(2)}) collective-permute-start(f32[32,256]{1,0:T(8,128)S(1)} %add.16), channel_id=1, source_target_pairs={{0,6},{1,7},{2,4},{3,5},{4,2},{5,3},{6,0},{7,1},{8,14},{9,15},{10,... | collective-permute-start | bytes 98312 | tf_op jit(solution)/shard_map/ppermute | solution.py:258
  37.3 0.6 collective-permute-start.13
  37.9 2.3 %collective-permute-start.12 = (f32[32,256]{1,0:T(8,128)S(1)}, f32[32,256]{1,0:T(8,128)S(1)}, u32[]{:S(2)}, u32[]{:S(2)}) collective-permute-start(f32[32,256]{1,0:T(8,128)S(1)} %add.16), channel_id=1, source_target_pairs={{0,2},{1,3},{2,0},{3,1},{4,6},{5,7},{6,4},{7,5},{8,10},{9,11},{10,... | collective-permute-start | bytes 98312 | tf_op jit(solution)/shard_map/ppermute | solution.py:258
  40.2 1.6 %collective-permute-done.14 = f32[32,256]{1,0:T(8,128)S(1)} collective-permute-done((f32[32,256]{1,0:T(8,128)S(1)}, f32[32,256]{1,0:T(8,128)S(1)}, u32[]{:S(2)}, u32[]{:S(2)}) %collective-permute-start.14) | collective-permute-done | bytes 32800 | tf_op jit(solution)/shard_map/ppermute | solution.py:258
  41.8 0.4 collective-permute-done.13
  42.6 1.2 %collective-permute-done.15.mate_ref = f32[32,256]{1,0:T(8,128)S(1)} collective-permute-done((f32[32,256]{1,0:T(8,128)S(1)}, f32[32,256]{1,0:T(8,128)S(1)}, u32[]{:S(2)}, u32[]{:S(2)}) %collective-permute-start.15) | collective-permute-done | bytes 32800 | tf_op jit(solution)/shard_map/ppermute | solution.py:258
  43.7 1.1 %shard_map.64 = (f32[32,640]{1,0:T(8,128)S(1)}, f32[32,640]{1,0:T(8,128)S(1)}, f32[32,640]{1,0:T(8,128)S(1)}, f32[32,640]{1,0:T(8,128)S(1)}, f32[32,8,128]{2,1,0:T(8,128)}) custom-call(f32[32,256]{1,0:T(8,128)S(1)} %add_add_fusion.mine_ref, f32[32,256]{1,0:T(8,128)S(1)} %collective-permute-done.15.mate_ref, ...), custom_call_target="tpu_custom_call" | custom-call | tf_op jit(solution)/shard_map/pallas_call | solution.py:25
  44.9 3.6 %all-to-all-start.1 = ((f32[32,8,128]{2,1,0:T(8,128)}), f32[32,8,128]{2,1,0:T(8,128)S(1)}, u32[]{:S(2)}, u32[]{:S(2)}) async-start(f32[32,8,128]{2,1,0:T(8,128)} %get-tuple-element.47), calls=%async_computation.1 | async-start | bytes 262144 | tf_op jit(solution)/shard_map/all_to_all | solution.py:368
  48.5 1.8 %collective-permute-start.16 = (f32[32,640]{1,0:T(8,128)S(1)}, f32[32,640]{1,0:T(8,128)S(1)}, u32[]{:S(2)}, u32[]{:S(2)}) collective-permute-start(f32[32,640]{1,0:T(8,128)S(1)} %get-tuple-element.49), channel_id=1, source_target_pairs={{0,1},{1,0},{2,3},{3,2},{4,5},{5,4},{6,7},{7,6},{8,24},{9,25},{10,... | collective-permute-start | bytes 245768 | tf_op jit(solution)/shard_map/ppermute | solution.py:246
  50.4 1.5 %collective-permute-start.17 = (f32[32,640]{1,0:T(8,128)S(1)}, f32[32,640]{1,0:T(8,128)S(1)}, u32[]{:S(2)}, u32[]{:S(2)}) collective-permute-start(f32[32,640]{1,0:T(8,128)S(1)} %get-tuple-element.50), channel_id=1, source_target_pairs={{0,16},{1,17},{2,18},{3,19},{4,20},{5,21},{6,22},{7,23},{8,9},{9,8... | collective-permute-start | bytes 245768 | tf_op jit(solution)/shard_map/ppermute | solution.py:246
  52.1 2.0 %collective-permute-done.16.refs_1_ = f32[32,640]{1,0:T(8,128)S(1)} collective-permute-done((f32[32,640]{1,0:T(8,128)S(1)}, f32[32,640]{1,0:T(8,128)S(1)}, u32[]{:S(2)}, u32[]{:S(2)}) %collective-permute-start.16) | collective-permute-done | bytes 81952 | tf_op jit(solution)/shard_map/ppermute | solution.py:246
  54.0 1.9 %collective-permute-done.17.refs_2_ = f32[32,640]{1,0:T(8,128)S(1)} collective-permute-done((f32[32,640]{1,0:T(8,128)S(1)}, f32[32,640]{1,0:T(8,128)S(1)}, u32[]{:S(2)}, u32[]{:S(2)}) %collective-permute-start.17) | collective-permute-done | bytes 81952 | tf_op jit(solution)/shard_map/ppermute | solution.py:246
  56.0 1.4 %collective-permute-done.18.refs_3_ = f32[32,640]{1,0:T(8,128)S(1)} collective-permute-done((f32[32,640]{1,0:T(8,128)S(1)}, f32[32,640]{1,0:T(8,128)S(1)}, u32[]{:S(2)}, u32[]{:S(2)}) %collective-permute-start.18) | collective-permute-done | bytes 81952 | tf_op jit(solution)/shard_map/ppermute | solution.py:246
  57.4 0.9 %shard_map.65 = (f32[128,128]{1,0:T(8,128)}, f32[512,128]{1,0:T(8,128)}) custom-call(f32[32,8,128]{2,1,0:T(8,128)S(1)} %all-to-all-done.1.squares_ref, f32[32,640]{1,0:T(8,128)S(1)} %get-tuple-element.48.refs_0_, f32[32,640]{1,0:T(8,128)S(1)} %collective-permute-done.16.refs_1_, f32[32,640]{1,0:T(8,128)S(1)} %collective-permute-done.17.refs_2_, ...), custom_call_target="tpu_custom_call" | custom-call | tf_op jit(solution)/shard_map/pallas_call | solution.py:25
  (29 shorter events, 1.6 us)
Async XLA Ops:
  0.6 4.5 %copy-start.3 = (s32[1,4,1,2]{1,3,2,0:T(2,128)S(1)}, s32[1,4,1,2]{1,3,2,0:T(2,128)}, u32[]{:S(2)}) copy-start(s32[1,4,1,2]{1,3,2,0:T(2,128)} %param.6) | copy-start | bytes 100
  0.6 11.3 %collective-permute-start.1 = (bf16[1024,128]{1,0:T(8,128)(2,1)}, bf16[1024,128]{1,0:T(8,128)(2,1)S(1)}, u32[]{:S(2)}, u32[]{:S(2)}) collective-permute-start(bf16[1024,128]{1,0:T(8,128)(2,1)} %bitcast.6), channel_id=1, source_target_pairs={{0,16},{1,17},{2,18},{3,19},{4,20},{5,21},{6,22},{7,23},{8,9},{9,8... | collective-permute-start | bytes 786440 | tf_op jit(solution)/shard_map/ppermute | solution.py:246
  3.7 8.3 %collective-permute-start = (bf16[1024,128]{1,0:T(8,128)(2,1)}, bf16[1024,128]{1,0:T(8,128)(2,1)S(1)}, u32[]{:S(2)}, u32[]{:S(2)}) collective-permute-start(bf16[1024,128]{1,0:T(8,128)(2,1)} %bitcast.7), channel_id=1, source_target_pairs={{0,1},{1,0},{2,3},{3,2},{4,5},{5,4},{6,7},{7,6},{8,24},{9,25},{10,... | collective-permute-start | bytes 786440 | tf_op jit(solution)/shard_map/ppermute | solution.py:246
  5.3 0.8 %copy-start.2 = (bf16[128,128]{1,0:T(8,128)(2,1)S(1)}, bf16[128,128]{1,0:T(8,128)(2,1)}, u32[]{:S(2)}) copy-start(bf16[128,128]{1,0:T(8,128)(2,1)} %start_ref.1) | copy-start | bytes 98308
  6.0 14.0 %copy-start = (bf16[1,4,1,2,128,128]{5,4,3,2,1,0:T(8,128)(2,1)S(1)}, bf16[1,4,1,2,128,128]{5,4,3,2,1,0:T(8,128)(2,1)}, u32[]{:S(2)}) copy-start(bf16[1,4,1,2,128,128]{5,4,3,2,1,0:T(8,128)(2,1)} %param.5) | copy-start | bytes 786436
  6.8 7.1 %copy-start.1 = (bf16[128,512]{1,0:T(8,128)(2,1)S(1)}, bf16[128,512]{1,0:T(8,128)(2,1)}, u32[]{:S(2)}) copy-start(bf16[128,512]{1,0:T(8,128)(2,1)} %refs_0_.1) | copy-start | bytes 393220
  6.8 13.2 %all-to-all-start = ((bf16[16,48,128]{2,1,0:T(8,128)(2,1)}), bf16[16,48,128]{2,1,0:T(8,128)(2,1)S(1)}, u32[]{:S(2)}, u32[]{:S(2)}) async-start(bf16[16,48,128]{2,1,0:T(8,128)(2,1)} %bitcast.1), calls=%async_computation | async-start | bytes 393216 | tf_op jit(solution)/shard_map/all_to_all | solution.py:297
  12.0 10.8 %collective-permute-start.2 = (bf16[1024,128]{1,0:T(8,128)(2,1)S(1)}, bf16[1024,128]{1,0:T(8,128)(2,1)S(1)}, u32[]{:S(2)}, u32[]{:S(2)}) collective-permute-start(bf16[1024,128]{1,0:T(8,128)(2,1)S(1)} %collective-permute-done.refs_1_.refs_5_), channel_id=1, source_target_pairs={{0,16},{1,17},{2,18},{3,19},{4,20},{5,21},{6,22},{7,23},{8,9},{9,8... | collective-permute-start | bytes 786440 | tf_op jit(solution)/shard_map/ppermute | solution.py:246
  14.0 8.8 %collective-permute-start.4 = (bf16[128,512]{1,0:T(8,128)(2,1)S(1)}, bf16[128,512]{1,0:T(8,128)(2,1)S(1)}, u32[]{:S(2)}, u32[]{:S(2)}) collective-permute-start(bf16[128,512]{1,0:T(8,128)(2,1)S(1)} %copy-done.1), channel_id=1, source_target_pairs={{0,16},{1,17},{2,18},{3,19},{4,20},{5,21},{6,22},{7,23},{8,9},{9,8... | collective-permute-start | bytes 393224 | tf_op jit(solution)/shard_map/ppermute | solution.py:246
  14.1 8.7 %collective-permute-start.3 = (bf16[128,512]{1,0:T(8,128)(2,1)S(1)}, bf16[128,512]{1,0:T(8,128)(2,1)S(1)}, u32[]{:S(2)}, u32[]{:S(2)}) collective-permute-start(bf16[128,512]{1,0:T(8,128)(2,1)S(1)} %copy-done.1), channel_id=1, source_target_pairs={{0,1},{1,0},{2,3},{3,2},{4,5},{5,4},{6,7},{7,6},{8,24},{9,25},{10,... | collective-permute-start | bytes 393224 | tf_op jit(solution)/shard_map/ppermute | solution.py:246
  23.0 1.4 %collective-permute-start.5 = (f32[2,2,32,128]{3,2,1,0:T(8,128)S(1)}, f32[2,2,32,128]{3,2,1,0:T(8,128)S(1)}, u32[]{:S(2)}, u32[]{:S(2)}) collective-permute-start(f32[2,2,32,128]{3,2,1,0:T(8,128)S(1)} %get-tuple-element.38), channel_id=1, source_target_pairs={{0,8},{1,9},{2,10},{3,11},{4,12},{5,13},{6,14},{7,15},{8,0},{9,1},... | collective-permute-start | bytes 196616 | tf_op jit(solution)/shard_map/ppermute | solution.py:258
  23.0 10.0 %collective-permute-start.10 = (bf16[128,512]{1,0:T(8,128)(2,1)S(1)}, bf16[128,512]{1,0:T(8,128)(2,1)S(1)}, u32[]{:S(2)}, u32[]{:S(2)}) collective-permute-start(bf16[128,512]{1,0:T(8,128)(2,1)S(1)} %collective-permute-done.3.refs_1_), channel_id=1, source_target_pairs={{0,16},{1,17},{2,18},{3,19},{4,20},{5,21},{6,22},{7,23},{8,9},{9,8... | collective-permute-start | bytes 393224 | tf_op jit(solution)/shard_map/ppermute | solution.py:246
  24.4 5.9 %collective-permute-start.8 = (bf16[2,2,32,128]{3,2,1,0:T(8,128)(2,1)S(1)}, bf16[2,2,32,128]{3,2,1,0:T(8,128)(2,1)S(1)}, u32[]{:S(2)}, u32[]{:S(2)}) collective-permute-start(bf16[2,2,32,128]{3,2,1,0:T(8,128)(2,1)S(1)} %add_convert_fusion.refs_0_), channel_id=1, source_target_pairs={{0,6},{1,7},{2,4},{3,5},{4,2},{5,3},{6,0},{7,1},{8,14},{9,15},{10,... | collective-permute-start | bytes 98312 | tf_op jit(solution)/shard_map/ppermute | solution.py:258
  27.5 4.8 %collective-permute-start.7 = (bf16[2,2,32,128]{3,2,1,0:T(8,128)(2,1)S(1)}, bf16[2,2,32,128]{3,2,1,0:T(8,128)(2,1)S(1)}, u32[]{:S(2)}, u32[]{:S(2)}) collective-permute-start(bf16[2,2,32,128]{3,2,1,0:T(8,128)(2,1)S(1)} %add_convert_fusion.refs_0_), channel_id=1, source_target_pairs={{0,4},{1,5},{2,6},{3,7},{4,0},{5,1},{6,2},{7,3},{8,12},{9,13},{10,... | collective-permute-start | bytes 98312 | tf_op jit(solution)/shard_map/ppermute | solution.py:258
  27.5 4.8 %collective-permute-start.6 = (bf16[2,2,32,128]{3,2,1,0:T(8,128)(2,1)S(1)}, bf16[2,2,32,128]{3,2,1,0:T(8,128)(2,1)S(1)}, u32[]{:S(2)}, u32[]{:S(2)}) collective-permute-start(bf16[2,2,32,128]{3,2,1,0:T(8,128)(2,1)S(1)} %add_convert_fusion.refs_0_), channel_id=1, source_target_pairs={{0,2},{1,3},{2,0},{3,1},{4,6},{5,7},{6,4},{7,5},{8,10},{9,11},{10,... | collective-permute-start | bytes 98312 | tf_op jit(solution)/shard_map/ppermute | solution.py:258
  33.0 1.3 %collective-permute-start.9 = (f32[2,2,32,128]{3,2,1,0:T(8,128)S(1)}, f32[2,2,32,128]{3,2,1,0:T(8,128)S(1)}, u32[]{:S(2)}, u32[]{:S(2)}) collective-permute-start(f32[2,2,32,128]{3,2,1,0:T(8,128)S(1)} %get-tuple-element.40), channel_id=1, source_target_pairs={{0,8},{1,9},{2,10},{3,11},{4,12},{5,13},{6,14},{7,15},{8,0},{9,1},... | collective-permute-start | bytes 196616 | tf_op jit(solution)/shard_map/ppermute | solution.py:258
  34.5 1.2 %collective-permute-start.11 = (f32[32,256]{1,0:T(8,128)S(1)}, f32[32,256]{1,0:T(8,128)S(1)}, u32[]{:S(2)}, u32[]{:S(2)}) collective-permute-start(f32[32,256]{1,0:T(8,128)S(1)} %get-tuple-element.45), channel_id=1, source_target_pairs={{0,8},{1,9},{2,10},{3,11},{4,12},{5,13},{6,14},{7,15},{8,0},{9,1},... | collective-permute-start | bytes 98312 | tf_op jit(solution)/shard_map/ppermute | solution.py:258
  35.8 6.0 %collective-permute-start.14 = (f32[32,256]{1,0:T(8,128)S(1)}, f32[32,256]{1,0:T(8,128)S(1)}, u32[]{:S(2)}, u32[]{:S(2)}) collective-permute-start(f32[32,256]{1,0:T(8,128)S(1)} %add.16), channel_id=1, source_target_pairs={{0,6},{1,7},{2,4},{3,5},{4,2},{5,3},{6,0},{7,1},{8,14},{9,15},{10,... | collective-permute-start | bytes 98312 | tf_op jit(solution)/shard_map/ppermute | solution.py:258
  37.3 4.9 %collective-permute-start.13 = (f32[32,256]{1,0:T(8,128)S(1)}, f32[32,256]{1,0:T(8,128)S(1)}, u32[]{:S(2)}, u32[]{:S(2)}) collective-permute-start(f32[32,256]{1,0:T(8,128)S(1)} %add.16), channel_id=1, source_target_pairs={{0,4},{1,5},{2,6},{3,7},{4,0},{5,1},{6,2},{7,3},{8,12},{9,13},{10,... | collective-permute-start | bytes 98312 | tf_op jit(solution)/shard_map/ppermute | solution.py:258
  37.9 4.6 %collective-permute-start.12 = (f32[32,256]{1,0:T(8,128)S(1)}, f32[32,256]{1,0:T(8,128)S(1)}, u32[]{:S(2)}, u32[]{:S(2)}) collective-permute-start(f32[32,256]{1,0:T(8,128)S(1)} %add.16), channel_id=1, source_target_pairs={{0,2},{1,3},{2,0},{3,1},{4,6},{5,7},{6,4},{7,5},{8,10},{9,11},{10,... | collective-permute-start | bytes 98312 | tf_op jit(solution)/shard_map/ppermute | solution.py:258
  42.5 1.3 %collective-permute-start.15 = (f32[32,256]{1,0:T(8,128)S(1)}, f32[32,256]{1,0:T(8,128)S(1)}, u32[]{:S(2)}, u32[]{:S(2)}) collective-permute-start(f32[32,256]{1,0:T(8,128)S(1)} %add_add_fusion.mine_ref), channel_id=1, source_target_pairs={{0,8},{1,9},{2,10},{3,11},{4,12},{5,13},{6,14},{7,15},{8,0},{9,1},... | collective-permute-start | bytes 98312 | tf_op jit(solution)/shard_map/ppermute | solution.py:258
  44.9 12.5 %all-to-all-start.1 = ((f32[32,8,128]{2,1,0:T(8,128)}), f32[32,8,128]{2,1,0:T(8,128)S(1)}, u32[]{:S(2)}, u32[]{:S(2)}) async-start(f32[32,8,128]{2,1,0:T(8,128)} %get-tuple-element.47), calls=%async_computation.1 | async-start | bytes 262144 | tf_op jit(solution)/shard_map/all_to_all | solution.py:368
  48.5 5.5 %collective-permute-start.16 = (f32[32,640]{1,0:T(8,128)S(1)}, f32[32,640]{1,0:T(8,128)S(1)}, u32[]{:S(2)}, u32[]{:S(2)}) collective-permute-start(f32[32,640]{1,0:T(8,128)S(1)} %get-tuple-element.49), channel_id=1, source_target_pairs={{0,1},{1,0},{2,3},{3,2},{4,5},{5,4},{6,7},{7,6},{8,24},{9,25},{10,... | collective-permute-start | bytes 245768 | tf_op jit(solution)/shard_map/ppermute | solution.py:246
  50.4 5.6 %collective-permute-start.17 = (f32[32,640]{1,0:T(8,128)S(1)}, f32[32,640]{1,0:T(8,128)S(1)}, u32[]{:S(2)}, u32[]{:S(2)}) collective-permute-start(f32[32,640]{1,0:T(8,128)S(1)} %get-tuple-element.50), channel_id=1, source_target_pairs={{0,16},{1,17},{2,18},{3,19},{4,20},{5,21},{6,22},{7,23},{8,9},{9,8... | collective-permute-start | bytes 245768 | tf_op jit(solution)/shard_map/ppermute | solution.py:246
  51.8 5.5 %collective-permute-start.18 = (f32[32,640]{1,0:T(8,128)S(1)}, f32[32,640]{1,0:T(8,128)S(1)}, u32[]{:S(2)}, u32[]{:S(2)}) collective-permute-start(f32[32,640]{1,0:T(8,128)S(1)} %get-tuple-element.51), channel_id=1, source_target_pairs={{0,17},{1,16},{2,19},{3,18},{4,21},{5,20},{6,23},{7,22},{8,25},{9,... | collective-permute-start | bytes 245768 | tf_op jit(solution)/shard_map/ppermute | solution.py:246

commit v4 on v3

--- a/solution.py
+++ b/solution.py
@@ -213,7 +213,7 @@
     width = slabs[0].shape[0]
     stored = out_ref.shape[0]
     block, core, _, me_lane = position(lanes)
-    for slab, entry in zip(slabs, near):
+    for slab, entry in zip(slabs, near[::-1]):
         q, u = place(entry, core)
         start = ((block ^ q) * lanes + (me_lane ^ u)) * width
         whole_ref[pl.ds(pl.multiple_of(start, width), width), :] = slab[...]
@@ -313,8 +313,6 @@
         ],
         (parts, *tiles[:early]),
     )
-    if plane:
-        tiles[early], *own = lax.optimization_barrier((tiles[early], *own))
     keep, give = call(
         functools.partial(rest, near, early, slots),
         [jax.ShapeDtypeStruct(piece, F32)] * 2,
@@ -322,7 +320,6 @@
         [sums],
     )
     if plane:
-        keep, own[1] = lax.optimization_barrier((keep, own[1]))
         own.append(crossed(own[1], near[2]))
     own = spread(own, near)
     mine = (keep + mate(give)).astype(BF16)
@@ -357,7 +354,7 @@
             step *= 2
     slab = jax.ShapeDtypeStruct((width, stored + order), F32)
     copies = 1
-    while nbytes(slab) > n_row * n_col * copies * n_vectors * 4:
+    while nbytes(slab) > 2 * n_row * n_col * copies * n_vectors * 4:
         copies *= 2
     *slabs, squares = call(
         functools.partial(clean, near),
@@ -372,7 +369,7 @@
             jax.ShapeDtypeStruct((order, n_vectors), F32),
             jax.ShapeDtypeStruct((stored, n_vectors), F32),
         ),
-        (squares, *slabs),
+        (squares, *slabs[::-1]),
         [((n_vectors, stored + order), F32)],
     )
 

time: 58.6 us -> 56.7 us (0.968)
  starting transfers between devices: 31.4 us -> 29.6 us
    ppermute x9, waiting for transfers between devices: 7.34 us -> 4.97 us  [crossed(): return lax.ppermute(value, BOTH, pairs)]
    ppermute x10, waiting for transfers between devices: 9.19 us -> 10.9 us  [swapped(): return lax.ppermute(value, BOTH, pairs)]
    all_to_all x1, starting transfers between devices: 3.62 us -> 2.57 us  [per_device(): squares = lax.all_to_all(squares, BOTH, 0, 0)]
    ppermute x10, starting transfers between devices: 9.21 us -> 8.3 us  [swapped(): return lax.ppermute(value, BOTH, pairs)]
  transfers between devices with their start and end apart: 21 -> 21, of which waited for: 13 -> 11; matrix products, arithmetic and copies ran while one was open for 0% -> 0% of each run, Pallas kernels for 4% -> 4%
where the time goes in v4:
time: 56.7 us; the launch traced here: 56.4 us
  starting transfers between devices  29.6 us (52%)
  waiting for transfers between devices  20.5 us (36%)
  Pallas kernels  4.65 us (8%)
  local copies, waits for them, and re-layouts  0.86 us (2%)
  between operations  0.75 us (1%)
    ppermute x9, starting transfers between devices, crossed(): return lax.ppermute(value, BOTH, pairs)  13.6 us
    ppermute x10, waiting for transfers between devices, swapped(): return lax.ppermute(value, BOTH, pairs)  10.9 us
    ppermute x10, starting transfers between devices, swapped(): return lax.ppermute(value, BOTH, pairs)  8.3 us
    all_to_all x1, starting transfers between devices, per_device(): lax.all_to_all(parts.reshape(n_block * n_col, tall, order), BOTH, 0, 0, a...  5.11 us
    ppermute x9, waiting for transfers between devices, crossed(): return lax.ppermute(value, BOTH, pairs)  4.97 us
    pallas_call x7, Pallas kernels, call(): pl.pallas_call(kernel, out_shape=out, in_specs=[VMEM] * len(args), out_sp...  4.65 us
    all_to_all x1, waiting for transfers between devices, per_device(): lax.all_to_all(parts.reshape(n_block * n_col, tall, order), BOTH, 0, 0, a...  4.64 us
    all_to_all x1, starting transfers between devices, per_device(): squares = lax.all_to_all(squares, BOTH, 0, 0)  2.57 us
  transfers between devices with their start and end apart: 21, of which 11 were waited for; matrix products, arithmetic and copies ran while one was open for 0% of the time, Pallas kernels for 4%

profile of v4, /device:TPU:0, one launch (start us, length us, event | category | flops | bytes accessed | tf_op | source)
XLA Modules:
  0.0 56.4 jit_solution(8412542057060114573)
XLA Ops:
  0.6 3.0 %collective-permute-start = (bf16[1024,128]{1,0:T(8,128)(2,1)}, bf16[1024,128]{1,0:T(8,128)(2,1)S(1)}, u32[]{:S(2)}, u32[]{:S(2)}) collective-permute-start(bf16[1024,128]{1,0:T(8,128)(2,1)} %bitcast.6), channel_id=1, source_target_pairs={{0,1},{1,0},{2,3},{3,2},{4,5},{5,4},{6,7},{7,6},{8,24},{9,25},{10,... | collective-permute-start | bytes 786440 | tf_op jit(solution)/shard_map/ppermute | solution.py:246
  3.6 1.5 %collective-permute-start.1 = (bf16[1024,128]{1,0:T(8,128)(2,1)}, bf16[1024,128]{1,0:T(8,128)(2,1)S(1)}, u32[]{:S(2)}, u32[]{:S(2)}) collective-permute-start(bf16[1024,128]{1,0:T(8,128)(2,1)} %bitcast.7), channel_id=1, source_target_pairs={{0,16},{1,17},{2,18},{3,19},{4,20},{5,21},{6,22},{7,23},{8,9},{9,8... | collective-permute-start | bytes 786440 | tf_op jit(solution)/shard_map/ppermute | solution.py:246
  5.3 0.8 %copy-done.2 = bf16[128,128]{1,0:T(8,128)(2,1)S(1)} copy-done((bf16[128,128]{1,0:T(8,128)(2,1)S(1)}, bf16[128,128]{1,0:T(8,128)(2,1)}, u32[]{:S(2)}) %copy-start.2) | copy-done | bytes 32792
  6.0 0.8 %shard_map.59 = bf16[2,8,48,128]{3,2,1,0:T(8,128)(2,1)} custom-call(s32[4,2]{1,0:T(4,128)S(1)} %copy.6.columns_ref, bf16[128,128]{1,0:T(8,128)(2,1)S(1)} %copy-done.2), custom_call_target="tpu_custom_call" | custom-call | tf_op jit(solution)/shard_map/pallas_call | solution.py:25
  6.8 5.1 %all-to-all-start = ((bf16[16,48,128]{2,1,0:T(8,128)(2,1)}), bf16[16,48,128]{2,1,0:T(8,128)(2,1)S(1)}, u32[]{:S(2)}, u32[]{:S(2)}) async-start(bf16[16,48,128]{2,1,0:T(8,128)(2,1)} %bitcast.1), calls=%async_computation | async-start | bytes 393216 | tf_op jit(solution)/shard_map/all_to_all | solution.py:297
  12.0 2.0 %collective-permute-start.2 = (bf16[1024,128]{1,0:T(8,128)(2,1)S(1)}, bf16[1024,128]{1,0:T(8,128)(2,1)S(1)}, u32[]{:S(2)}, u32[]{:S(2)}) collective-permute-start(bf16[1024,128]{1,0:T(8,128)(2,1)S(1)} %collective-permute-done.refs_1_.refs_5_), channel_id=1, source_target_pairs={{0,16},{1,17},{2,18},{3,19},{4,20},{5,21},{6,22},{7,23},{8,9},{9,8... | collective-permute-start | bytes 786440 | tf_op jit(solution)/shard_map/ppermute | solution.py:246
  14.0 1.5 %collective-permute-start.8 = (bf16[128,512]{1,0:T(8,128)(2,1)S(1)}, bf16[128,512]{1,0:T(8,128)(2,1)S(1)}, u32[]{:S(2)}, u32[]{:S(2)}) collective-permute-start(bf16[128,512]{1,0:T(8,128)(2,1)S(1)} %copy-done.1), channel_id=1, source_target_pairs={{0,1},{1,0},{2,3},{3,2},{4,5},{5,4},{6,7},{7,6},{8,24},{9,25},{10,... | collective-permute-start | bytes 393224 | tf_op jit(solution)/shard_map/ppermute | solution.py:246
  15.4 4.6 %all-to-all-done = bf16[16,48,128]{2,1,0:T(8,128)(2,1)S(1)} async-done(((bf16[16,48,128]{2,1,0:T(8,128)(2,1)}), bf16[16,48,128]{2,1,0:T(8,128)(2,1)S(1)}, u32[]{:S(2)}, u32[]{:S(2)}) %all-to-all-start) | async-done | bytes 196640 | tf_op jit(solution)/shard_map/all_to_all | solution.py:297
  20.1 0.6 %shard_map.60 = (f32[2,4,32,128]{3,2,1,0:T(8,128)S(1)}, s32[4,128,8]{2,1,0:T(8,128)S(1)}, bf16[2,2,32,128]{3,2,1,0:T(8,128)(2,1)S(1)}) custom-call(bf16[2,8,48,128]{3,2,1,0:T(8,128)(2,1)S(1)} %bitcast.4, bf16[1024,128]{1,0:T(8,128)(2,1)S(1)} %bitcast.8, bf16[1024,128]{1,0:T(8,128)(2,1)S(1)} %collective-permute-done.refs_1_.refs_5_, ...), custom_call_target="tpu_custom_call" | custom-call | tf_op jit(solution)/shard_map/pallas_call | solution.py:25
  20.7 0.6 %collective-permute-done.2.refs_0_.refs_7_ = bf16[1024,128]{1,0:T(8,128)(2,1)S(1)} collective-permute-done((bf16[1024,128]{1,0:T(8,128)(2,1)S(1)}, bf16[1024,128]{1,0:T(8,128)(2,1)S(1)}, u32[]{:S(2)}, u32[]{:S(2)}) %collective-permute-start.2) | collective-permute-done | bytes 262176 | tf_op jit(solution)/shard_map/ppermute | solution.py:246
  21.6 0.8 %collective-permute-start.9 = (bf16[128,512]{1,0:T(8,128)(2,1)S(1)}, bf16[128,512]{1,0:T(8,128)(2,1)S(1)}, u32[]{:S(2)}, u32[]{:S(2)}) collective-permute-start(bf16[128,512]{1,0:T(8,128)(2,1)S(1)} %copy-done.1), channel_id=1, source_target_pairs={{0,16},{1,17},{2,18},{3,19},{4,20},{5,21},{6,22},{7,23},{8,9},{9,8... | collective-permute-start | bytes 393224 | tf_op jit(solution)/shard_map/ppermute | solution.py:246
  22.4 1.2 %collective-permute-start.10 = (bf16[128,512]{1,0:T(8,128)(2,1)S(1)}, bf16[128,512]{1,0:T(8,128)(2,1)S(1)}, u32[]{:S(2)}, u32[]{:S(2)}) collective-permute-start(bf16[128,512]{1,0:T(8,128)(2,1)S(1)} %collective-permute-done.8.refs_1_), channel_id=1, source_target_pairs={{0,16},{1,17},{2,18},{3,19},{4,20},{5,21},{6,22},{7,23},{8,9},{9,8... | collective-permute-start | bytes 393224 | tf_op jit(solution)/shard_map/ppermute | solution.py:246
  23.7 1.5 %collective-permute-start.4 = (bf16[2,2,32,128]{3,2,1,0:T(8,128)(2,1)S(1)}, bf16[2,2,32,128]{3,2,1,0:T(8,128)(2,1)S(1)}, u32[]{:S(2)}, u32[]{:S(2)}) collective-permute-start(bf16[2,2,32,128]{3,2,1,0:T(8,128)(2,1)S(1)} %add_convert_fusion.refs_0_), channel_id=1, source_target_pairs={{0,2},{1,3},{2,0},{3,1},{4,6},{5,7},{6,4},{7,5},{8,10},{9,11},{10,... | collective-permute-start | bytes 98312 | tf_op jit(solution)/shard_map/ppermute | solution.py:258
  25.2 2.2 %collective-permute-start.5 = (bf16[2,2,32,128]{3,2,1,0:T(8,128)(2,1)S(1)}, bf16[2,2,32,128]{3,2,1,0:T(8,128)(2,1)S(1)}, u32[]{:S(2)}, u32[]{:S(2)}) collective-permute-start(bf16[2,2,32,128]{3,2,1,0:T(8,128)(2,1)S(1)} %add_convert_fusion.refs_0_), channel_id=1, source_target_pairs={{0,4},{1,5},{2,6},{3,7},{4,0},{5,1},{6,2},{7,3},{8,12},{9,13},{10,... | collective-permute-start | bytes 98312 | tf_op jit(solution)/shard_map/ppermute | solution.py:258
  27.4 0.7 %collective-permute-start.6 = (bf16[2,2,32,128]{3,2,1,0:T(8,128)(2,1)S(1)}, bf16[2,2,32,128]{3,2,1,0:T(8,128)(2,1)S(1)}, u32[]{:S(2)}, u32[]{:S(2)}) collective-permute-start(bf16[2,2,32,128]{3,2,1,0:T(8,128)(2,1)S(1)} %add_convert_fusion.refs_0_), channel_id=1, source_target_pairs={{0,6},{1,7},{2,4},{3,5},{4,2},{5,3},{6,0},{7,1},{8,14},{9,15},{10,... | collective-permute-start | bytes 98312 | tf_op jit(solution)/shard_map/ppermute | solution.py:258
  28.1 2.4 %collective-permute-done.5.refs_2_ = bf16[2,2,32,128]{3,2,1,0:T(8,128)(2,1)S(1)} collective-permute-done((bf16[2,2,32,128]{3,2,1,0:T(8,128)(2,1)S(1)}, bf16[2,2,32,128]{3,2,1,0:T(8,128)(2,1)S(1)}, u32[]{:S(2)}, u32[]{:S(2)}) %collective-permute-start.5) | collective-permute-done | bytes 32800 | tf_op jit(solution)/shard_map/ppermute | solution.py:258
  30.5 2.7 %collective-permute-done.6.refs_3_ = bf16[2,2,32,128]{3,2,1,0:T(8,128)(2,1)S(1)} collective-permute-done((bf16[2,2,32,128]{3,2,1,0:T(8,128)(2,1)S(1)}, bf16[2,2,32,128]{3,2,1,0:T(8,128)(2,1)S(1)}, u32[]{:S(2)}, u32[]{:S(2)}) %collective-permute-start.6) | collective-permute-done | bytes 32800 | tf_op jit(solution)/shard_map/ppermute | solution.py:258
  33.2 0.7 %shard_map.62 = (f32[2,2,32,128]{3,2,1,0:T(8,128)S(1)}, f32[2,2,32,128]{3,2,1,0:T(8,128)S(1)}) custom-call(s32[4,128,8]{2,1,0:T(8,128)S(1)} %get-tuple-element.24.columns_ref, bf16[2,2,32,128]{3,2,1,0:T(8,128)(2,1)S(1)} %get-tuple-element.25.start_ref, bf16[2,2,32,128]{3,2,1,0:T(8,128)(2,1)S(1)} %add_convert_fusion.refs_0_, ...), custom_call_target="tpu_custom_call" | custom-call | tf_op jit(solution)/shard_map/pallas_call | solution.py:25
  34.0 1.2 %collective-permute-done.7.given_ref = f32[2,2,32,128]{3,2,1,0:T(8,128)S(1)} collective-permute-done((f32[2,2,32,128]{3,2,1,0:T(8,128)S(1)}, f32[2,2,32,128]{3,2,1,0:T(8,128)S(1)}, u32[]{:S(2)}, u32[]{:S(2)}) %collective-permute-start.7) | collective-permute-done | bytes 65568 | tf_op jit(solution)/shard_map/ppermute | solution.py:258
  35.6 1.1 %collective-permute-done.11 = f32[32,256]{1,0:T(8,128)S(1)} collective-permute-done((f32[32,256]{1,0:T(8,128)S(1)}, f32[32,256]{1,0:T(8,128)S(1)}, u32[]{:S(2)}, u32[]{:S(2)}) %collective-permute-start.11) | collective-permute-done | bytes 32800 | tf_op jit(solution)/shard_map/ppermute | solution.py:258
  36.7 1.6 %collective-permute-start.14 = (f32[32,256]{1,0:T(8,128)S(1)}, f32[32,256]{1,0:T(8,128)S(1)}, u32[]{:S(2)}, u32[]{:S(2)}) collective-permute-start(f32[32,256]{1,0:T(8,128)S(1)} %add.16), channel_id=1, source_target_pairs={{0,6},{1,7},{2,4},{3,5},{4,2},{5,3},{6,0},{7,1},{8,14},{9,15},{10,... | collective-permute-start | bytes 98312 | tf_op jit(solution)/shard_map/ppermute | solution.py:258
  38.2 1.9 %collective-permute-start.12 = (f32[32,256]{1,0:T(8,128)S(1)}, f32[32,256]{1,0:T(8,128)S(1)}, u32[]{:S(2)}, u32[]{:S(2)}) collective-permute-start(f32[32,256]{1,0:T(8,128)S(1)} %add.16), channel_id=1, source_target_pairs={{0,2},{1,3},{2,0},{3,1},{4,6},{5,7},{6,4},{7,5},{8,10},{9,11},{10,... | collective-permute-start | bytes 98312 | tf_op jit(solution)/shard_map/ppermute | solution.py:258
  40.2 1.7 %collective-permute-done.13 = f32[32,256]{1,0:T(8,128)S(1)} collective-permute-done((f32[32,256]{1,0:T(8,128)S(1)}, f32[32,256]{1,0:T(8,128)S(1)}, u32[]{:S(2)}, u32[]{:S(2)}) %collective-permute-start.13) | collective-permute-done | bytes 32800 | tf_op jit(solution)/shard_map/ppermute | solution.py:258
  41.8 0.7 %collective-permute-done.14 = f32[32,256]{1,0:T(8,128)S(1)} collective-permute-done((f32[32,256]{1,0:T(8,128)S(1)}, f32[32,256]{1,0:T(8,128)S(1)}, u32[]{:S(2)}, u32[]{:S(2)}) %collective-permute-start.14) | collective-permute-done | bytes 32800 | tf_op jit(solution)/shard_map/ppermute | solution.py:258
  42.6 1.2 %collective-permute-done.15.mate_ref = f32[32,256]{1,0:T(8,128)S(1)} collective-permute-done((f32[32,256]{1,0:T(8,128)S(1)}, f32[32,256]{1,0:T(8,128)S(1)}, u32[]{:S(2)}, u32[]{:S(2)}) %collective-permute-start.15) | collective-permute-done | bytes 32800 | tf_op jit(solution)/shard_map/ppermute | solution.py:258
  43.8 1.1 %shard_map.64 = (f32[32,640]{1,0:T(8,128)S(1)}, f32[32,640]{1,0:T(8,128)S(1)}, f32[32,640]{1,0:T(8,128)S(1)}, f32[32,640]{1,0:T(8,128)S(1)}, f32[32,4,128]{2,1,0:T(4,128)}) custom-call(f32[32,256]{1,0:T(8,128)S(1)} %add_add_fusion.mine_ref, f32[32,256]{1,0:T(8,128)S(1)} %collective-permute-done.15.mate_ref, ...), custom_call_target="tpu_custom_call" | custom-call | tf_op jit(solution)/shard_map/pallas_call | solution.py:25
  44.9 2.6 %all-to-all-start.1 = ((f32[32,4,128]{2,1,0:T(4,128)}), f32[32,4,128]{2,1,0:T(4,128)S(1)}, u32[]{:S(2)}, u32[]{:S(2)}) async-start(f32[32,4,128]{2,1,0:T(4,128)} %get-tuple-element.35), calls=%async_computation.1 | async-start | bytes 131072 | tf_op jit(solution)/shard_map/all_to_all | solution.py:365
  47.5 2.6 %collective-permute-start.16 = (f32[32,640]{1,0:T(8,128)S(1)}, f32[32,640]{1,0:T(8,128)S(1)}, u32[]{:S(2)}, u32[]{:S(2)}) collective-permute-start(f32[32,640]{1,0:T(8,128)S(1)} %get-tuple-element.36), channel_id=1, source_target_pairs={{0,17},{1,16},{2,19},{3,18},{4,21},{5,20},{6,23},{7,22},{8,25},{9,... | collective-permute-start | bytes 245768 | tf_op jit(solution)/shard_map/ppermute | solution.py:246
  50.2 0.6 collective-permute-start.17
  51.1 3.0 %collective-permute-done.16.refs_0_ = f32[32,640]{1,0:T(8,128)S(1)} collective-permute-done((f32[32,640]{1,0:T(8,128)S(1)}, f32[32,640]{1,0:T(8,128)S(1)}, u32[]{:S(2)}, u32[]{:S(2)}) %collective-permute-start.16) | collective-permute-done | bytes 81952 | tf_op jit(solution)/shard_map/ppermute | solution.py:246
  54.1 1.4 %collective-permute-done.17.refs_1_ = f32[32,640]{1,0:T(8,128)S(1)} collective-permute-done((f32[32,640]{1,0:T(8,128)S(1)}, f32[32,640]{1,0:T(8,128)S(1)}, u32[]{:S(2)}, u32[]{:S(2)}) %collective-permute-start.17) | collective-permute-done | bytes 81952 | tf_op jit(solution)/shard_map/ppermute | solution.py:246
  55.5 0.9 %shard_map.65 = (f32[128,128]{1,0:T(8,128)}, f32[512,128]{1,0:T(8,128)}) custom-call(f32[32,4,128]{2,1,0:T(4,128)S(1)} %all-to-all-done.1.squares_ref, f32[32,640]{1,0:T(8,128)S(1)} %collective-permute-done.16.refs_0_, f32[32,640]{1,0:T(8,128)S(1)} %collective-permute-done.17.refs_1_, f32[32,640]{1,0:T(8,128)S(1)} %collective-permute-done.18.refs_2_, ...), custom_call_target="tpu_custom_call" | custom-call | tf_op jit(solution)/shard_map/pallas_call | solution.py:25
  (29 shorter events, 1.4 us)
Async XLA Ops:
  0.6 4.5 %copy-start.3 = (s32[1,4,1,2]{1,3,2,0:T(2,128)S(1)}, s32[1,4,1,2]{1,3,2,0:T(2,128)}, u32[]{:S(2)}) copy-start(s32[1,4,1,2]{1,3,2,0:T(2,128)} %param.6) | copy-start | bytes 100
  0.6 11.3 %collective-permute-start = (bf16[1024,128]{1,0:T(8,128)(2,1)}, bf16[1024,128]{1,0:T(8,128)(2,1)S(1)}, u32[]{:S(2)}, u32[]{:S(2)}) collective-permute-start(bf16[1024,128]{1,0:T(8,128)(2,1)} %bitcast.6), channel_id=1, source_target_pairs={{0,1},{1,0},{2,3},{3,2},{4,5},{5,4},{6,7},{7,6},{8,24},{9,25},{10,... | collective-permute-start | bytes 786440 | tf_op jit(solution)/shard_map/ppermute | solution.py:246
  3.6 8.3 %collective-permute-start.1 = (bf16[1024,128]{1,0:T(8,128)(2,1)}, bf16[1024,128]{1,0:T(8,128)(2,1)S(1)}, u32[]{:S(2)}, u32[]{:S(2)}) collective-permute-start(bf16[1024,128]{1,0:T(8,128)(2,1)} %bitcast.7), channel_id=1, source_target_pairs={{0,16},{1,17},{2,18},{3,19},{4,20},{5,21},{6,22},{7,23},{8,9},{9,8... | collective-permute-start | bytes 786440 | tf_op jit(solution)/shard_map/ppermute | solution.py:246
  5.3 0.8 %copy-start.2 = (bf16[128,128]{1,0:T(8,128)(2,1)S(1)}, bf16[128,128]{1,0:T(8,128)(2,1)}, u32[]{:S(2)}) copy-start(bf16[128,128]{1,0:T(8,128)(2,1)} %start_ref.1) | copy-start | bytes 98308
  6.0 14.0 %copy-start = (bf16[1,4,1,2,128,128]{5,4,3,2,1,0:T(8,128)(2,1)S(1)}, bf16[1,4,1,2,128,128]{5,4,3,2,1,0:T(8,128)(2,1)}, u32[]{:S(2)}) copy-start(bf16[1,4,1,2,128,128]{5,4,3,2,1,0:T(8,128)(2,1)} %param.5) | copy-start | bytes 786436
  6.8 7.1 %copy-start.1 = (bf16[128,512]{1,0:T(8,128)(2,1)S(1)}, bf16[128,512]{1,0:T(8,128)(2,1)}, u32[]{:S(2)}) copy-start(bf16[128,512]{1,0:T(8,128)(2,1)} %refs_0_.3) | copy-start | bytes 393220
  6.8 13.2 %all-to-all-start = ((bf16[16,48,128]{2,1,0:T(8,128)(2,1)}), bf16[16,48,128]{2,1,0:T(8,128)(2,1)S(1)}, u32[]{:S(2)}, u32[]{:S(2)}) async-start(bf16[16,48,128]{2,1,0:T(8,128)(2,1)} %bitcast.1), calls=%async_computation | async-start | bytes 393216 | tf_op jit(solution)/shard_map/all_to_all | solution.py:297
  12.0 9.3 %collective-permute-start.2 = (bf16[1024,128]{1,0:T(8,128)(2,1)S(1)}, bf16[1024,128]{1,0:T(8,128)(2,1)S(1)}, u32[]{:S(2)}, u32[]{:S(2)}) collective-permute-start(bf16[1024,128]{1,0:T(8,128)(2,1)S(1)} %collective-permute-done.refs_1_.refs_5_), channel_id=1, source_target_pairs={{0,16},{1,17},{2,18},{3,19},{4,20},{5,21},{6,22},{7,23},{8,9},{9,8... | collective-permute-start | bytes 786440 | tf_op jit(solution)/shard_map/ppermute | solution.py:246
  14.0 8.5 %collective-permute-start.8 = (bf16[128,512]{1,0:T(8,128)(2,1)S(1)}, bf16[128,512]{1,0:T(8,128)(2,1)S(1)}, u32[]{:S(2)}, u32[]{:S(2)}) collective-permute-start(bf16[128,512]{1,0:T(8,128)(2,1)S(1)} %copy-done.1), channel_id=1, source_target_pairs={{0,1},{1,0},{2,3},{3,2},{4,5},{5,4},{6,7},{7,6},{8,24},{9,25},{10,... | collective-permute-start | bytes 393224 | tf_op jit(solution)/shard_map/ppermute | solution.py:246
  21.5 2.1 %collective-permute-start.3 = (f32[2,2,32,128]{3,2,1,0:T(8,128)S(1)}, f32[2,2,32,128]{3,2,1,0:T(8,128)S(1)}, u32[]{:S(2)}, u32[]{:S(2)}) collective-permute-start(f32[2,2,32,128]{3,2,1,0:T(8,128)S(1)} %get-tuple-element.28), channel_id=1, source_target_pairs={{0,8},{1,9},{2,10},{3,11},{4,12},{5,13},{6,14},{7,15},{8,0},{9,1},... | collective-permute-start | bytes 196616 | tf_op jit(solution)/shard_map/ppermute | solution.py:258
  21.6 12.4 %collective-permute-start.9 = (bf16[128,512]{1,0:T(8,128)(2,1)S(1)}, bf16[128,512]{1,0:T(8,128)(2,1)S(1)}, u32[]{:S(2)}, u32[]{:S(2)}) collective-permute-start(bf16[128,512]{1,0:T(8,128)(2,1)S(1)} %copy-done.1), channel_id=1, source_target_pairs={{0,16},{1,17},{2,18},{3,19},{4,20},{5,21},{6,22},{7,23},{8,9},{9,8... | collective-permute-start | bytes 393224 | tf_op jit(solution)/shard_map/ppermute | solution.py:246
  22.4 11.5 %collective-permute-start.10 = (bf16[128,512]{1,0:T(8,128)(2,1)S(1)}, bf16[128,512]{1,0:T(8,128)(2,1)S(1)}, u32[]{:S(2)}, u32[]{:S(2)}) collective-permute-start(bf16[128,512]{1,0:T(8,128)(2,1)S(1)} %collective-permute-done.8.refs_1_), channel_id=1, source_target_pairs={{0,16},{1,17},{2,18},{3,19},{4,20},{5,21},{6,22},{7,23},{8,9},{9,8... | collective-permute-start | bytes 393224 | tf_op jit(solution)/shard_map/ppermute | solution.py:246
  23.7 4.5 %collective-permute-start.4 = (bf16[2,2,32,128]{3,2,1,0:T(8,128)(2,1)S(1)}, bf16[2,2,32,128]{3,2,1,0:T(8,128)(2,1)S(1)}, u32[]{:S(2)}, u32[]{:S(2)}) collective-permute-start(bf16[2,2,32,128]{3,2,1,0:T(8,128)(2,1)S(1)} %add_convert_fusion.refs_0_), channel_id=1, source_target_pairs={{0,2},{1,3},{2,0},{3,1},{4,6},{5,7},{6,4},{7,5},{8,10},{9,11},{10,... | collective-permute-start | bytes 98312 | tf_op jit(solution)/shard_map/ppermute | solution.py:258
  25.2 5.3 %collective-permute-start.5 = (bf16[2,2,32,128]{3,2,1,0:T(8,128)(2,1)S(1)}, bf16[2,2,32,128]{3,2,1,0:T(8,128)(2,1)S(1)}, u32[]{:S(2)}, u32[]{:S(2)}) collective-permute-start(bf16[2,2,32,128]{3,2,1,0:T(8,128)(2,1)S(1)} %add_convert_fusion.refs_0_), channel_id=1, source_target_pairs={{0,4},{1,5},{2,6},{3,7},{4,0},{5,1},{6,2},{7,3},{8,12},{9,13},{10,... | collective-permute-start | bytes 98312 | tf_op jit(solution)/shard_map/ppermute | solution.py:258
  27.4 5.7 %collective-permute-start.6 = (bf16[2,2,32,128]{3,2,1,0:T(8,128)(2,1)S(1)}, bf16[2,2,32,128]{3,2,1,0:T(8,128)(2,1)S(1)}, u32[]{:S(2)}, u32[]{:S(2)}) collective-permute-start(bf16[2,2,32,128]{3,2,1,0:T(8,128)(2,1)S(1)} %add_convert_fusion.refs_0_), channel_id=1, source_target_pairs={{0,6},{1,7},{2,4},{3,5},{4,2},{5,3},{6,0},{7,1},{8,14},{9,15},{10,... | collective-permute-start | bytes 98312 | tf_op jit(solution)/shard_map/ppermute | solution.py:258
  33.9 1.3 %collective-permute-start.7 = (f32[2,2,32,128]{3,2,1,0:T(8,128)S(1)}, f32[2,2,32,128]{3,2,1,0:T(8,128)S(1)}, u32[]{:S(2)}, u32[]{:S(2)}) collective-permute-start(f32[2,2,32,128]{3,2,1,0:T(8,128)S(1)} %get-tuple-element.30), channel_id=1, source_target_pairs={{0,8},{1,9},{2,10},{3,11},{4,12},{5,13},{6,14},{7,15},{8,0},{9,1},... | collective-permute-start | bytes 196616 | tf_op jit(solution)/shard_map/ppermute | solution.py:258
  35.4 1.2 %collective-permute-start.11 = (f32[32,256]{1,0:T(8,128)S(1)}, f32[32,256]{1,0:T(8,128)S(1)}, u32[]{:S(2)}, u32[]{:S(2)}) collective-permute-start(f32[32,256]{1,0:T(8,128)S(1)} %get-tuple-element.33), channel_id=1, source_target_pairs={{0,8},{1,9},{2,10},{3,11},{4,12},{5,13},{6,14},{7,15},{8,0},{9,1},... | collective-permute-start | bytes 98312 | tf_op jit(solution)/shard_map/ppermute | solution.py:258
  36.7 5.2 %collective-permute-start.13 = (f32[32,256]{1,0:T(8,128)S(1)}, f32[32,256]{1,0:T(8,128)S(1)}, u32[]{:S(2)}, u32[]{:S(2)}) collective-permute-start(f32[32,256]{1,0:T(8,128)S(1)} %add.16), channel_id=1, source_target_pairs={{0,4},{1,5},{2,6},{3,7},{4,0},{5,1},{6,2},{7,3},{8,12},{9,13},{10,... | collective-permute-start | bytes 98312 | tf_op jit(solution)/shard_map/ppermute | solution.py:258
  36.7 5.8 %collective-permute-start.14 = (f32[32,256]{1,0:T(8,128)S(1)}, f32[32,256]{1,0:T(8,128)S(1)}, u32[]{:S(2)}, u32[]{:S(2)}) collective-permute-start(f32[32,256]{1,0:T(8,128)S(1)} %add.16), channel_id=1, source_target_pairs={{0,6},{1,7},{2,4},{3,5},{4,2},{5,3},{6,0},{7,1},{8,14},{9,15},{10,... | collective-permute-start | bytes 98312 | tf_op jit(solution)/shard_map/ppermute | solution.py:258
  38.2 4.3 %collective-permute-start.12 = (f32[32,256]{1,0:T(8,128)S(1)}, f32[32,256]{1,0:T(8,128)S(1)}, u32[]{:S(2)}, u32[]{:S(2)}) collective-permute-start(f32[32,256]{1,0:T(8,128)S(1)} %add.16), channel_id=1, source_target_pairs={{0,2},{1,3},{2,0},{3,1},{4,6},{5,7},{6,4},{7,5},{8,10},{9,11},{10,... | collective-permute-start | bytes 98312 | tf_op jit(solution)/shard_map/ppermute | solution.py:258
  42.5 1.3 %collective-permute-start.15 = (f32[32,256]{1,0:T(8,128)S(1)}, f32[32,256]{1,0:T(8,128)S(1)}, u32[]{:S(2)}, u32[]{:S(2)}) collective-permute-start(f32[32,256]{1,0:T(8,128)S(1)} %add_add_fusion.mine_ref), channel_id=1, source_target_pairs={{0,8},{1,9},{2,10},{3,11},{4,12},{5,13},{6,14},{7,15},{8,0},{9,1},... | collective-permute-start | bytes 98312 | tf_op jit(solution)/shard_map/ppermute | solution.py:258
  44.9 10.5 %all-to-all-start.1 = ((f32[32,4,128]{2,1,0:T(4,128)}), f32[32,4,128]{2,1,0:T(4,128)S(1)}, u32[]{:S(2)}, u32[]{:S(2)}) async-start(f32[32,4,128]{2,1,0:T(4,128)} %get-tuple-element.35), calls=%async_computation.1 | async-start | bytes 131072 | tf_op jit(solution)/shard_map/all_to_all | solution.py:365
  47.5 6.6 %collective-permute-start.16 = (f32[32,640]{1,0:T(8,128)S(1)}, f32[32,640]{1,0:T(8,128)S(1)}, u32[]{:S(2)}, u32[]{:S(2)}) collective-permute-start(f32[32,640]{1,0:T(8,128)S(1)} %get-tuple-element.36), channel_id=1, source_target_pairs={{0,17},{1,16},{2,19},{3,18},{4,21},{5,20},{6,23},{7,22},{8,25},{9,... | collective-permute-start | bytes 245768 | tf_op jit(solution)/shard_map/ppermute | solution.py:246
  50.2 5.3 %collective-permute-start.17 = (f32[32,640]{1,0:T(8,128)S(1)}, f32[32,640]{1,0:T(8,128)S(1)}, u32[]{:S(2)}, u32[]{:S(2)}) collective-permute-start(f32[32,640]{1,0:T(8,128)S(1)} %get-tuple-element.37), channel_id=1, source_target_pairs={{0,16},{1,17},{2,18},{3,19},{4,20},{5,21},{6,22},{7,23},{8,9},{9,8... | collective-permute-start | bytes 245768 | tf_op jit(solution)/shard_map/ppermute | solution.py:246
  50.7 4.7 %collective-permute-start.18 = (f32[32,640]{1,0:T(8,128)S(1)}, f32[32,640]{1,0:T(8,128)S(1)}, u32[]{:S(2)}, u32[]{:S(2)}) collective-permute-start(f32[32,640]{1,0:T(8,128)S(1)} %get-tuple-element.38), channel_id=1, source_target_pairs={{0,1},{1,0},{2,3},{3,2},{4,5},{5,4},{6,7},{7,6},{8,24},{9,25},{10,... | collective-permute-start | bytes 245768 | tf_op jit(solution)/shard_map/ppermute | solution.py:246

commit v5 on v4

--- a/solution.py
+++ b/solution.py
@@ -69,12 +69,12 @@
 
 def prepare(lanes, width, columns_ref, start_ref, parts_ref):
     n_block, n_col, rows, order = parts_ref.shape
-    groups, slots = columns_ref.shape
+    slots, groups = columns_ref.shape
     lane = lax.broadcasted_iota(jnp.int32, (PAD, order), 1)
     numbers = jnp.zeros(lane.shape, jnp.int32)
     for p in range(groups):
         for s in range(slots):
-            numbers = jnp.where(lane == p * slots + s, columns_ref[p, s], numbers)
+            numbers = jnp.where(lane == p * slots + s, columns_ref[s, p], numbers)
     numbers = numbers.astype(F32).astype(BF16)
     turned = start_ref[...].astype(F32).T
     for r in range(n_block):
@@ -143,11 +143,11 @@
 def second(near, slots, n_vectors, columns_ref, start_ref, *refs):
     count = len(near)
     vectors, tiles, refs = refs[:n_vectors], refs[n_vectors : n_vectors + count], refs[n_vectors + count :]
-    keep_ref, give_ref, sums_ref = refs[:3]
-    lanes, n_block, _, _ = keep_ref.shape
+    out_ref, sums_ref = refs[:2]
+    lanes, n_block, _, _ = start_ref.shape
     _, core, me_z, me_lane = position(lanes)
     if n_vectors > 1:
-        all_ref = refs[3]
+        all_ref = refs[2]
         for k in range(n_vectors):
             all_ref[me_z ^ k] = vectors[k][...]
     else:
@@ -160,42 +160,51 @@
     multiply(near, lanes, slots, columns_ref, segment, list(enumerate(tiles)), sums_ref)
     for u in range(lanes):
         for r in range(n_block):
-            keep_ref[u, r] = 2.0 * sums_ref[u, 2 * r + core] - start_ref[u, r].astype(F32)
-            give_ref[u, r] = 2.0 * sums_ref[u, 2 * r + (1 - core)]
-
-
-def project(near, keep_ref, given_ref, *refs):
-    history, (filtered_ref, coeffs_keep_ref, coeffs_give_ref) = refs[: len(near)], refs[len(near) :]
-    lanes = keep_ref.shape[0]
+            out_ref[u, 2 * r + core] = 2.0 * sums_ref[u, 2 * r + core] - start_ref[u, r].astype(F32)
+            out_ref[u, 2 * r + (1 - core)] = 2.0 * sums_ref[u, 2 * r + (1 - core)]
+
+
+def project(near, ours_ref, theirs_ref, *refs):
+    history, (filtered_ref, coeffs_ref) = refs[: len(near)], refs[len(near) :]
+    lanes = ours_ref.shape[0]
     block, core, _, _ = position(lanes)
-    filtered_ref[...] = keep_ref[...] + given_ref[...]
+    filtered_ref[...] = ours_ref[...] + theirs_ref[...]
     total = None
     for i, entry in enumerate(near):
         q, u = place(entry, core)
-        split = pieces(filtered_ref[u, block ^ q])
-        term = joined(jnp.dot(split, history[i][...], preferred_element_type=F32))
-        total = term if total is None else total + term
-    half = total.shape[1] // 2
-    low, high = total[:, :half], total[:, half:]
-    coeffs_keep_ref[...] = jnp.where(core == 0, low, high)
-    coeffs_give_ref[...] = jnp.where(core == 0, high, low)
-
-
-def clean(near, mine_ref, mate_ref, filtered_ref, *refs):
+        for side in range(2):
+            split = pieces(filtered_ref[u, 2 * (block ^ q) + side])
+            term = joined(jnp.dot(split, history[i][side], preferred_element_type=F32))
+            total = term if total is None else total + term
+    coeffs_ref[...] = total
+
+
+def correct(near, coeffs_ref, *refs):
+    history, (keep_ref, give_ref) = refs[: len(near)], refs[len(near) :]
+    lanes = keep_ref.shape[0]
+    block, core, _, _ = position(lanes)
+    split = pieces(coeffs_ref[...])
+    for i, entry in enumerate(near):
+        q, u = place(entry, core)
+        keep_ref[u, block ^ q] = joined(nt(split, history[i][core]))
+        give_ref[u, block ^ q] = joined(nt(split, history[i][1 - core]))
+
+
+def clean(near, mine_ref, mate_ref, filtered_ref, ours_ref, theirs_ref, *refs):
     count = len(near)
-    history, outs, squares_ref = refs[:count], refs[count : 2 * count], refs[2 * count]
-    lanes, _, width, order = filtered_ref.shape
+    outs, squares_ref = refs[:count], refs[count]
+    lanes, _, width, order = ours_ref.shape
     block, core, _, me_lane = position(lanes)
     mine, mate = mine_ref[...], mate_ref[...]
     coeffs = jnp.concatenate(
         [jnp.where(core == 0, mine, mate), jnp.where(core == 0, mate, mine)], axis=1
     )
     stored = coeffs.shape[1]
-    split = pieces(coeffs)
     squares = jnp.zeros((width, order), F32)
     for i, entry in enumerate(near):
         q, u = place(entry, core)
-        cleaned = filtered_ref[u, block ^ q] - joined(nt(split, history[i][...]))
+        r = block ^ q
+        cleaned = filtered_ref[u, 2 * r + core] - (ours_ref[u, r] + theirs_ref[u, r])
         squares = squares + cleaned * cleaned
         outs[i][:, :stored] = coeffs
         outs[i][:, stored:] = cleaned
@@ -289,7 +298,7 @@
     parts = call(
         functools.partial(prepare, lanes, width),
         jax.ShapeDtypeStruct((n_block, n_col, tall, order), BF16),
-        (tile_columns.reshape(groups, slots), start_block),
+        (tile_columns.reshape(groups, slots).T, start_block),
     )
     cores = [
         [(2 * r + core) * n_col + c for r in range(n_block) for c in range(n_col)] for core in range(2)
@@ -297,6 +306,12 @@
     parts = lax.all_to_all(
         parts.reshape(n_block * n_col, tall, order), BOTH, 0, 0, axis_index_groups=cores
     ).reshape(n_block, n_col, tall, order)
+    core = lax.axis_index("row") & 1
+    half = stored // 2
+    low, high = history[:, :half], history[:, half:]
+    ours = jnp.where(core == 0, low, high)
+    theirs = mate(jnp.where(core == 0, high, low))
+    history = jnp.where(core == 0, jnp.stack([ours, theirs]), jnp.stack([theirs, ours]))
     own = [history]
     if plane:
         history, tiles[2] = lax.optimization_barrier((history, tiles[2]))
@@ -332,18 +347,17 @@
                 jnp.broadcast_to(mine, (members,) + piece), "col", 0, 0, axis_index_groups=alike
             )
         ]
-    keep, give = call(
+    ours = call(
         functools.partial(second, near, slots, len(vectors)),
-        [jax.ShapeDtypeStruct(piece, F32)] * 2,
+        jax.ShapeDtypeStruct(sums[0], F32),
         (columns, start, *vectors, *tiles),
         [sums] + ([((members,) + piece, BF16)] if few else []),
     )
-    filtered, coeffs, coeffs_give = call(
+    filtered, coeffs = call(
         functools.partial(project, near),
-        [jax.ShapeDtypeStruct(piece, F32)] + [jax.ShapeDtypeStruct((width, stored // 2), F32)] * 2,
-        (keep, mate(give), *own),
-    )
-    coeffs = coeffs + mate(coeffs_give)
+        [jax.ShapeDtypeStruct(sums[0], F32), jax.ShapeDtypeStruct((width, half), F32)],
+        (ours, mate(ours), *own),
+    )
     if members == 4:
         zero, one, two, three = over_members(coeffs)
         coeffs = (zero + one) + (two + three)
@@ -356,10 +370,15 @@
     copies = 1
     while nbytes(slab) > 2 * n_row * n_col * copies * n_vectors * 4:
         copies *= 2
+    keep, give = call(
+        functools.partial(correct, near),
+        [jax.ShapeDtypeStruct(piece, F32)] * 2,
+        (coeffs, *own),
+    )
     *slabs, squares = call(
         functools.partial(clean, near),
         [slab] * count + [jax.ShapeDtypeStruct((n_row * n_col, copies, n_vectors), F32)],
-        (coeffs, mate(coeffs), filtered, *own),
+        (coeffs, mate(coeffs), filtered, keep, mate(give)),
     )
     slabs = [slabs[0]] + [crossed(a, entry) for a, entry in zip(slabs[1:], near[1:])]
     squares = lax.all_to_all(squares, BOTH, 0, 0)

time: 56.7 us -> 55.1 us (0.972)
  waiting for transfers between devices: 20.5 us -> 17.9 us
  starting transfers between devices: 29.6 us -> 30.6 us
    ppermute x10 -> x11, waiting for transfers between devices: 10.9 us -> 7.31 us  [swapped(): return lax.ppermute(value, BOTH, pairs)]
    ppermute x9, waiting for transfers between devices: 4.97 us -> 5.87 us  [crossed(): return lax.ppermute(value, BOTH, pairs)]
    all_to_all x1, starting transfers between devices: 2.57 us -> 3.19 us  [per_device(): squares = lax.all_to_all(squares, BOTH, 0, 0)]
    ppermute x10 -> x11, starting transfers between devices: 8.3 us -> 8.73 us  [swapped(): return lax.ppermute(value, BOTH, pairs)]
    pallas_call x7 -> x8, Pallas kernels: 4.65 us -> 4.71 us  [call(): pl.pallas_call(kernel, out_shape=out, in_specs=[VMEM] * len(args), out_sp...]
  transfers between devices with their start and end apart: 21 -> 22, of which waited for: 11 -> 10; matrix products, arithmetic and copies ran while one was open for 0% -> 0% of each run, Pallas kernels for 4% -> 4%
where the time goes in v5:
time: 55.1 us; the launch traced here: 54.8 us
  starting transfers between devices  30.6 us (56%)
  waiting for transfers between devices  17.9 us (32%)
  Pallas kernels  4.71 us (9%)
  between operations  0.78 us (1%)
  local copies, waits for them, and re-layouts  0.77 us (1%)
    ppermute x9, starting transfers between devices, crossed(): return lax.ppermute(value, BOTH, pairs)  13.6 us
    ppermute x11, starting transfers between devices, swapped(): return lax.ppermute(value, BOTH, pairs)  8.73 us
    ppermute x11, waiting for transfers between devices, swapped(): return lax.ppermute(value, BOTH, pairs)  7.31 us
    ppermute x9, waiting for transfers between devices, crossed(): return lax.ppermute(value, BOTH, pairs)  5.87 us
    all_to_all x1, starting transfers between devices, per_device(): lax.all_to_all(parts.reshape(n_block * n_col, tall, order), BOTH, 0, 0, a...  5.11 us
    pallas_call x8, Pallas kernels, call(): pl.pallas_call(kernel, out_shape=out, in_specs=[VMEM] * len(args), out_sp...  4.71 us
    all_to_all x1, waiting for transfers between devices, per_device(): lax.all_to_all(parts.reshape(n_block * n_col, tall, order), BOTH, 0, 0, a...  4.7 us
    all_to_all x1, starting transfers between devices, per_device(): squares = lax.all_to_all(squares, BOTH, 0, 0)  3.19 us
  transfers between devices with their start and end apart: 22, of which 10 were waited for; matrix products, arithmetic and copies ran while one was open for 0% of the time, Pallas kernels for 4%

profile of v5, /device:TPU:0, one launch (start us, length us, event | category | flops | bytes accessed | tf_op | source)
XLA Modules:
  0.0 54.8 jit_solution(11488575091471910070)
XLA Ops:
  0.6 3.0 %collective-permute-start = (bf16[1024,128]{1,0:T(8,128)(2,1)}, bf16[1024,128]{1,0:T(8,128)(2,1)S(1)}, u32[]{:S(2)}, u32[]{:S(2)}) collective-permute-start(bf16[1024,128]{1,0:T(8,128)(2,1)} %bitcast.11), channel_id=1, source_target_pairs={{0,1},{1,0},{2,3},{3,2},{4,5},{5,4},{6,7},{7,6},{8,24},{9,25},{10,... | collective-permute-start | bytes 786440 | tf_op jit(solution)/shard_map/ppermute | solution.py:255
  3.6 1.5 %collective-permute-start.1 = (bf16[1024,128]{1,0:T(8,128)(2,1)}, bf16[1024,128]{1,0:T(8,128)(2,1)S(1)}, u32[]{:S(2)}, u32[]{:S(2)}) collective-permute-start(bf16[1024,128]{1,0:T(8,128)(2,1)} %bitcast.12), channel_id=1, source_target_pairs={{0,16},{1,17},{2,18},{3,19},{4,20},{5,21},{6,22},{7,23},{8,9},{9,8... | collective-permute-start | bytes 786440 | tf_op jit(solution)/shard_map/ppermute | solution.py:255
  5.2 0.8 %copy-done.1 = bf16[128,128]{1,0:T(8,128)(2,1)S(1)} copy-done((bf16[128,128]{1,0:T(8,128)(2,1)S(1)}, bf16[128,128]{1,0:T(8,128)(2,1)}, u32[]{:S(2)}) %copy-start.1) | copy-done | bytes 32792
  5.9 0.8 %shard_map.59 = bf16[2,8,48,128]{3,2,1,0:T(8,128)(2,1)} custom-call(s32[2,4]{1,0:T(2,128)S(1)} %bitcast.15, bf16[128,128]{1,0:T(8,128)(2,1)S(1)} %copy-done.1), custom_call_target="tpu_custom_call" | custom-call | tf_op jit(solution)/shard_map/pallas_call | solution.py:25
  6.7 5.1 %all-to-all-start = ((bf16[16,48,128]{2,1,0:T(8,128)(2,1)}), bf16[16,48,128]{2,1,0:T(8,128)(2,1)S(1)}, u32[]{:S(2)}, u32[]{:S(2)}) async-start(bf16[16,48,128]{2,1,0:T(8,128)(2,1)} %bitcast.2), calls=%async_computation | async-start | bytes 393216 | tf_op jit(solution)/shard_map/all_to_all | solution.py:306
  11.9 2.0 %collective-permute-start.3 = (bf16[1024,128]{1,0:T(8,128)(2,1)S(1)}, bf16[1024,128]{1,0:T(8,128)(2,1)S(1)}, u32[]{:S(2)}, u32[]{:S(2)}) collective-permute-start(bf16[1024,128]{1,0:T(8,128)(2,1)S(1)} %collective-permute-done.refs_1_.refs_5_), channel_id=1, source_target_pairs={{0,16},{1,17},{2,18},{3,19},{4,20},{5,21},{6,22},{7,23},{8,9},{9,8... | collective-permute-start | bytes 786440 | tf_op jit(solution)/shard_map/ppermute | solution.py:255
  14.0 1.2 %collective-permute-done.2 = bf16[128,256]{1,0:T(8,128)(2,1)S(1)} collective-permute-done((bf16[128,256]{1,0:T(8,128)(2,1)S(1)}, bf16[128,256]{1,0:T(8,128)(2,1)S(1)}, u32[]{:S(2)}, u32[]{:S(2)}) %collective-permute-start.2) | collective-permute-done | bytes 65568 | tf_op jit(solution)/shard_map/ppermute | solution.py:267
  15.2 4.7 %all-to-all-done = bf16[16,48,128]{2,1,0:T(8,128)(2,1)S(1)} async-done(((bf16[16,48,128]{2,1,0:T(8,128)(2,1)}), bf16[16,48,128]{2,1,0:T(8,128)(2,1)S(1)}, u32[]{:S(2)}, u32[]{:S(2)}) %all-to-all-start) | async-done | bytes 196640 | tf_op jit(solution)/shard_map/all_to_all | solution.py:306
  19.9 0.6 %shard_map.60 = (f32[2,4,32,128]{3,2,1,0:T(8,128)S(1)}, s32[4,128,8]{2,1,0:T(8,128)S(1)}, bf16[2,2,32,128]{3,2,1,0:T(8,128)(2,1)S(1)}) custom-call(bf16[2,8,48,128]{3,2,1,0:T(8,128)(2,1)S(1)} %bitcast.9, bf16[1024,128]{1,0:T(8,128)(2,1)S(1)} %bitcast.13, bf16[1024,128]{1,0:T(8,128)(2,1)S(1)} %collective-permute-done.refs_1_.refs_5_, ...), custom_call_target="tpu_custom_call" | custom-call | tf_op jit(solution)/shard_map/pallas_call | solution.py:25
  20.9 1.5 %collective-permute-start.9 = (bf16[2,128,256]{2,1,0:T(8,128)(2,1)S(1)}, bf16[2,128,256]{2,1,0:T(8,128)(2,1)S(1)}, u32[]{:S(2)}, u32[]{:S(2)}) collective-permute-start(bf16[2,128,256]{2,1,0:T(8,128)(2,1)S(1)} %maximum_select_fusion.refs_0_), channel_id=1, source_target_pairs={{0,1},{1,0},{2,3},{3,2},{4,5},{5,4},{6,7},{7,6},{8,24},{9,25},{10,... | collective-permute-start | bytes 393224 | tf_op jit(solution)/shard_map/ppermute | solution.py:255
  22.4 0.6 %collective-permute-start.5 = (bf16[2,2,32,128]{3,2,1,0:T(8,128)(2,1)S(1)}, bf16[2,2,32,128]{3,2,1,0:T(8,128)(2,1)S(1)}, u32[]{:S(2)}, u32[]{:S(2)}) collective-permute-start(bf16[2,2,32,128]{3,2,1,0:T(8,128)(2,1)S(1)} %add_convert_fusion.refs_0_), channel_id=1, source_target_pairs={{0,2},{1,3},{2,0},{3,1},{4,6},{5,7},{6,4},{7,5},{8,10},{9,11},{10,... | collective-permute-start | bytes 98312 | tf_op jit(solution)/shard_map/ppermute | solution.py:267
  23.0 2.3 %collective-permute-start.6 = (bf16[2,2,32,128]{3,2,1,0:T(8,128)(2,1)S(1)}, bf16[2,2,32,128]{3,2,1,0:T(8,128)(2,1)S(1)}, u32[]{:S(2)}, u32[]{:S(2)}) collective-permute-start(bf16[2,2,32,128]{3,2,1,0:T(8,128)(2,1)S(1)} %add_convert_fusion.refs_0_), channel_id=1, source_target_pairs={{0,4},{1,5},{2,6},{3,7},{4,0},{5,1},{6,2},{7,3},{8,12},{9,13},{10,... | collective-permute-start | bytes 98312 | tf_op jit(solution)/shard_map/ppermute | solution.py:267
  25.3 1.6 %collective-permute-start.7 = (bf16[2,2,32,128]{3,2,1,0:T(8,128)(2,1)S(1)}, bf16[2,2,32,128]{3,2,1,0:T(8,128)(2,1)S(1)}, u32[]{:S(2)}, u32[]{:S(2)}) collective-permute-start(bf16[2,2,32,128]{3,2,1,0:T(8,128)(2,1)S(1)} %add_convert_fusion.refs_0_), channel_id=1, source_target_pairs={{0,6},{1,7},{2,4},{3,5},{4,2},{5,3},{6,0},{7,1},{8,14},{9,15},{10,... | collective-permute-start | bytes 98312 | tf_op jit(solution)/shard_map/ppermute | solution.py:267
  26.9 0.8 %collective-permute-start.10 = (bf16[2,128,256]{2,1,0:T(8,128)(2,1)S(1)}, bf16[2,128,256]{2,1,0:T(8,128)(2,1)S(1)}, u32[]{:S(2)}, u32[]{:S(2)}) collective-permute-start(bf16[2,128,256]{2,1,0:T(8,128)(2,1)S(1)} %maximum_select_fusion.refs_0_), channel_id=1, source_target_pairs={{0,16},{1,17},{2,18},{3,19},{4,20},{5,21},{6,22},{7,23},{8,9},{9,8... | collective-permute-start | bytes 393224 | tf_op jit(solution)/shard_map/ppermute | solution.py:255
  27.7 1.2 %collective-permute-start.11 = (bf16[2,128,256]{2,1,0:T(8,128)(2,1)S(1)}, bf16[2,128,256]{2,1,0:T(8,128)(2,1)S(1)}, u32[]{:S(2)}, u32[]{:S(2)}) collective-permute-start(bf16[2,128,256]{2,1,0:T(8,128)(2,1)S(1)} %collective-permute-done.9.refs_1_), channel_id=1, source_target_pairs={{0,16},{1,17},{2,18},{3,19},{4,20},{5,21},{6,22},{7,23},{8,9},{9,8... | collective-permute-start | bytes 393224 | tf_op jit(solution)/shard_map/ppermute | solution.py:255
  28.9 2.1 %collective-permute-done.7.refs_3_ = bf16[2,2,32,128]{3,2,1,0:T(8,128)(2,1)S(1)} collective-permute-done((bf16[2,2,32,128]{3,2,1,0:T(8,128)(2,1)S(1)}, bf16[2,2,32,128]{3,2,1,0:T(8,128)(2,1)S(1)}, u32[]{:S(2)}, u32[]{:S(2)}) %collective-permute-start.7) | collective-permute-done | bytes 32800 | tf_op jit(solution)/shard_map/ppermute | solution.py:267
  31.0 0.7 %shard_map.62.ours_ref = f32[2,4,32,128]{3,2,1,0:T(8,128)S(1)} custom-call(s32[4,128,8]{2,1,0:T(8,128)S(1)} %get-tuple-element.23.columns_ref, bf16[2,2,32,128]{3,2,1,0:T(8,128)(2,1)S(1)} %get-tuple-element.24.start_ref, bf16[2,2,32,128]{3,2,1,0:T(8,128)(2,1)S(1)} %add_convert_fusion.refs_0_, bf16[2,2,32,128]{3,2,1,0:T(8,128)(2,1)S(1)} %collective-permute-done.5.refs_1_, ...), custom_call_target="tpu_custom_call" | custom-call | tf_op jit(solution)/shard_map/pallas_call | solution.py:25
  31.8 1.4 %collective-permute-done.11.refs_3_ = bf16[2,128,256]{2,1,0:T(8,128)(2,1)S(1)} collective-permute-done((bf16[2,128,256]{2,1,0:T(8,128)(2,1)S(1)}, bf16[2,128,256]{2,1,0:T(8,128)(2,1)S(1)}, u32[]{:S(2)}, u32[]{:S(2)}) %collective-permute-start.11) | collective-permute-done | bytes 131104 | tf_op jit(solution)/shard_map/ppermute | solution.py:255
  33.5 0.6 %collective-permute-start.13 = (f32[32,256]{1,0:T(8,128)S(1)}, f32[32,256]{1,0:T(8,128)S(1)}, u32[]{:S(2)}, u32[]{:S(2)}) collective-permute-start(f32[32,256]{1,0:T(8,128)S(1)} %get-tuple-element.29), channel_id=1, source_target_pairs={{0,4},{1,5},{2,6},{3,7},{4,0},{5,1},{6,2},{7,3},{8,12},{9,13},{10,... | collective-permute-start | bytes 98312 | tf_op jit(solution)/shard_map/ppermute | solution.py:267
  34.1 1.8 %collective-permute-start.14 = (f32[32,256]{1,0:T(8,128)S(1)}, f32[32,256]{1,0:T(8,128)S(1)}, u32[]{:S(2)}, u32[]{:S(2)}) collective-permute-start(f32[32,256]{1,0:T(8,128)S(1)} %get-tuple-element.29), channel_id=1, source_target_pairs={{0,6},{1,7},{2,4},{3,5},{4,2},{5,3},{6,0},{7,1},{8,14},{9,15},{10,... | collective-permute-start | bytes 98312 | tf_op jit(solution)/shard_map/ppermute | solution.py:267
  35.9 1.2 %collective-permute-start.12 = (f32[32,256]{1,0:T(8,128)S(1)}, f32[32,256]{1,0:T(8,128)S(1)}, u32[]{:S(2)}, u32[]{:S(2)}) collective-permute-start(f32[32,256]{1,0:T(8,128)S(1)} %get-tuple-element.29), channel_id=1, source_target_pairs={{0,2},{1,3},{2,0},{3,1},{4,6},{5,7},{6,4},{7,5},{8,10},{9,11},{10,... | collective-permute-start | bytes 98312 | tf_op jit(solution)/shard_map/ppermute | solution.py:267
  37.1 1.8 %collective-permute-done.13 = f32[32,256]{1,0:T(8,128)S(1)} collective-permute-done((f32[32,256]{1,0:T(8,128)S(1)}, f32[32,256]{1,0:T(8,128)S(1)}, u32[]{:S(2)}, u32[]{:S(2)}) %collective-permute-start.13) | collective-permute-done | bytes 32800 | tf_op jit(solution)/shard_map/ppermute | solution.py:267
  38.8 1.1 %collective-permute-done.14 = f32[32,256]{1,0:T(8,128)S(1)} collective-permute-done((f32[32,256]{1,0:T(8,128)S(1)}, f32[32,256]{1,0:T(8,128)S(1)}, u32[]{:S(2)}, u32[]{:S(2)}) %collective-permute-start.14) | collective-permute-done | bytes 32800 | tf_op jit(solution)/shard_map/ppermute | solution.py:267
  40.5 0.5 collective-permute-start.15
  41.0 0.9 %collective-permute-done.15.mate_ref = f32[32,256]{1,0:T(8,128)S(1)} collective-permute-done((f32[32,256]{1,0:T(8,128)S(1)}, f32[32,256]{1,0:T(8,128)S(1)}, u32[]{:S(2)}, u32[]{:S(2)}) %collective-permute-start.15) | collective-permute-done | bytes 32800 | tf_op jit(solution)/shard_map/ppermute | solution.py:267
  41.9 0.9 %shard_map.65 = (f32[32,640]{1,0:T(8,128)S(1)}, f32[32,640]{1,0:T(8,128)S(1)}, f32[32,640]{1,0:T(8,128)S(1)}, f32[32,640]{1,0:T(8,128)S(1)}, f32[32,4,128]{2,1,0:T(4,128)}) custom-call(f32[32,256]{1,0:T(8,128)S(1)} %add_add_fusion.coeffs_ref.mine_ref, f32[32,256]{1,0:T(8,128)S(1)} %collective-permute-done.15.mate_ref, ...), custom_call_target="tpu_custom_call" | custom-call | tf_op jit(solution)/shard_map/pallas_call | solution.py:25
  42.7 3.2 %all-to-all-start.1 = ((f32[32,4,128]{2,1,0:T(4,128)}), f32[32,4,128]{2,1,0:T(4,128)S(1)}, u32[]{:S(2)}, u32[]{:S(2)}) async-start(f32[32,4,128]{2,1,0:T(4,128)} %get-tuple-element.33), calls=%async_computation.1 | async-start | bytes 131072 | tf_op jit(solution)/shard_map/all_to_all | solution.py:384
  45.9 2.7 %collective-permute-start.17 = (f32[32,640]{1,0:T(8,128)S(1)}, f32[32,640]{1,0:T(8,128)S(1)}, u32[]{:S(2)}, u32[]{:S(2)}) collective-permute-start(f32[32,640]{1,0:T(8,128)S(1)} %get-tuple-element.34), channel_id=1, source_target_pairs={{0,17},{1,16},{2,19},{3,18},{4,21},{5,20},{6,23},{7,22},{8,25},{9,... | collective-permute-start | bytes 245768 | tf_op jit(solution)/shard_map/ppermute | solution.py:255
  48.7 0.6 %collective-permute-start.18 = (f32[32,640]{1,0:T(8,128)S(1)}, f32[32,640]{1,0:T(8,128)S(1)}, u32[]{:S(2)}, u32[]{:S(2)}) collective-permute-start(f32[32,640]{1,0:T(8,128)S(1)} %get-tuple-element.35), channel_id=1, source_target_pairs={{0,16},{1,17},{2,18},{3,19},{4,20},{5,21},{6,22},{7,23},{8,9},{9,8... | collective-permute-start | bytes 245768 | tf_op jit(solution)/shard_map/ppermute | solution.py:255
  49.5 3.0 %collective-permute-done.17.refs_0_ = f32[32,640]{1,0:T(8,128)S(1)} collective-permute-done((f32[32,640]{1,0:T(8,128)S(1)}, f32[32,640]{1,0:T(8,128)S(1)}, u32[]{:S(2)}, u32[]{:S(2)}) %collective-permute-start.17) | collective-permute-done | bytes 81952 | tf_op jit(solution)/shard_map/ppermute | solution.py:255
  52.5 1.4 %collective-permute-done.18.refs_1_ = f32[32,640]{1,0:T(8,128)S(1)} collective-permute-done((f32[32,640]{1,0:T(8,128)S(1)}, f32[32,640]{1,0:T(8,128)S(1)}, u32[]{:S(2)}, u32[]{:S(2)}) %collective-permute-start.18) | collective-permute-done | bytes 81952 | tf_op jit(solution)/shard_map/ppermute | solution.py:255
  53.9 0.9 %shard_map.66 = (f32[128,128]{1,0:T(8,128)}, f32[512,128]{1,0:T(8,128)}) custom-call(f32[32,4,128]{2,1,0:T(4,128)S(1)} %all-to-all-done.1.squares_ref, f32[32,640]{1,0:T(8,128)S(1)} %collective-permute-done.17.refs_0_, f32[32,640]{1,0:T(8,128)S(1)} %collective-permute-done.18.refs_1_, f32[32,640]{1,0:T(8,128)S(1)} %collective-permute-done.19.refs_2_, ...), custom_call_target="tpu_custom_call" | custom-call | tf_op jit(solution)/shard_map/pallas_call | solution.py:25
  (32 shorter events, 1.6 us)
Async XLA Ops:
  0.6 4.5 %copy-start.2 = (s32[1,4,1,2]{1,3,2,0:T(2,128)S(1)}, s32[1,4,1,2]{1,3,2,0:T(2,128)}, u32[]{:S(2)}) copy-start(s32[1,4,1,2]{1,3,2,0:T(2,128)} %param.6) | copy-start | bytes 100
  0.6 11.2 %collective-permute-start = (bf16[1024,128]{1,0:T(8,128)(2,1)}, bf16[1024,128]{1,0:T(8,128)(2,1)S(1)}, u32[]{:S(2)}, u32[]{:S(2)}) collective-permute-start(bf16[1024,128]{1,0:T(8,128)(2,1)} %bitcast.11), channel_id=1, source_target_pairs={{0,1},{1,0},{2,3},{3,2},{4,5},{5,4},{6,7},{7,6},{8,24},{9,25},{10,... | collective-permute-start | bytes 786440 | tf_op jit(solution)/shard_map/ppermute | solution.py:255
  3.6 8.2 %collective-permute-start.1 = (bf16[1024,128]{1,0:T(8,128)(2,1)}, bf16[1024,128]{1,0:T(8,128)(2,1)S(1)}, u32[]{:S(2)}, u32[]{:S(2)}) collective-permute-start(bf16[1024,128]{1,0:T(8,128)(2,1)} %bitcast.12), channel_id=1, source_target_pairs={{0,16},{1,17},{2,18},{3,19},{4,20},{5,21},{6,22},{7,23},{8,9},{9,8... | collective-permute-start | bytes 786440 | tf_op jit(solution)/shard_map/ppermute | solution.py:255
  5.2 0.8 %copy-start.1 = (bf16[128,128]{1,0:T(8,128)(2,1)S(1)}, bf16[128,128]{1,0:T(8,128)(2,1)}, u32[]{:S(2)}) copy-start(bf16[128,128]{1,0:T(8,128)(2,1)} %start_ref.1) | copy-start | bytes 98308
  6.7 7.1 %copy-start.3 = (bf16[128,512]{1,0:T(8,128)(2,1)S(1)}, bf16[128,512]{1,0:T(8,128)(2,1)}, u32[]{:S(2)}) copy-start(bf16[128,512]{1,0:T(8,128)(2,1)} %param.7) | copy-start | bytes 393220
  6.7 13.2 %all-to-all-start = ((bf16[16,48,128]{2,1,0:T(8,128)(2,1)}), bf16[16,48,128]{2,1,0:T(8,128)(2,1)S(1)}, u32[]{:S(2)}, u32[]{:S(2)}) async-start(bf16[16,48,128]{2,1,0:T(8,128)(2,1)} %bitcast.2), calls=%async_computation | async-start | bytes 393216 | tf_op jit(solution)/shard_map/all_to_all | solution.py:306
  11.9 8.1 %copy-start = (bf16[1,4,1,2,128,128]{5,4,3,2,1,0:T(8,128)(2,1)S(1)}, bf16[1,4,1,2,128,128]{5,4,3,2,1,0:T(8,128)(2,1)}, u32[]{:S(2)}) copy-start(bf16[1,4,1,2,128,128]{5,4,3,2,1,0:T(8,128)(2,1)} %param.5) | copy-start | bytes 786436
  11.9 8.7 %collective-permute-start.3 = (bf16[1024,128]{1,0:T(8,128)(2,1)S(1)}, bf16[1024,128]{1,0:T(8,128)(2,1)S(1)}, u32[]{:S(2)}, u32[]{:S(2)}) collective-permute-start(bf16[1024,128]{1,0:T(8,128)(2,1)S(1)} %collective-permute-done.refs_1_.refs_5_), channel_id=1, source_target_pairs={{0,16},{1,17},{2,18},{3,19},{4,20},{5,21},{6,22},{7,23},{8,9},{9,8... | collective-permute-start | bytes 786440 | tf_op jit(solution)/shard_map/ppermute | solution.py:255
  13.9 1.3 %collective-permute-start.2 = (bf16[128,256]{1,0:T(8,128)(2,1)S(1)}, bf16[128,256]{1,0:T(8,128)(2,1)S(1)}, u32[]{:S(2)}, u32[]{:S(2)}) collective-permute-start(bf16[128,256]{1,0:T(8,128)(2,1)S(1)} %get-tuple-element.39), channel_id=1, source_target_pairs={{0,8},{1,9},{2,10},{3,11},{4,12},{5,13},{6,14},{7,15},{8,0},{9,1},... | collective-permute-start | bytes 196616 | tf_op jit(solution)/shard_map/ppermute | solution.py:267
  20.8 1.5 %collective-permute-start.4 = (f32[2,2,32,128]{3,2,1,0:T(8,128)S(1)}, f32[2,2,32,128]{3,2,1,0:T(8,128)S(1)}, u32[]{:S(2)}, u32[]{:S(2)}) collective-permute-start(f32[2,2,32,128]{3,2,1,0:T(8,128)S(1)} %get-tuple-element.27), channel_id=1, source_target_pairs={{0,8},{1,9},{2,10},{3,11},{4,12},{5,13},{6,14},{7,15},{8,0},{9,1},... | collective-permute-start | bytes 196616 | tf_op jit(solution)/shard_map/ppermute | solution.py:267
  20.9 6.8 %collective-permute-start.9 = (bf16[2,128,256]{2,1,0:T(8,128)(2,1)S(1)}, bf16[2,128,256]{2,1,0:T(8,128)(2,1)S(1)}, u32[]{:S(2)}, u32[]{:S(2)}) collective-permute-start(bf16[2,128,256]{2,1,0:T(8,128)(2,1)S(1)} %maximum_select_fusion.refs_0_), channel_id=1, source_target_pairs={{0,1},{1,0},{2,3},{3,2},{4,5},{5,4},{6,7},{7,6},{8,24},{9,25},{10,... | collective-permute-start | bytes 393224 | tf_op jit(solution)/shard_map/ppermute | solution.py:255
  22.4 6.5 %collective-permute-start.5 = (bf16[2,2,32,128]{3,2,1,0:T(8,128)(2,1)S(1)}, bf16[2,2,32,128]{3,2,1,0:T(8,128)(2,1)S(1)}, u32[]{:S(2)}, u32[]{:S(2)}) collective-permute-start(bf16[2,2,32,128]{3,2,1,0:T(8,128)(2,1)S(1)} %add_convert_fusion.refs_0_), channel_id=1, source_target_pairs={{0,2},{1,3},{2,0},{3,1},{4,6},{5,7},{6,4},{7,5},{8,10},{9,11},{10,... | collective-permute-start | bytes 98312 | tf_op jit(solution)/shard_map/ppermute | solution.py:267
  23.0 5.9 %collective-permute-start.6 = (bf16[2,2,32,128]{3,2,1,0:T(8,128)(2,1)S(1)}, bf16[2,2,32,128]{3,2,1,0:T(8,128)(2,1)S(1)}, u32[]{:S(2)}, u32[]{:S(2)}) collective-permute-start(bf16[2,2,32,128]{3,2,1,0:T(8,128)(2,1)S(1)} %add_convert_fusion.refs_0_), channel_id=1, source_target_pairs={{0,4},{1,5},{2,6},{3,7},{4,0},{5,1},{6,2},{7,3},{8,12},{9,13},{10,... | collective-permute-start | bytes 98312 | tf_op jit(solution)/shard_map/ppermute | solution.py:267
  25.3 5.7 %collective-permute-start.7 = (bf16[2,2,32,128]{3,2,1,0:T(8,128)(2,1)S(1)}, bf16[2,2,32,128]{3,2,1,0:T(8,128)(2,1)S(1)}, u32[]{:S(2)}, u32[]{:S(2)}) collective-permute-start(bf16[2,2,32,128]{3,2,1,0:T(8,128)(2,1)S(1)} %add_convert_fusion.refs_0_), channel_id=1, source_target_pairs={{0,6},{1,7},{2,4},{3,5},{4,2},{5,3},{6,0},{7,1},{8,14},{9,15},{10,... | collective-permute-start | bytes 98312 | tf_op jit(solution)/shard_map/ppermute | solution.py:267
  26.9 5.0 %collective-permute-start.10 = (bf16[2,128,256]{2,1,0:T(8,128)(2,1)S(1)}, bf16[2,128,256]{2,1,0:T(8,128)(2,1)S(1)}, u32[]{:S(2)}, u32[]{:S(2)}) collective-permute-start(bf16[2,128,256]{2,1,0:T(8,128)(2,1)S(1)} %maximum_select_fusion.refs_0_), channel_id=1, source_target_pairs={{0,16},{1,17},{2,18},{3,19},{4,20},{5,21},{6,22},{7,23},{8,9},{9,8... | collective-permute-start | bytes 393224 | tf_op jit(solution)/shard_map/ppermute | solution.py:255
  27.7 5.6 %collective-permute-start.11 = (bf16[2,128,256]{2,1,0:T(8,128)(2,1)S(1)}, bf16[2,128,256]{2,1,0:T(8,128)(2,1)S(1)}, u32[]{:S(2)}, u32[]{:S(2)}) collective-permute-start(bf16[2,128,256]{2,1,0:T(8,128)(2,1)S(1)} %collective-permute-done.9.refs_1_), channel_id=1, source_target_pairs={{0,16},{1,17},{2,18},{3,19},{4,20},{5,21},{6,22},{7,23},{8,9},{9,8... | collective-permute-start | bytes 393224 | tf_op jit(solution)/shard_map/ppermute | solution.py:255
  31.7 1.5 %collective-permute-start.8 = (f32[2,4,32,128]{3,2,1,0:T(8,128)S(1)}, f32[2,4,32,128]{3,2,1,0:T(8,128)S(1)}, u32[]{:S(2)}, u32[]{:S(2)}) collective-permute-start(f32[2,4,32,128]{3,2,1,0:T(8,128)S(1)} %shard_map.62.ours_ref), channel_id=1, source_target_pairs={{0,8},{1,9},{2,10},{3,11},{4,12},{5,13},{6,14},{7,15},{8,0},{9,1},... | collective-permute-start | bytes 393224 | tf_op jit(solution)/shard_map/ppermute | solution.py:267
  33.5 5.3 %collective-permute-start.13 = (f32[32,256]{1,0:T(8,128)S(1)}, f32[32,256]{1,0:T(8,128)S(1)}, u32[]{:S(2)}, u32[]{:S(2)}) collective-permute-start(f32[32,256]{1,0:T(8,128)S(1)} %get-tuple-element.29), channel_id=1, source_target_pairs={{0,4},{1,5},{2,6},{3,7},{4,0},{5,1},{6,2},{7,3},{8,12},{9,13},{10,... | collective-permute-start | bytes 98312 | tf_op jit(solution)/shard_map/ppermute | solution.py:267
  34.1 5.8 %collective-permute-start.14 = (f32[32,256]{1,0:T(8,128)S(1)}, f32[32,256]{1,0:T(8,128)S(1)}, u32[]{:S(2)}, u32[]{:S(2)}) collective-permute-start(f32[32,256]{1,0:T(8,128)S(1)} %get-tuple-element.29), channel_id=1, source_target_pairs={{0,6},{1,7},{2,4},{3,5},{4,2},{5,3},{6,0},{7,1},{8,14},{9,15},{10,... | collective-permute-start | bytes 98312 | tf_op jit(solution)/shard_map/ppermute | solution.py:267
  35.9 4.3 %collective-permute-start.12 = (f32[32,256]{1,0:T(8,128)S(1)}, f32[32,256]{1,0:T(8,128)S(1)}, u32[]{:S(2)}, u32[]{:S(2)}) collective-permute-start(f32[32,256]{1,0:T(8,128)S(1)} %get-tuple-element.29), channel_id=1, source_target_pairs={{0,2},{1,3},{2,0},{3,1},{4,6},{5,7},{6,4},{7,5},{8,10},{9,11},{10,... | collective-permute-start | bytes 98312 | tf_op jit(solution)/shard_map/ppermute | solution.py:267
  40.5 1.4 %collective-permute-start.16 = (f32[2,2,32,128]{3,2,1,0:T(8,128)S(1)}, f32[2,2,32,128]{3,2,1,0:T(8,128)S(1)}, u32[]{:S(2)}, u32[]{:S(2)}) collective-permute-start(f32[2,2,32,128]{3,2,1,0:T(8,128)S(1)} %get-tuple-element.32), channel_id=1, source_target_pairs={{0,8},{1,9},{2,10},{3,11},{4,12},{5,13},{6,14},{7,15},{8,0},{9,1},... | collective-permute-start | bytes 196616 | tf_op jit(solution)/shard_map/ppermute | solution.py:267
  40.5 1.4 %collective-permute-start.15 = (f32[32,256]{1,0:T(8,128)S(1)}, f32[32,256]{1,0:T(8,128)S(1)}, u32[]{:S(2)}, u32[]{:S(2)}) collective-permute-start(f32[32,256]{1,0:T(8,128)S(1)} %add_add_fusion.coeffs_ref.mine_ref), channel_id=1, source_target_pairs={{0,8},{1,9},{2,10},{3,11},{4,12},{5,13},{6,14},{7,15},{8,0},{9,1},... | collective-permute-start | bytes 98312 | tf_op jit(solution)/shard_map/ppermute | solution.py:267
  42.7 11.2 %all-to-all-start.1 = ((f32[32,4,128]{2,1,0:T(4,128)}), f32[32,4,128]{2,1,0:T(4,128)S(1)}, u32[]{:S(2)}, u32[]{:S(2)}) async-start(f32[32,4,128]{2,1,0:T(4,128)} %get-tuple-element.33), calls=%async_computation.1 | async-start | bytes 131072 | tf_op jit(solution)/shard_map/all_to_all | solution.py:384
  45.9 6.6 %collective-permute-start.17 = (f32[32,640]{1,0:T(8,128)S(1)}, f32[32,640]{1,0:T(8,128)S(1)}, u32[]{:S(2)}, u32[]{:S(2)}) collective-permute-start(f32[32,640]{1,0:T(8,128)S(1)} %get-tuple-element.34), channel_id=1, source_target_pairs={{0,17},{1,16},{2,19},{3,18},{4,21},{5,20},{6,23},{7,22},{8,25},{9,... | collective-permute-start | bytes 245768 | tf_op jit(solution)/shard_map/ppermute | solution.py:255
  48.7 5.2 %collective-permute-start.18 = (f32[32,640]{1,0:T(8,128)S(1)}, f32[32,640]{1,0:T(8,128)S(1)}, u32[]{:S(2)}, u32[]{:S(2)}) collective-permute-start(f32[32,640]{1,0:T(8,128)S(1)} %get-tuple-element.35), channel_id=1, source_target_pairs={{0,16},{1,17},{2,18},{3,19},{4,20},{5,21},{6,22},{7,23},{8,9},{9,8... | collective-permute-start | bytes 245768 | tf_op jit(solution)/shard_map/ppermute | solution.py:255
  49.2 4.7 %collective-permute-start.19 = (f32[32,640]{1,0:T(8,128)S(1)}, f32[32,640]{1,0:T(8,128)S(1)}, u32[]{:S(2)}, u32[]{:S(2)}) collective-permute-start(f32[32,640]{1,0:T(8,128)S(1)} %get-tuple-element.36), channel_id=1, source_target_pairs={{0,1},{1,0},{2,3},{3,2},{4,5},{5,4},{6,7},{7,6},{8,24},{9,25},{10,... | collective-permute-start | bytes 245768 | tf_op jit(solution)/shard_map/ppermute | solution.py:255

commit v6 on v5

--- a/solution.py
+++ b/solution.py
@@ -93,15 +93,14 @@
         q, u = place(near[i], core)
 
         def row(p):
-            total = None
+            picked, kept = [], []
             for s in range(slots):
                 start = (p * slots + s) * order
                 if not isinstance(start, int):
                     start = pl.multiple_of(start, order)
-                picked = segment(block ^ q, columns_ref[i, p * slots + s, 0])
-                term = nt(picked, tile_ref[pl.ds(start, order), :])
-                total = term if total is None else total + term
-            sums_ref[u, p] += total
+                picked.append(segment(block ^ q, columns_ref[i, p * slots + s, 0]))
+                kept.append(tile_ref[pl.ds(start, order), :])
+            sums_ref[u, p] += nt(jnp.concatenate(picked, axis=1), jnp.concatenate(kept, axis=1))
 
         each(groups, row)
 

time: 55.1 us -> 55.1 us (level)
  transfers between devices with their start and end apart: 22 -> 22, of which waited for: 10 -> 11; matrix products, arithmetic and copies ran while one was open for 0% -> 0% of each run, Pallas kernels for 4% -> 3%
where the time goes in v6:
time: 55.1 us; the launch traced here: 54.8 us
  starting transfers between devices  30.7 us (56%)
  waiting for transfers between devices  18.3 us (33%)
  Pallas kernels  4.25 us (8%)
  between operations  0.78 us (1%)
  local copies, waits for them, and re-layouts  0.77 us (1%)
    ppermute x9, starting transfers between devices, crossed(): return lax.ppermute(value, BOTH, pairs)  13.6 us
    ppermute x11, starting transfers between devices, swapped(): return lax.ppermute(value, BOTH, pairs)  8.77 us
    ppermute x11, waiting for transfers between devices, swapped(): return lax.ppermute(value, BOTH, pairs)  7.66 us
    ppermute x9, waiting for transfers between devices, crossed(): return lax.ppermute(value, BOTH, pairs)  5.94 us
    all_to_all x1, starting transfers between devices, per_device(): lax.all_to_all(parts.reshape(n_block * n_col, tall, order), BOTH, 0, 0, a...  5.11 us
    all_to_all x1, waiting for transfers between devices, per_device(): lax.all_to_all(parts.reshape(n_block * n_col, tall, order), BOTH, 0, 0, a...  4.7 us
    pallas_call x8, Pallas kernels, call(): pl.pallas_call(kernel, out_shape=out, in_specs=[VMEM] * len(args), out_sp...  4.25 us
    all_to_all x1, starting transfers between devices, per_device(): squares = lax.all_to_all(squares, BOTH, 0, 0)  3.17 us
  transfers between devices with their start and end apart: 22, of which 11 were waited for; matrix products, arithmetic and copies ran while one was open for 0% of the time, Pallas kernels for 3%

profile of v6, /device:TPU:0, one launch (start us, length us, event | category | flops | bytes accessed | tf_op | source)
XLA Modules:
  0.0 54.8 jit_solution(3602846025949325962)
XLA Ops:
  0.6 3.0 %collective-permute-start = (bf16[1024,128]{1,0:T(8,128)(2,1)}, bf16[1024,128]{1,0:T(8,128)(2,1)S(1)}, u32[]{:S(2)}, u32[]{:S(2)}) collective-permute-start(bf16[1024,128]{1,0:T(8,128)(2,1)} %bitcast.11), channel_id=1, source_target_pairs={{0,1},{1,0},{2,3},{3,2},{4,5},{5,4},{6,7},{7,6},{8,24},{9,25},{10,... | collective-permute-start | bytes 786440 | tf_op jit(solution)/shard_map/ppermute | solution.py:254
  3.6 1.5 %collective-permute-start.1 = (bf16[1024,128]{1,0:T(8,128)(2,1)}, bf16[1024,128]{1,0:T(8,128)(2,1)S(1)}, u32[]{:S(2)}, u32[]{:S(2)}) collective-permute-start(bf16[1024,128]{1,0:T(8,128)(2,1)} %bitcast.12), channel_id=1, source_target_pairs={{0,16},{1,17},{2,18},{3,19},{4,20},{5,21},{6,22},{7,23},{8,9},{9,8... | collective-permute-start | bytes 786440 | tf_op jit(solution)/shard_map/ppermute | solution.py:254
  5.2 0.8 %copy-done.1 = bf16[128,128]{1,0:T(8,128)(2,1)S(1)} copy-done((bf16[128,128]{1,0:T(8,128)(2,1)S(1)}, bf16[128,128]{1,0:T(8,128)(2,1)}, u32[]{:S(2)}) %copy-start.1) | copy-done | bytes 32792
  5.9 0.8 %shard_map.59 = bf16[2,8,48,128]{3,2,1,0:T(8,128)(2,1)} custom-call(s32[2,4]{1,0:T(2,128)S(1)} %bitcast.15, bf16[128,128]{1,0:T(8,128)(2,1)S(1)} %copy-done.1), custom_call_target="tpu_custom_call" | custom-call | tf_op jit(solution)/shard_map/pallas_call | solution.py:25
  6.7 5.1 %all-to-all-start = ((bf16[16,48,128]{2,1,0:T(8,128)(2,1)}), bf16[16,48,128]{2,1,0:T(8,128)(2,1)S(1)}, u32[]{:S(2)}, u32[]{:S(2)}) async-start(bf16[16,48,128]{2,1,0:T(8,128)(2,1)} %bitcast.2), calls=%async_computation | async-start | bytes 393216 | tf_op jit(solution)/shard_map/all_to_all | solution.py:305
  11.9 2.0 %collective-permute-start.3 = (bf16[1024,128]{1,0:T(8,128)(2,1)S(1)}, bf16[1024,128]{1,0:T(8,128)(2,1)S(1)}, u32[]{:S(2)}, u32[]{:S(2)}) collective-permute-start(bf16[1024,128]{1,0:T(8,128)(2,1)S(1)} %collective-permute-done.refs_1_.refs_5_), channel_id=1, source_target_pairs={{0,16},{1,17},{2,18},{3,19},{4,20},{5,21},{6,22},{7,23},{8,9},{9,8... | collective-permute-start | bytes 786440 | tf_op jit(solution)/shard_map/ppermute | solution.py:254
  14.0 1.2 %collective-permute-done.2 = bf16[128,256]{1,0:T(8,128)(2,1)S(1)} collective-permute-done((bf16[128,256]{1,0:T(8,128)(2,1)S(1)}, bf16[128,256]{1,0:T(8,128)(2,1)S(1)}, u32[]{:S(2)}, u32[]{:S(2)}) %collective-permute-start.2) | collective-permute-done | bytes 65568 | tf_op jit(solution)/shard_map/ppermute | solution.py:266
  15.2 4.7 %all-to-all-done = bf16[16,48,128]{2,1,0:T(8,128)(2,1)S(1)} async-done(((bf16[16,48,128]{2,1,0:T(8,128)(2,1)}), bf16[16,48,128]{2,1,0:T(8,128)(2,1)S(1)}, u32[]{:S(2)}, u32[]{:S(2)}) %all-to-all-start) | async-done | bytes 196640 | tf_op jit(solution)/shard_map/all_to_all | solution.py:305
  19.9 0.5 shard_map.60
  20.7 1.5 %collective-permute-start.9 = (bf16[2,128,256]{2,1,0:T(8,128)(2,1)S(1)}, bf16[2,128,256]{2,1,0:T(8,128)(2,1)S(1)}, u32[]{:S(2)}, u32[]{:S(2)}) collective-permute-start(bf16[2,128,256]{2,1,0:T(8,128)(2,1)S(1)} %maximum_select_fusion.refs_0_), channel_id=1, source_target_pairs={{0,1},{1,0},{2,3},{3,2},{4,5},{5,4},{6,7},{7,6},{8,24},{9,25},{10,... | collective-permute-start | bytes 393224 | tf_op jit(solution)/shard_map/ppermute | solution.py:254
  22.2 0.8 %collective-permute-start.5 = (bf16[2,2,32,128]{3,2,1,0:T(8,128)(2,1)S(1)}, bf16[2,2,32,128]{3,2,1,0:T(8,128)(2,1)S(1)}, u32[]{:S(2)}, u32[]{:S(2)}) collective-permute-start(bf16[2,2,32,128]{3,2,1,0:T(8,128)(2,1)S(1)} %add_convert_fusion.refs_0_), channel_id=1, source_target_pairs={{0,2},{1,3},{2,0},{3,1},{4,6},{5,7},{6,4},{7,5},{8,10},{9,11},{10,... | collective-permute-start | bytes 98312 | tf_op jit(solution)/shard_map/ppermute | solution.py:266
  23.0 2.3 %collective-permute-start.6 = (bf16[2,2,32,128]{3,2,1,0:T(8,128)(2,1)S(1)}, bf16[2,2,32,128]{3,2,1,0:T(8,128)(2,1)S(1)}, u32[]{:S(2)}, u32[]{:S(2)}) collective-permute-start(bf16[2,2,32,128]{3,2,1,0:T(8,128)(2,1)S(1)} %add_convert_fusion.refs_0_), channel_id=1, source_target_pairs={{0,4},{1,5},{2,6},{3,7},{4,0},{5,1},{6,2},{7,3},{8,12},{9,13},{10,... | collective-permute-start | bytes 98312 | tf_op jit(solution)/shard_map/ppermute | solution.py:266
  25.3 1.4 %collective-permute-start.7 = (bf16[2,2,32,128]{3,2,1,0:T(8,128)(2,1)S(1)}, bf16[2,2,32,128]{3,2,1,0:T(8,128)(2,1)S(1)}, u32[]{:S(2)}, u32[]{:S(2)}) collective-permute-start(bf16[2,2,32,128]{3,2,1,0:T(8,128)(2,1)S(1)} %add_convert_fusion.refs_0_), channel_id=1, source_target_pairs={{0,6},{1,7},{2,4},{3,5},{4,2},{5,3},{6,0},{7,1},{8,14},{9,15},{10,... | collective-permute-start | bytes 98312 | tf_op jit(solution)/shard_map/ppermute | solution.py:266
  26.7 0.8 %collective-permute-start.10 = (bf16[2,128,256]{2,1,0:T(8,128)(2,1)S(1)}, bf16[2,128,256]{2,1,0:T(8,128)(2,1)S(1)}, u32[]{:S(2)}, u32[]{:S(2)}) collective-permute-start(bf16[2,128,256]{2,1,0:T(8,128)(2,1)S(1)} %maximum_select_fusion.refs_0_), channel_id=1, source_target_pairs={{0,16},{1,17},{2,18},{3,19},{4,20},{5,21},{6,22},{7,23},{8,9},{9,8... | collective-permute-start | bytes 393224 | tf_op jit(solution)/shard_map/ppermute | solution.py:254
  27.5 1.2 %collective-permute-start.11 = (bf16[2,128,256]{2,1,0:T(8,128)(2,1)S(1)}, bf16[2,128,256]{2,1,0:T(8,128)(2,1)S(1)}, u32[]{:S(2)}, u32[]{:S(2)}) collective-permute-start(bf16[2,128,256]{2,1,0:T(8,128)(2,1)S(1)} %collective-permute-done.9.refs_1_), channel_id=1, source_target_pairs={{0,16},{1,17},{2,18},{3,19},{4,20},{5,21},{6,22},{7,23},{8,9},{9,8... | collective-permute-start | bytes 393224 | tf_op jit(solution)/shard_map/ppermute | solution.py:254
  28.7 2.3 %collective-permute-done.7.refs_3_ = bf16[2,2,32,128]{3,2,1,0:T(8,128)(2,1)S(1)} collective-permute-done((bf16[2,2,32,128]{3,2,1,0:T(8,128)(2,1)S(1)}, bf16[2,2,32,128]{3,2,1,0:T(8,128)(2,1)S(1)}, u32[]{:S(2)}, u32[]{:S(2)}) %collective-permute-start.7) | collective-permute-done | bytes 32800 | tf_op jit(solution)/shard_map/ppermute | solution.py:266
  31.0 0.5 shard_map.62.ours_ref
  31.7 1.4 %collective-permute-done.11.refs_3_ = bf16[2,128,256]{2,1,0:T(8,128)(2,1)S(1)} collective-permute-done((bf16[2,128,256]{2,1,0:T(8,128)(2,1)S(1)}, bf16[2,128,256]{2,1,0:T(8,128)(2,1)S(1)}, u32[]{:S(2)}, u32[]{:S(2)}) %collective-permute-start.11) | collective-permute-done | bytes 131104 | tf_op jit(solution)/shard_map/ppermute | solution.py:254
  33.3 0.8 %collective-permute-start.13 = (f32[32,256]{1,0:T(8,128)S(1)}, f32[32,256]{1,0:T(8,128)S(1)}, u32[]{:S(2)}, u32[]{:S(2)}) collective-permute-start(f32[32,256]{1,0:T(8,128)S(1)} %get-tuple-element.29), channel_id=1, source_target_pairs={{0,4},{1,5},{2,6},{3,7},{4,0},{5,1},{6,2},{7,3},{8,12},{9,13},{10,... | collective-permute-start | bytes 98312 | tf_op jit(solution)/shard_map/ppermute | solution.py:266
  34.1 1.8 %collective-permute-start.14 = (f32[32,256]{1,0:T(8,128)S(1)}, f32[32,256]{1,0:T(8,128)S(1)}, u32[]{:S(2)}, u32[]{:S(2)}) collective-permute-start(f32[32,256]{1,0:T(8,128)S(1)} %get-tuple-element.29), channel_id=1, source_target_pairs={{0,6},{1,7},{2,4},{3,5},{4,2},{5,3},{6,0},{7,1},{8,14},{9,15},{10,... | collective-permute-start | bytes 98312 | tf_op jit(solution)/shard_map/ppermute | solution.py:266
  35.9 1.0 %collective-permute-start.12 = (f32[32,256]{1,0:T(8,128)S(1)}, f32[32,256]{1,0:T(8,128)S(1)}, u32[]{:S(2)}, u32[]{:S(2)}) collective-permute-start(f32[32,256]{1,0:T(8,128)S(1)} %get-tuple-element.29), channel_id=1, source_target_pairs={{0,2},{1,3},{2,0},{3,1},{4,6},{5,7},{6,4},{7,5},{8,10},{9,11},{10,... | collective-permute-start | bytes 98312 | tf_op jit(solution)/shard_map/ppermute | solution.py:266
  36.9 1.7 %collective-permute-done.13 = f32[32,256]{1,0:T(8,128)S(1)} collective-permute-done((f32[32,256]{1,0:T(8,128)S(1)}, f32[32,256]{1,0:T(8,128)S(1)}, u32[]{:S(2)}, u32[]{:S(2)}) %collective-permute-start.13) | collective-permute-done | bytes 32800 | tf_op jit(solution)/shard_map/ppermute | solution.py:266
  38.6 1.4 %collective-permute-done.14 = f32[32,256]{1,0:T(8,128)S(1)} collective-permute-done((f32[32,256]{1,0:T(8,128)S(1)}, f32[32,256]{1,0:T(8,128)S(1)}, u32[]{:S(2)}, u32[]{:S(2)}) %collective-permute-start.14) | collective-permute-done | bytes 32800 | tf_op jit(solution)/shard_map/ppermute | solution.py:266
  40.5 0.5 collective-permute-start.15
  41.0 0.9 %collective-permute-done.15.mate_ref = f32[32,256]{1,0:T(8,128)S(1)} collective-permute-done((f32[32,256]{1,0:T(8,128)S(1)}, f32[32,256]{1,0:T(8,128)S(1)}, u32[]{:S(2)}, u32[]{:S(2)}) %collective-permute-start.15) | collective-permute-done | bytes 32800 | tf_op jit(solution)/shard_map/ppermute | solution.py:266
  41.9 0.9 %shard_map.65 = (f32[32,640]{1,0:T(8,128)S(1)}, f32[32,640]{1,0:T(8,128)S(1)}, f32[32,640]{1,0:T(8,128)S(1)}, f32[32,640]{1,0:T(8,128)S(1)}, f32[32,4,128]{2,1,0:T(4,128)}) custom-call(f32[32,256]{1,0:T(8,128)S(1)} %add_add_fusion.coeffs_ref.mine_ref, f32[32,256]{1,0:T(8,128)S(1)} %collective-permute-done.15.mate_ref, ...), custom_call_target="tpu_custom_call" | custom-call | tf_op jit(solution)/shard_map/pallas_call | solution.py:25
  42.7 3.2 %all-to-all-start.1 = ((f32[32,4,128]{2,1,0:T(4,128)}), f32[32,4,128]{2,1,0:T(4,128)S(1)}, u32[]{:S(2)}, u32[]{:S(2)}) async-start(f32[32,4,128]{2,1,0:T(4,128)} %get-tuple-element.33), calls=%async_computation.1 | async-start | bytes 131072 | tf_op jit(solution)/shard_map/all_to_all | solution.py:383
  45.9 2.7 %collective-permute-start.17 = (f32[32,640]{1,0:T(8,128)S(1)}, f32[32,640]{1,0:T(8,128)S(1)}, u32[]{:S(2)}, u32[]{:S(2)}) collective-permute-start(f32[32,640]{1,0:T(8,128)S(1)} %get-tuple-element.34), channel_id=1, source_target_pairs={{0,17},{1,16},{2,19},{3,18},{4,21},{5,20},{6,23},{7,22},{8,25},{9,... | collective-permute-start | bytes 245768 | tf_op jit(solution)/shard_map/ppermute | solution.py:254
  48.7 0.6 %collective-permute-start.18 = (f32[32,640]{1,0:T(8,128)S(1)}, f32[32,640]{1,0:T(8,128)S(1)}, u32[]{:S(2)}, u32[]{:S(2)}) collective-permute-start(f32[32,640]{1,0:T(8,128)S(1)} %get-tuple-element.35), channel_id=1, source_target_pairs={{0,16},{1,17},{2,18},{3,19},{4,20},{5,21},{6,22},{7,23},{8,9},{9,8... | collective-permute-start | bytes 245768 | tf_op jit(solution)/shard_map/ppermute | solution.py:254
  49.5 3.0 %collective-permute-done.17.refs_0_ = f32[32,640]{1,0:T(8,128)S(1)} collective-permute-done((f32[32,640]{1,0:T(8,128)S(1)}, f32[32,640]{1,0:T(8,128)S(1)}, u32[]{:S(2)}, u32[]{:S(2)}) %collective-permute-start.17) | collective-permute-done | bytes 81952 | tf_op jit(solution)/shard_map/ppermute | solution.py:254
  52.5 1.4 %collective-permute-done.18.refs_1_ = f32[32,640]{1,0:T(8,128)S(1)} collective-permute-done((f32[32,640]{1,0:T(8,128)S(1)}, f32[32,640]{1,0:T(8,128)S(1)}, u32[]{:S(2)}, u32[]{:S(2)}) %collective-permute-start.18) | collective-permute-done | bytes 81952 | tf_op jit(solution)/shard_map/ppermute | solution.py:254
  53.9 0.9 %shard_map.66 = (f32[128,128]{1,0:T(8,128)}, f32[512,128]{1,0:T(8,128)}) custom-call(f32[32,4,128]{2,1,0:T(4,128)S(1)} %all-to-all-done.1.squares_ref, f32[32,640]{1,0:T(8,128)S(1)} %collective-permute-done.17.refs_0_, f32[32,640]{1,0:T(8,128)S(1)} %collective-permute-done.18.refs_1_, f32[32,640]{1,0:T(8,128)S(1)} %collective-permute-done.19.refs_2_, ...), custom_call_target="tpu_custom_call" | custom-call | tf_op jit(solution)/shard_map/pallas_call | solution.py:25
  (32 shorter events, 1.7 us)
Async XLA Ops:
  0.6 4.5 %copy-start.2 = (s32[1,4,1,2]{1,3,2,0:T(2,128)S(1)}, s32[1,4,1,2]{1,3,2,0:T(2,128)}, u32[]{:S(2)}) copy-start(s32[1,4,1,2]{1,3,2,0:T(2,128)} %param.6) | copy-start | bytes 100
  0.6 11.2 %collective-permute-start = (bf16[1024,128]{1,0:T(8,128)(2,1)}, bf16[1024,128]{1,0:T(8,128)(2,1)S(1)}, u32[]{:S(2)}, u32[]{:S(2)}) collective-permute-start(bf16[1024,128]{1,0:T(8,128)(2,1)} %bitcast.11), channel_id=1, source_target_pairs={{0,1},{1,0},{2,3},{3,2},{4,5},{5,4},{6,7},{7,6},{8,24},{9,25},{10,... | collective-permute-start | bytes 786440 | tf_op jit(solution)/shard_map/ppermute | solution.py:254
  3.6 8.2 %collective-permute-start.1 = (bf16[1024,128]{1,0:T(8,128)(2,1)}, bf16[1024,128]{1,0:T(8,128)(2,1)S(1)}, u32[]{:S(2)}, u32[]{:S(2)}) collective-permute-start(bf16[1024,128]{1,0:T(8,128)(2,1)} %bitcast.12), channel_id=1, source_target_pairs={{0,16},{1,17},{2,18},{3,19},{4,20},{5,21},{6,22},{7,23},{8,9},{9,8... | collective-permute-start | bytes 786440 | tf_op jit(solution)/shard_map/ppermute | solution.py:254
  5.2 0.8 %copy-start.1 = (bf16[128,128]{1,0:T(8,128)(2,1)S(1)}, bf16[128,128]{1,0:T(8,128)(2,1)}, u32[]{:S(2)}) copy-start(bf16[128,128]{1,0:T(8,128)(2,1)} %start_ref.1) | copy-start | bytes 98308
  6.7 7.1 %copy-start.3 = (bf16[128,512]{1,0:T(8,128)(2,1)S(1)}, bf16[128,512]{1,0:T(8,128)(2,1)}, u32[]{:S(2)}) copy-start(bf16[128,512]{1,0:T(8,128)(2,1)} %param.7) | copy-start | bytes 393220
  6.7 13.2 %all-to-all-start = ((bf16[16,48,128]{2,1,0:T(8,128)(2,1)}), bf16[16,48,128]{2,1,0:T(8,128)(2,1)S(1)}, u32[]{:S(2)}, u32[]{:S(2)}) async-start(bf16[16,48,128]{2,1,0:T(8,128)(2,1)} %bitcast.2), calls=%async_computation | async-start | bytes 393216 | tf_op jit(solution)/shard_map/all_to_all | solution.py:305
  11.9 8.1 %copy-start = (bf16[1,4,1,2,128,128]{5,4,3,2,1,0:T(8,128)(2,1)S(1)}, bf16[1,4,1,2,128,128]{5,4,3,2,1,0:T(8,128)(2,1)}, u32[]{:S(2)}) copy-start(bf16[1,4,1,2,128,128]{5,4,3,2,1,0:T(8,128)(2,1)} %param.5) | copy-start | bytes 786436
  11.9 8.5 %collective-permute-start.3 = (bf16[1024,128]{1,0:T(8,128)(2,1)S(1)}, bf16[1024,128]{1,0:T(8,128)(2,1)S(1)}, u32[]{:S(2)}, u32[]{:S(2)}) collective-permute-start(bf16[1024,128]{1,0:T(8,128)(2,1)S(1)} %collective-permute-done.refs_1_.refs_5_), channel_id=1, source_target_pairs={{0,16},{1,17},{2,18},{3,19},{4,20},{5,21},{6,22},{7,23},{8,9},{9,8... | collective-permute-start | bytes 786440 | tf_op jit(solution)/shard_map/ppermute | solution.py:254
  13.9 1.3 %collective-permute-start.2 = (bf16[128,256]{1,0:T(8,128)(2,1)S(1)}, bf16[128,256]{1,0:T(8,128)(2,1)S(1)}, u32[]{:S(2)}, u32[]{:S(2)}) collective-permute-start(bf16[128,256]{1,0:T(8,128)(2,1)S(1)} %get-tuple-element.39), channel_id=1, source_target_pairs={{0,8},{1,9},{2,10},{3,11},{4,12},{5,13},{6,14},{7,15},{8,0},{9,1},... | collective-permute-start | bytes 196616 | tf_op jit(solution)/shard_map/ppermute | solution.py:266
  20.6 1.6 %collective-permute-start.4 = (f32[2,2,32,128]{3,2,1,0:T(8,128)S(1)}, f32[2,2,32,128]{3,2,1,0:T(8,128)S(1)}, u32[]{:S(2)}, u32[]{:S(2)}) collective-permute-start(f32[2,2,32,128]{3,2,1,0:T(8,128)S(1)} %get-tuple-element.27), channel_id=1, source_target_pairs={{0,8},{1,9},{2,10},{3,11},{4,12},{5,13},{6,14},{7,15},{8,0},{9,1},... | collective-permute-start | bytes 196616 | tf_op jit(solution)/shard_map/ppermute | solution.py:266
  20.7 6.8 %collective-permute-start.9 = (bf16[2,128,256]{2,1,0:T(8,128)(2,1)S(1)}, bf16[2,128,256]{2,1,0:T(8,128)(2,1)S(1)}, u32[]{:S(2)}, u32[]{:S(2)}) collective-permute-start(bf16[2,128,256]{2,1,0:T(8,128)(2,1)S(1)} %maximum_select_fusion.refs_0_), channel_id=1, source_target_pairs={{0,1},{1,0},{2,3},{3,2},{4,5},{5,4},{6,7},{7,6},{8,24},{9,25},{10,... | collective-permute-start | bytes 393224 | tf_op jit(solution)/shard_map/ppermute | solution.py:254
  22.2 6.5 %collective-permute-start.5 = (bf16[2,2,32,128]{3,2,1,0:T(8,128)(2,1)S(1)}, bf16[2,2,32,128]{3,2,1,0:T(8,128)(2,1)S(1)}, u32[]{:S(2)}, u32[]{:S(2)}) collective-permute-start(bf16[2,2,32,128]{3,2,1,0:T(8,128)(2,1)S(1)} %add_convert_fusion.refs_0_), channel_id=1, source_target_pairs={{0,2},{1,3},{2,0},{3,1},{4,6},{5,7},{6,4},{7,5},{8,10},{9,11},{10,... | collective-permute-start | bytes 98312 | tf_op jit(solution)/shard_map/ppermute | solution.py:266
  23.0 5.7 %collective-permute-start.6 = (bf16[2,2,32,128]{3,2,1,0:T(8,128)(2,1)S(1)}, bf16[2,2,32,128]{3,2,1,0:T(8,128)(2,1)S(1)}, u32[]{:S(2)}, u32[]{:S(2)}) collective-permute-start(bf16[2,2,32,128]{3,2,1,0:T(8,128)(2,1)S(1)} %add_convert_fusion.refs_0_), channel_id=1, source_target_pairs={{0,4},{1,5},{2,6},{3,7},{4,0},{5,1},{6,2},{7,3},{8,12},{9,13},{10,... | collective-permute-start | bytes 98312 | tf_op jit(solution)/shard_map/ppermute | solution.py:266
  25.3 5.7 %collective-permute-start.7 = (bf16[2,2,32,128]{3,2,1,0:T(8,128)(2,1)S(1)}, bf16[2,2,32,128]{3,2,1,0:T(8,128)(2,1)S(1)}, u32[]{:S(2)}, u32[]{:S(2)}) collective-permute-start(bf16[2,2,32,128]{3,2,1,0:T(8,128)(2,1)S(1)} %add_convert_fusion.refs_0_), channel_id=1, source_target_pairs={{0,6},{1,7},{2,4},{3,5},{4,2},{5,3},{6,0},{7,1},{8,14},{9,15},{10,... | collective-permute-start | bytes 98312 | tf_op jit(solution)/shard_map/ppermute | solution.py:266
  26.7 5.0 %collective-permute-start.10 = (bf16[2,128,256]{2,1,0:T(8,128)(2,1)S(1)}, bf16[2,128,256]{2,1,0:T(8,128)(2,1)S(1)}, u32[]{:S(2)}, u32[]{:S(2)}) collective-permute-start(bf16[2,128,256]{2,1,0:T(8,128)(2,1)S(1)} %maximum_select_fusion.refs_0_), channel_id=1, source_target_pairs={{0,16},{1,17},{2,18},{3,19},{4,20},{5,21},{6,22},{7,23},{8,9},{9,8... | collective-permute-start | bytes 393224 | tf_op jit(solution)/shard_map/ppermute | solution.py:254
  27.5 5.6 %collective-permute-start.11 = (bf16[2,128,256]{2,1,0:T(8,128)(2,1)S(1)}, bf16[2,128,256]{2,1,0:T(8,128)(2,1)S(1)}, u32[]{:S(2)}, u32[]{:S(2)}) collective-permute-start(bf16[2,128,256]{2,1,0:T(8,128)(2,1)S(1)} %collective-permute-done.9.refs_1_), channel_id=1, source_target_pairs={{0,16},{1,17},{2,18},{3,19},{4,20},{5,21},{6,22},{7,23},{8,9},{9,8... | collective-permute-start | bytes 393224 | tf_op jit(solution)/shard_map/ppermute | solution.py:254
  31.5 1.6 %collective-permute-start.8 = (f32[2,4,32,128]{3,2,1,0:T(8,128)S(1)}, f32[2,4,32,128]{3,2,1,0:T(8,128)S(1)}, u32[]{:S(2)}, u32[]{:S(2)}) collective-permute-start(f32[2,4,32,128]{3,2,1,0:T(8,128)S(1)} %shard_map.62.ours_ref), channel_id=1, source_target_pairs={{0,8},{1,9},{2,10},{3,11},{4,12},{5,13},{6,14},{7,15},{8,0},{9,1},... | collective-permute-start | bytes 393224 | tf_op jit(solution)/shard_map/ppermute | solution.py:266
  33.3 5.3 %collective-permute-start.13 = (f32[32,256]{1,0:T(8,128)S(1)}, f32[32,256]{1,0:T(8,128)S(1)}, u32[]{:S(2)}, u32[]{:S(2)}) collective-permute-start(f32[32,256]{1,0:T(8,128)S(1)} %get-tuple-element.29), channel_id=1, source_target_pairs={{0,4},{1,5},{2,6},{3,7},{4,0},{5,1},{6,2},{7,3},{8,12},{9,13},{10,... | collective-permute-start | bytes 98312 | tf_op jit(solution)/shard_map/ppermute | solution.py:266
  34.1 5.9 %collective-permute-start.14 = (f32[32,256]{1,0:T(8,128)S(1)}, f32[32,256]{1,0:T(8,128)S(1)}, u32[]{:S(2)}, u32[]{:S(2)}) collective-permute-start(f32[32,256]{1,0:T(8,128)S(1)} %get-tuple-element.29), channel_id=1, source_target_pairs={{0,6},{1,7},{2,4},{3,5},{4,2},{5,3},{6,0},{7,1},{8,14},{9,15},{10,... | collective-permute-start | bytes 98312 | tf_op jit(solution)/shard_map/ppermute | solution.py:266
  35.9 4.3 %collective-permute-start.12 = (f32[32,256]{1,0:T(8,128)S(1)}, f32[32,256]{1,0:T(8,128)S(1)}, u32[]{:S(2)}, u32[]{:S(2)}) collective-permute-start(f32[32,256]{1,0:T(8,128)S(1)} %get-tuple-element.29), channel_id=1, source_target_pairs={{0,2},{1,3},{2,0},{3,1},{4,6},{5,7},{6,4},{7,5},{8,10},{9,11},{10,... | collective-permute-start | bytes 98312 | tf_op jit(solution)/shard_map/ppermute | solution.py:266
  40.5 1.4 %collective-permute-start.16 = (f32[2,2,32,128]{3,2,1,0:T(8,128)S(1)}, f32[2,2,32,128]{3,2,1,0:T(8,128)S(1)}, u32[]{:S(2)}, u32[]{:S(2)}) collective-permute-start(f32[2,2,32,128]{3,2,1,0:T(8,128)S(1)} %get-tuple-element.32), channel_id=1, source_target_pairs={{0,8},{1,9},{2,10},{3,11},{4,12},{5,13},{6,14},{7,15},{8,0},{9,1},... | collective-permute-start | bytes 196616 | tf_op jit(solution)/shard_map/ppermute | solution.py:266
  40.5 1.4 %collective-permute-start.15 = (f32[32,256]{1,0:T(8,128)S(1)}, f32[32,256]{1,0:T(8,128)S(1)}, u32[]{:S(2)}, u32[]{:S(2)}) collective-permute-start(f32[32,256]{1,0:T(8,128)S(1)} %add_add_fusion.coeffs_ref.mine_ref), channel_id=1, source_target_pairs={{0,8},{1,9},{2,10},{3,11},{4,12},{5,13},{6,14},{7,15},{8,0},{9,1},... | collective-permute-start | bytes 98312 | tf_op jit(solution)/shard_map/ppermute | solution.py:266
  42.7 11.2 %all-to-all-start.1 = ((f32[32,4,128]{2,1,0:T(4,128)}), f32[32,4,128]{2,1,0:T(4,128)S(1)}, u32[]{:S(2)}, u32[]{:S(2)}) async-start(f32[32,4,128]{2,1,0:T(4,128)} %get-tuple-element.33), calls=%async_computation.1 | async-start | bytes 131072 | tf_op jit(solution)/shard_map/all_to_all | solution.py:383
  45.9 6.6 %collective-permute-start.17 = (f32[32,640]{1,0:T(8,128)S(1)}, f32[32,640]{1,0:T(8,128)S(1)}, u32[]{:S(2)}, u32[]{:S(2)}) collective-permute-start(f32[32,640]{1,0:T(8,128)S(1)} %get-tuple-element.34), channel_id=1, source_target_pairs={{0,17},{1,16},{2,19},{3,18},{4,21},{5,20},{6,23},{7,22},{8,25},{9,... | collective-permute-start | bytes 245768 | tf_op jit(solution)/shard_map/ppermute | solution.py:254
  48.7 5.2 %collective-permute-start.18 = (f32[32,640]{1,0:T(8,128)S(1)}, f32[32,640]{1,0:T(8,128)S(1)}, u32[]{:S(2)}, u32[]{:S(2)}) collective-permute-start(f32[32,640]{1,0:T(8,128)S(1)} %get-tuple-element.35), channel_id=1, source_target_pairs={{0,16},{1,17},{2,18},{3,19},{4,20},{5,21},{6,22},{7,23},{8,9},{9,8... | collective-permute-start | bytes 245768 | tf_op jit(solution)/shard_map/ppermute | solution.py:254
  49.2 4.7 %collective-permute-start.19 = (f32[32,640]{1,0:T(8,128)S(1)}, f32[32,640]{1,0:T(8,128)S(1)}, u32[]{:S(2)}, u32[]{:S(2)}) collective-permute-start(f32[32,640]{1,0:T(8,128)S(1)} %get-tuple-element.36), channel_id=1, source_target_pairs={{0,1},{1,0},{2,3},{3,2},{4,5},{5,4},{6,7},{7,6},{8,24},{9,25},{10,... | collective-permute-start | bytes 245768 | tf_op jit(solution)/shard_map/ppermute | solution.py:254

commit v7 on v6

--- a/solution.py
+++ b/solution.py
@@ -40,6 +40,10 @@
 def place(entry, core):
     (even_q, even_u), (odd_q, odd_u) = entry
     return jnp.where(core == 0, even_q, odd_q), jnp.where(core == 0, even_u, odd_u)
+
+
+def gray(k):
+    return k ^ (k >> 1)
 
 
 def nt(a, b):
@@ -148,7 +152,7 @@
     if n_vectors > 1:
         all_ref = refs[2]
         for k in range(n_vectors):
-            all_ref[me_z ^ k] = vectors[k][...]
+            all_ref[me_z ^ gray(k)] = vectors[k][...]
     else:
         all_ref = vectors[0]
 
@@ -338,7 +342,7 @@
     own = spread(own, near)
     mine = (keep + mate(give)).astype(BF16)
     if few:
-        vectors = over_members(mine)
+        vectors = [mine] + [swapped(mine, 0, gray(k) * lanes) for k in range(1, members)]
     else:
         alike = [list(range(u, n_col, lanes)) for u in range(lanes)]
         vectors = [
@@ -359,7 +363,7 @@
     )
     if members == 4:
         zero, one, two, three = over_members(coeffs)
-        coeffs = (zero + one) + (two + three)
+        coeffs = (zero + one) + (three + two)
     else:
         step = lanes
         while step < n_col:

time: 55.1 us -> 55 us (level)
  no operation moved by 1% of the time
where the time goes in v7:
time: 55 us; the launch traced here: 54.7 us
  starting transfers between devices  30.6 us (56%)
  waiting for transfers between devices  18.2 us (33%)
  Pallas kernels  4.24 us (8%)
  between operations  0.79 us (1%)
  local copies, waits for them, and re-layouts  0.77 us (1%)
    ppermute x9, starting transfers between devices, crossed(): return lax.ppermute(value, BOTH, pairs)  13.6 us
    ppermute x11, starting transfers between devices, swapped(): return lax.ppermute(value, BOTH, pairs)  8.77 us
    ppermute x11, waiting for transfers between devices, swapped(): return lax.ppermute(value, BOTH, pairs)  7.95 us
    ppermute x9, waiting for transfers between devices, crossed(): return lax.ppermute(value, BOTH, pairs)  5.59 us
    all_to_all x1, starting transfers between devices, per_device(): lax.all_to_all(parts.reshape(n_block * n_col, tall, order), BOTH, 0, 0, a...  5.11 us
    all_to_all x1, waiting for transfers between devices, per_device(): lax.all_to_all(parts.reshape(n_block * n_col, tall, order), BOTH, 0, 0, a...  4.7 us
    pallas_call x8, Pallas kernels, call(): pl.pallas_call(kernel, out_shape=out, in_specs=[VMEM] * len(args), out_sp...  4.24 us
    all_to_all x1, starting transfers between devices, per_device(): squares = lax.all_to_all(squares, BOTH, 0, 0)  3.1 us
  transfers between devices with their start and end apart: 22, of which 11 were waited for; matrix products, arithmetic and copies ran while one was open for 0% of the time, Pallas kernels for 3%

profile of v7, /device:TPU:0, one launch (start us, length us, event | category | flops | bytes accessed | tf_op | source)
XLA Modules:
  0.0 54.7 jit_solution(11678523719124367353)
XLA Ops:
  0.6 3.0 %collective-permute-start = (bf16[1024,128]{1,0:T(8,128)(2,1)}, bf16[1024,128]{1,0:T(8,128)(2,1)S(1)}, u32[]{:S(2)}, u32[]{:S(2)}) collective-permute-start(bf16[1024,128]{1,0:T(8,128)(2,1)} %bitcast.11), channel_id=1, source_target_pairs={{0,1},{1,0},{2,3},{3,2},{4,5},{5,4},{6,7},{7,6},{8,24},{9,25},{10,... | collective-permute-start | bytes 786440 | tf_op jit(solution)/shard_map/ppermute | solution.py:258
  3.6 1.5 %collective-permute-start.1 = (bf16[1024,128]{1,0:T(8,128)(2,1)}, bf16[1024,128]{1,0:T(8,128)(2,1)S(1)}, u32[]{:S(2)}, u32[]{:S(2)}) collective-permute-start(bf16[1024,128]{1,0:T(8,128)(2,1)} %bitcast.12), channel_id=1, source_target_pairs={{0,16},{1,17},{2,18},{3,19},{4,20},{5,21},{6,22},{7,23},{8,9},{9,8... | collective-permute-start | bytes 786440 | tf_op jit(solution)/shard_map/ppermute | solution.py:258
  5.2 0.8 %copy-done.1 = bf16[128,128]{1,0:T(8,128)(2,1)S(1)} copy-done((bf16[128,128]{1,0:T(8,128)(2,1)S(1)}, bf16[128,128]{1,0:T(8,128)(2,1)}, u32[]{:S(2)}) %copy-start.1) | copy-done | bytes 32792
  5.9 0.8 %shard_map.59 = bf16[2,8,48,128]{3,2,1,0:T(8,128)(2,1)} custom-call(s32[2,4]{1,0:T(2,128)S(1)} %bitcast.15, bf16[128,128]{1,0:T(8,128)(2,1)S(1)} %copy-done.1), custom_call_target="tpu_custom_call" | custom-call | tf_op jit(solution)/shard_map/pallas_call | solution.py:25
  6.7 5.1 %all-to-all-start = ((bf16[16,48,128]{2,1,0:T(8,128)(2,1)}), bf16[16,48,128]{2,1,0:T(8,128)(2,1)S(1)}, u32[]{:S(2)}, u32[]{:S(2)}) async-start(bf16[16,48,128]{2,1,0:T(8,128)(2,1)} %bitcast.2), calls=%async_computation | async-start | bytes 393216 | tf_op jit(solution)/shard_map/all_to_all | solution.py:309
  11.9 2.0 %collective-permute-start.3 = (bf16[1024,128]{1,0:T(8,128)(2,1)S(1)}, bf16[1024,128]{1,0:T(8,128)(2,1)S(1)}, u32[]{:S(2)}, u32[]{:S(2)}) collective-permute-start(bf16[1024,128]{1,0:T(8,128)(2,1)S(1)} %collective-permute-done.refs_1_.refs_5_), channel_id=1, source_target_pairs={{0,16},{1,17},{2,18},{3,19},{4,20},{5,21},{6,22},{7,23},{8,9},{9,8... | collective-permute-start | bytes 786440 | tf_op jit(solution)/shard_map/ppermute | solution.py:258
  14.0 1.2 %collective-permute-done.2 = bf16[128,256]{1,0:T(8,128)(2,1)S(1)} collective-permute-done((bf16[128,256]{1,0:T(8,128)(2,1)S(1)}, bf16[128,256]{1,0:T(8,128)(2,1)S(1)}, u32[]{:S(2)}, u32[]{:S(2)}) %collective-permute-start.2) | collective-permute-done | bytes 65568 | tf_op jit(solution)/shard_map/ppermute | solution.py:270
  15.2 4.7 %all-to-all-done = bf16[16,48,128]{2,1,0:T(8,128)(2,1)S(1)} async-done(((bf16[16,48,128]{2,1,0:T(8,128)(2,1)}), bf16[16,48,128]{2,1,0:T(8,128)(2,1)S(1)}, u32[]{:S(2)}, u32[]{:S(2)}) %all-to-all-start) | async-done | bytes 196640 | tf_op jit(solution)/shard_map/all_to_all | solution.py:309
  19.9 0.5 shard_map.60
  20.7 1.5 %collective-permute-start.9 = (bf16[2,128,256]{2,1,0:T(8,128)(2,1)S(1)}, bf16[2,128,256]{2,1,0:T(8,128)(2,1)S(1)}, u32[]{:S(2)}, u32[]{:S(2)}) collective-permute-start(bf16[2,128,256]{2,1,0:T(8,128)(2,1)S(1)} %maximum_select_fusion.refs_0_), channel_id=1, source_target_pairs={{0,1},{1,0},{2,3},{3,2},{4,5},{5,4},{6,7},{7,6},{8,24},{9,25},{10,... | collective-permute-start | bytes 393224 | tf_op jit(solution)/shard_map/ppermute | solution.py:258
  22.2 0.8 %collective-permute-start.5 = (bf16[2,2,32,128]{3,2,1,0:T(8,128)(2,1)S(1)}, bf16[2,2,32,128]{3,2,1,0:T(8,128)(2,1)S(1)}, u32[]{:S(2)}, u32[]{:S(2)}) collective-permute-start(bf16[2,2,32,128]{3,2,1,0:T(8,128)(2,1)S(1)} %add_convert_fusion.refs_0_), channel_id=1, source_target_pairs={{0,2},{1,3},{2,0},{3,1},{4,6},{5,7},{6,4},{7,5},{8,10},{9,11},{10,... | collective-permute-start | bytes 98312 | tf_op jit(solution)/shard_map/ppermute | solution.py:270
  23.0 2.4 %collective-permute-start.6 = (bf16[2,2,32,128]{3,2,1,0:T(8,128)(2,1)S(1)}, bf16[2,2,32,128]{3,2,1,0:T(8,128)(2,1)S(1)}, u32[]{:S(2)}, u32[]{:S(2)}) collective-permute-start(bf16[2,2,32,128]{3,2,1,0:T(8,128)(2,1)S(1)} %add_convert_fusion.refs_0_), channel_id=1, source_target_pairs={{0,6},{1,7},{2,4},{3,5},{4,2},{5,3},{6,0},{7,1},{8,14},{9,15},{10,... | collective-permute-start | bytes 98312 | tf_op jit(solution)/shard_map/ppermute | solution.py:270
  25.8 0.8 %collective-permute-start.10 = (bf16[2,128,256]{2,1,0:T(8,128)(2,1)S(1)}, bf16[2,128,256]{2,1,0:T(8,128)(2,1)S(1)}, u32[]{:S(2)}, u32[]{:S(2)}) collective-permute-start(bf16[2,128,256]{2,1,0:T(8,128)(2,1)S(1)} %maximum_select_fusion.refs_0_), channel_id=1, source_target_pairs={{0,16},{1,17},{2,18},{3,19},{4,20},{5,21},{6,22},{7,23},{8,9},{9,8... | collective-permute-start | bytes 393224 | tf_op jit(solution)/shard_map/ppermute | solution.py:258
  26.6 1.2 %collective-permute-start.11 = (bf16[2,128,256]{2,1,0:T(8,128)(2,1)S(1)}, bf16[2,128,256]{2,1,0:T(8,128)(2,1)S(1)}, u32[]{:S(2)}, u32[]{:S(2)}) collective-permute-start(bf16[2,128,256]{2,1,0:T(8,128)(2,1)S(1)} %collective-permute-done.9.refs_1_), channel_id=1, source_target_pairs={{0,16},{1,17},{2,18},{3,19},{4,20},{5,21},{6,22},{7,23},{8,9},{9,8... | collective-permute-start | bytes 393224 | tf_op jit(solution)/shard_map/ppermute | solution.py:258
  27.8 1.2 %collective-permute-done.6.refs_2_ = bf16[2,2,32,128]{3,2,1,0:T(8,128)(2,1)S(1)} collective-permute-done((bf16[2,2,32,128]{3,2,1,0:T(8,128)(2,1)S(1)}, bf16[2,2,32,128]{3,2,1,0:T(8,128)(2,1)S(1)}, u32[]{:S(2)}, u32[]{:S(2)}) %collective-permute-start.6) | collective-permute-done | bytes 32800 | tf_op jit(solution)/shard_map/ppermute | solution.py:270
  29.0 1.5 %collective-permute-done.7.refs_3_ = bf16[2,2,32,128]{3,2,1,0:T(8,128)(2,1)S(1)} collective-permute-done((bf16[2,2,32,128]{3,2,1,0:T(8,128)(2,1)S(1)}, bf16[2,2,32,128]{3,2,1,0:T(8,128)(2,1)S(1)}, u32[]{:S(2)}, u32[]{:S(2)}) %collective-permute-start.7) | collective-permute-done | bytes 32800 | tf_op jit(solution)/shard_map/ppermute | solution.py:270
  30.4 0.5 shard_map.62.ours_ref
  31.0 1.2 %collective-permute-done.11.refs_3_ = bf16[2,128,256]{2,1,0:T(8,128)(2,1)S(1)} collective-permute-done((bf16[2,128,256]{2,1,0:T(8,128)(2,1)S(1)}, bf16[2,128,256]{2,1,0:T(8,128)(2,1)S(1)}, u32[]{:S(2)}, u32[]{:S(2)}) %collective-permute-start.11) | collective-permute-done | bytes 131104 | tf_op jit(solution)/shard_map/ppermute | solution.py:258
  32.6 2.3 %collective-permute-start.13 = (f32[32,256]{1,0:T(8,128)S(1)}, f32[32,256]{1,0:T(8,128)S(1)}, u32[]{:S(2)}, u32[]{:S(2)}) collective-permute-start(f32[32,256]{1,0:T(8,128)S(1)} %get-tuple-element.29), channel_id=1, source_target_pairs={{0,6},{1,7},{2,4},{3,5},{4,2},{5,3},{6,0},{7,1},{8,14},{9,15},{10,... | collective-permute-start | bytes 98312 | tf_op jit(solution)/shard_map/ppermute | solution.py:270
  34.9 0.7 %collective-permute-start.14 = (f32[32,256]{1,0:T(8,128)S(1)}, f32[32,256]{1,0:T(8,128)S(1)}, u32[]{:S(2)}, u32[]{:S(2)}) collective-permute-start(f32[32,256]{1,0:T(8,128)S(1)} %get-tuple-element.29), channel_id=1, source_target_pairs={{0,4},{1,5},{2,6},{3,7},{4,0},{5,1},{6,2},{7,3},{8,12},{9,13},{10,... | collective-permute-start | bytes 98312 | tf_op jit(solution)/shard_map/ppermute | solution.py:270
  35.6 1.5 %collective-permute-start.12 = (f32[32,256]{1,0:T(8,128)S(1)}, f32[32,256]{1,0:T(8,128)S(1)}, u32[]{:S(2)}, u32[]{:S(2)}) collective-permute-start(f32[32,256]{1,0:T(8,128)S(1)} %get-tuple-element.29), channel_id=1, source_target_pairs={{0,2},{1,3},{2,0},{3,1},{4,6},{5,7},{6,4},{7,5},{8,10},{9,11},{10,... | collective-permute-start | bytes 98312 | tf_op jit(solution)/shard_map/ppermute | solution.py:270
  37.0 1.3 %collective-permute-done.13 = f32[32,256]{1,0:T(8,128)S(1)} collective-permute-done((f32[32,256]{1,0:T(8,128)S(1)}, f32[32,256]{1,0:T(8,128)S(1)}, u32[]{:S(2)}, u32[]{:S(2)}) %collective-permute-start.13) | collective-permute-done | bytes 32800 | tf_op jit(solution)/shard_map/ppermute | solution.py:270
  38.4 1.7 %collective-permute-done.14 = f32[32,256]{1,0:T(8,128)S(1)} collective-permute-done((f32[32,256]{1,0:T(8,128)S(1)}, f32[32,256]{1,0:T(8,128)S(1)}, u32[]{:S(2)}, u32[]{:S(2)}) %collective-permute-start.14) | collective-permute-done | bytes 32800 | tf_op jit(solution)/shard_map/ppermute | solution.py:270
  40.5 0.5 collective-permute-start.15
  41.0 0.9 %collective-permute-done.15.mate_ref = f32[32,256]{1,0:T(8,128)S(1)} collective-permute-done((f32[32,256]{1,0:T(8,128)S(1)}, f32[32,256]{1,0:T(8,128)S(1)}, u32[]{:S(2)}, u32[]{:S(2)}) %collective-permute-start.15) | collective-permute-done | bytes 32800 | tf_op jit(solution)/shard_map/ppermute | solution.py:270
  41.8 0.9 %shard_map.65 = (f32[32,640]{1,0:T(8,128)S(1)}, f32[32,640]{1,0:T(8,128)S(1)}, f32[32,640]{1,0:T(8,128)S(1)}, f32[32,640]{1,0:T(8,128)S(1)}, f32[32,4,128]{2,1,0:T(4,128)}) custom-call(f32[32,256]{1,0:T(8,128)S(1)} %add_add_fusion.coeffs_ref.mine_ref, f32[32,256]{1,0:T(8,128)S(1)} %collective-permute-done.15.mate_ref, ...), custom_call_target="tpu_custom_call" | custom-call | tf_op jit(solution)/shard_map/pallas_call | solution.py:25
  42.7 3.1 %all-to-all-start.1 = ((f32[32,4,128]{2,1,0:T(4,128)}), f32[32,4,128]{2,1,0:T(4,128)S(1)}, u32[]{:S(2)}, u32[]{:S(2)}) async-start(f32[32,4,128]{2,1,0:T(4,128)} %get-tuple-element.33), calls=%async_computation.1 | async-start | bytes 131072 | tf_op jit(solution)/shard_map/all_to_all | solution.py:387
  45.8 2.7 %collective-permute-start.17 = (f32[32,640]{1,0:T(8,128)S(1)}, f32[32,640]{1,0:T(8,128)S(1)}, u32[]{:S(2)}, u32[]{:S(2)}) collective-permute-start(f32[32,640]{1,0:T(8,128)S(1)} %get-tuple-element.34), channel_id=1, source_target_pairs={{0,17},{1,16},{2,19},{3,18},{4,21},{5,20},{6,23},{7,22},{8,25},{9,... | collective-permute-start | bytes 245768 | tf_op jit(solution)/shard_map/ppermute | solution.py:258
  48.5 0.6 %collective-permute-start.18 = (f32[32,640]{1,0:T(8,128)S(1)}, f32[32,640]{1,0:T(8,128)S(1)}, u32[]{:S(2)}, u32[]{:S(2)}) collective-permute-start(f32[32,640]{1,0:T(8,128)S(1)} %get-tuple-element.35), channel_id=1, source_target_pairs={{0,16},{1,17},{2,18},{3,19},{4,20},{5,21},{6,22},{7,23},{8,9},{9,8... | collective-permute-start | bytes 245768 | tf_op jit(solution)/shard_map/ppermute | solution.py:258
  49.3 3.0 %collective-permute-done.17.refs_0_ = f32[32,640]{1,0:T(8,128)S(1)} collective-permute-done((f32[32,640]{1,0:T(8,128)S(1)}, f32[32,640]{1,0:T(8,128)S(1)}, u32[]{:S(2)}, u32[]{:S(2)}) %collective-permute-start.17) | collective-permute-done | bytes 81952 | tf_op jit(solution)/shard_map/ppermute | solution.py:258
  52.4 1.4 %collective-permute-done.18.refs_1_ = f32[32,640]{1,0:T(8,128)S(1)} collective-permute-done((f32[32,640]{1,0:T(8,128)S(1)}, f32[32,640]{1,0:T(8,128)S(1)}, u32[]{:S(2)}, u32[]{:S(2)}) %collective-permute-start.18) | collective-permute-done | bytes 81952 | tf_op jit(solution)/shard_map/ppermute | solution.py:258
  53.8 0.9 %shard_map.66 = (f32[128,128]{1,0:T(8,128)}, f32[512,128]{1,0:T(8,128)}) custom-call(f32[32,4,128]{2,1,0:T(4,128)S(1)} %all-to-all-done.1.squares_ref, f32[32,640]{1,0:T(8,128)S(1)} %collective-permute-done.17.refs_0_, f32[32,640]{1,0:T(8,128)S(1)} %collective-permute-done.18.refs_1_, f32[32,640]{1,0:T(8,128)S(1)} %collective-permute-done.19.refs_2_, ...), custom_call_target="tpu_custom_call" | custom-call | tf_op jit(solution)/shard_map/pallas_call | solution.py:25
  (32 shorter events, 2.0 us)
Async XLA Ops:
  0.6 4.5 %copy-start.2 = (s32[1,4,1,2]{1,3,2,0:T(2,128)S(1)}, s32[1,4,1,2]{1,3,2,0:T(2,128)}, u32[]{:S(2)}) copy-start(s32[1,4,1,2]{1,3,2,0:T(2,128)} %param.6) | copy-start | bytes 100
  0.6 11.2 %collective-permute-start = (bf16[1024,128]{1,0:T(8,128)(2,1)}, bf16[1024,128]{1,0:T(8,128)(2,1)S(1)}, u32[]{:S(2)}, u32[]{:S(2)}) collective-permute-start(bf16[1024,128]{1,0:T(8,128)(2,1)} %bitcast.11), channel_id=1, source_target_pairs={{0,1},{1,0},{2,3},{3,2},{4,5},{5,4},{6,7},{7,6},{8,24},{9,25},{10,... | collective-permute-start | bytes 786440 | tf_op jit(solution)/shard_map/ppermute | solution.py:258
  3.6 8.2 %collective-permute-start.1 = (bf16[1024,128]{1,0:T(8,128)(2,1)}, bf16[1024,128]{1,0:T(8,128)(2,1)S(1)}, u32[]{:S(2)}, u32[]{:S(2)}) collective-permute-start(bf16[1024,128]{1,0:T(8,128)(2,1)} %bitcast.12), channel_id=1, source_target_pairs={{0,16},{1,17},{2,18},{3,19},{4,20},{5,21},{6,22},{7,23},{8,9},{9,8... | collective-permute-start | bytes 786440 | tf_op jit(solution)/shard_map/ppermute | solution.py:258
  5.2 0.8 %copy-start.1 = (bf16[128,128]{1,0:T(8,128)(2,1)S(1)}, bf16[128,128]{1,0:T(8,128)(2,1)}, u32[]{:S(2)}) copy-start(bf16[128,128]{1,0:T(8,128)(2,1)} %start_ref.1) | copy-start | bytes 98308
  6.7 7.1 %copy-start.3 = (bf16[128,512]{1,0:T(8,128)(2,1)S(1)}, bf16[128,512]{1,0:T(8,128)(2,1)}, u32[]{:S(2)}) copy-start(bf16[128,512]{1,0:T(8,128)(2,1)} %param.7) | copy-start | bytes 393220
  6.7 13.2 %all-to-all-start = ((bf16[16,48,128]{2,1,0:T(8,128)(2,1)}), bf16[16,48,128]{2,1,0:T(8,128)(2,1)S(1)}, u32[]{:S(2)}, u32[]{:S(2)}) async-start(bf16[16,48,128]{2,1,0:T(8,128)(2,1)} %bitcast.2), calls=%async_computation | async-start | bytes 393216 | tf_op jit(solution)/shard_map/all_to_all | solution.py:309
  11.9 8.1 %copy-start = (bf16[1,4,1,2,128,128]{5,4,3,2,1,0:T(8,128)(2,1)S(1)}, bf16[1,4,1,2,128,128]{5,4,3,2,1,0:T(8,128)(2,1)}, u32[]{:S(2)}) copy-start(bf16[1,4,1,2,128,128]{5,4,3,2,1,0:T(8,128)(2,1)} %param.5) | copy-start | bytes 786436
  11.9 8.5 %collective-permute-start.3 = (bf16[1024,128]{1,0:T(8,128)(2,1)S(1)}, bf16[1024,128]{1,0:T(8,128)(2,1)S(1)}, u32[]{:S(2)}, u32[]{:S(2)}) collective-permute-start(bf16[1024,128]{1,0:T(8,128)(2,1)S(1)} %collective-permute-done.refs_1_.refs_5_), channel_id=1, source_target_pairs={{0,16},{1,17},{2,18},{3,19},{4,20},{5,21},{6,22},{7,23},{8,9},{9,8... | collective-permute-start | bytes 786440 | tf_op jit(solution)/shard_map/ppermute | solution.py:258
  13.9 1.3 %collective-permute-start.2 = (bf16[128,256]{1,0:T(8,128)(2,1)S(1)}, bf16[128,256]{1,0:T(8,128)(2,1)S(1)}, u32[]{:S(2)}, u32[]{:S(2)}) collective-permute-start(bf16[128,256]{1,0:T(8,128)(2,1)S(1)} %get-tuple-element.39), channel_id=1, source_target_pairs={{0,8},{1,9},{2,10},{3,11},{4,12},{5,13},{6,14},{7,15},{8,0},{9,1},... | collective-permute-start | bytes 196616 | tf_op jit(solution)/shard_map/ppermute | solution.py:270
  20.6 1.6 %collective-permute-start.4 = (f32[2,2,32,128]{3,2,1,0:T(8,128)S(1)}, f32[2,2,32,128]{3,2,1,0:T(8,128)S(1)}, u32[]{:S(2)}, u32[]{:S(2)}) collective-permute-start(f32[2,2,32,128]{3,2,1,0:T(8,128)S(1)} %get-tuple-element.27), channel_id=1, source_target_pairs={{0,8},{1,9},{2,10},{3,11},{4,12},{5,13},{6,14},{7,15},{8,0},{9,1},... | collective-permute-start | bytes 196616 | tf_op jit(solution)/shard_map/ppermute | solution.py:270
  20.7 5.9 %collective-permute-start.9 = (bf16[2,128,256]{2,1,0:T(8,128)(2,1)S(1)}, bf16[2,128,256]{2,1,0:T(8,128)(2,1)S(1)}, u32[]{:S(2)}, u32[]{:S(2)}) collective-permute-start(bf16[2,128,256]{2,1,0:T(8,128)(2,1)S(1)} %maximum_select_fusion.refs_0_), channel_id=1, source_target_pairs={{0,1},{1,0},{2,3},{3,2},{4,5},{5,4},{6,7},{7,6},{8,24},{9,25},{10,... | collective-permute-start | bytes 393224 | tf_op jit(solution)/shard_map/ppermute | solution.py:258
  22.2 5.6 %collective-permute-start.5 = (bf16[2,2,32,128]{3,2,1,0:T(8,128)(2,1)S(1)}, bf16[2,2,32,128]{3,2,1,0:T(8,128)(2,1)S(1)}, u32[]{:S(2)}, u32[]{:S(2)}) collective-permute-start(bf16[2,2,32,128]{3,2,1,0:T(8,128)(2,1)S(1)} %add_convert_fusion.refs_0_), channel_id=1, source_target_pairs={{0,2},{1,3},{2,0},{3,1},{4,6},{5,7},{6,4},{7,5},{8,10},{9,11},{10,... | collective-permute-start | bytes 98312 | tf_op jit(solution)/shard_map/ppermute | solution.py:270
  23.0 6.0 %collective-permute-start.6 = (bf16[2,2,32,128]{3,2,1,0:T(8,128)(2,1)S(1)}, bf16[2,2,32,128]{3,2,1,0:T(8,128)(2,1)S(1)}, u32[]{:S(2)}, u32[]{:S(2)}) collective-permute-start(bf16[2,2,32,128]{3,2,1,0:T(8,128)(2,1)S(1)} %add_convert_fusion.refs_0_), channel_id=1, source_target_pairs={{0,6},{1,7},{2,4},{3,5},{4,2},{5,3},{6,0},{7,1},{8,14},{9,15},{10,... | collective-permute-start | bytes 98312 | tf_op jit(solution)/shard_map/ppermute | solution.py:270
  25.4 5.1 %collective-permute-start.7 = (bf16[2,2,32,128]{3,2,1,0:T(8,128)(2,1)S(1)}, bf16[2,2,32,128]{3,2,1,0:T(8,128)(2,1)S(1)}, u32[]{:S(2)}, u32[]{:S(2)}) collective-permute-start(bf16[2,2,32,128]{3,2,1,0:T(8,128)(2,1)S(1)} %add_convert_fusion.refs_0_), channel_id=1, source_target_pairs={{0,4},{1,5},{2,6},{3,7},{4,0},{5,1},{6,2},{7,3},{8,12},{9,13},{10,... | collective-permute-start | bytes 98312 | tf_op jit(solution)/shard_map/ppermute | solution.py:270
  25.8 5.2 %collective-permute-start.10 = (bf16[2,128,256]{2,1,0:T(8,128)(2,1)S(1)}, bf16[2,128,256]{2,1,0:T(8,128)(2,1)S(1)}, u32[]{:S(2)}, u32[]{:S(2)}) collective-permute-start(bf16[2,128,256]{2,1,0:T(8,128)(2,1)S(1)} %maximum_select_fusion.refs_0_), channel_id=1, source_target_pairs={{0,16},{1,17},{2,18},{3,19},{4,20},{5,21},{6,22},{7,23},{8,9},{9,8... | collective-permute-start | bytes 393224 | tf_op jit(solution)/shard_map/ppermute | solution.py:258
  26.6 5.6 %collective-permute-start.11 = (bf16[2,128,256]{2,1,0:T(8,128)(2,1)S(1)}, bf16[2,128,256]{2,1,0:T(8,128)(2,1)S(1)}, u32[]{:S(2)}, u32[]{:S(2)}) collective-permute-start(bf16[2,128,256]{2,1,0:T(8,128)(2,1)S(1)} %collective-permute-done.9.refs_1_), channel_id=1, source_target_pairs={{0,16},{1,17},{2,18},{3,19},{4,20},{5,21},{6,22},{7,23},{8,9},{9,8... | collective-permute-start | bytes 393224 | tf_op jit(solution)/shard_map/ppermute | solution.py:258
  30.9 1.4 %collective-permute-start.8 = (f32[2,4,32,128]{3,2,1,0:T(8,128)S(1)}, f32[2,4,32,128]{3,2,1,0:T(8,128)S(1)}, u32[]{:S(2)}, u32[]{:S(2)}) collective-permute-start(f32[2,4,32,128]{3,2,1,0:T(8,128)S(1)} %shard_map.62.ours_ref), channel_id=1, source_target_pairs={{0,8},{1,9},{2,10},{3,11},{4,12},{5,13},{6,14},{7,15},{8,0},{9,1},... | collective-permute-start | bytes 393224 | tf_op jit(solution)/shard_map/ppermute | solution.py:270
  32.6 5.8 %collective-permute-start.13 = (f32[32,256]{1,0:T(8,128)S(1)}, f32[32,256]{1,0:T(8,128)S(1)}, u32[]{:S(2)}, u32[]{:S(2)}) collective-permute-start(f32[32,256]{1,0:T(8,128)S(1)} %get-tuple-element.29), channel_id=1, source_target_pairs={{0,6},{1,7},{2,4},{3,5},{4,2},{5,3},{6,0},{7,1},{8,14},{9,15},{10,... | collective-permute-start | bytes 98312 | tf_op jit(solution)/shard_map/ppermute | solution.py:270
  34.9 5.2 %collective-permute-start.14 = (f32[32,256]{1,0:T(8,128)S(1)}, f32[32,256]{1,0:T(8,128)S(1)}, u32[]{:S(2)}, u32[]{:S(2)}) collective-permute-start(f32[32,256]{1,0:T(8,128)S(1)} %get-tuple-element.29), channel_id=1, source_target_pairs={{0,4},{1,5},{2,6},{3,7},{4,0},{5,1},{6,2},{7,3},{8,12},{9,13},{10,... | collective-permute-start | bytes 98312 | tf_op jit(solution)/shard_map/ppermute | solution.py:270
  35.6 4.5 %collective-permute-start.12 = (f32[32,256]{1,0:T(8,128)S(1)}, f32[32,256]{1,0:T(8,128)S(1)}, u32[]{:S(2)}, u32[]{:S(2)}) collective-permute-start(f32[32,256]{1,0:T(8,128)S(1)} %get-tuple-element.29), channel_id=1, source_target_pairs={{0,2},{1,3},{2,0},{3,1},{4,6},{5,7},{6,4},{7,5},{8,10},{9,11},{10,... | collective-permute-start | bytes 98312 | tf_op jit(solution)/shard_map/ppermute | solution.py:270
  40.4 1.4 %collective-permute-start.16 = (f32[2,2,32,128]{3,2,1,0:T(8,128)S(1)}, f32[2,2,32,128]{3,2,1,0:T(8,128)S(1)}, u32[]{:S(2)}, u32[]{:S(2)}) collective-permute-start(f32[2,2,32,128]{3,2,1,0:T(8,128)S(1)} %get-tuple-element.32), channel_id=1, source_target_pairs={{0,8},{1,9},{2,10},{3,11},{4,12},{5,13},{6,14},{7,15},{8,0},{9,1},... | collective-permute-start | bytes 196616 | tf_op jit(solution)/shard_map/ppermute | solution.py:270
  40.5 1.4 %collective-permute-start.15 = (f32[32,256]{1,0:T(8,128)S(1)}, f32[32,256]{1,0:T(8,128)S(1)}, u32[]{:S(2)}, u32[]{:S(2)}) collective-permute-start(f32[32,256]{1,0:T(8,128)S(1)} %add_add_fusion.coeffs_ref.mine_ref), channel_id=1, source_target_pairs={{0,8},{1,9},{2,10},{3,11},{4,12},{5,13},{6,14},{7,15},{8,0},{9,1},... | collective-permute-start | bytes 98312 | tf_op jit(solution)/shard_map/ppermute | solution.py:270
  42.7 11.1 %all-to-all-start.1 = ((f32[32,4,128]{2,1,0:T(4,128)}), f32[32,4,128]{2,1,0:T(4,128)S(1)}, u32[]{:S(2)}, u32[]{:S(2)}) async-start(f32[32,4,128]{2,1,0:T(4,128)} %get-tuple-element.33), calls=%async_computation.1 | async-start | bytes 131072 | tf_op jit(solution)/shard_map/all_to_all | solution.py:387
  45.8 6.6 %collective-permute-start.17 = (f32[32,640]{1,0:T(8,128)S(1)}, f32[32,640]{1,0:T(8,128)S(1)}, u32[]{:S(2)}, u32[]{:S(2)}) collective-permute-start(f32[32,640]{1,0:T(8,128)S(1)} %get-tuple-element.34), channel_id=1, source_target_pairs={{0,17},{1,16},{2,19},{3,18},{4,21},{5,20},{6,23},{7,22},{8,25},{9,... | collective-permute-start | bytes 245768 | tf_op jit(solution)/shard_map/ppermute | solution.py:258
  48.5 5.2 %collective-permute-start.18 = (f32[32,640]{1,0:T(8,128)S(1)}, f32[32,640]{1,0:T(8,128)S(1)}, u32[]{:S(2)}, u32[]{:S(2)}) collective-permute-start(f32[32,640]{1,0:T(8,128)S(1)} %get-tuple-element.35), channel_id=1, source_target_pairs={{0,16},{1,17},{2,18},{3,19},{4,20},{5,21},{6,22},{7,23},{8,9},{9,8... | collective-permute-start | bytes 245768 | tf_op jit(solution)/shard_map/ppermute | solution.py:258
  49.1 4.7 %collective-permute-start.19 = (f32[32,640]{1,0:T(8,128)S(1)}, f32[32,640]{1,0:T(8,128)S(1)}, u32[]{:S(2)}, u32[]{:S(2)}) collective-permute-start(f32[32,640]{1,0:T(8,128)S(1)} %get-tuple-element.36), channel_id=1, source_target_pairs={{0,1},{1,0},{2,3},{3,2},{4,5},{5,4},{6,7},{7,6},{8,24},{9,25},{10,... | collective-permute-start | bytes 245768 | tf_op jit(solution)/shard_map/ppermute | solution.py:258

commit v8 on v6

--- a/solution.py
+++ b/solution.py
@@ -313,7 +313,6 @@
     history = jnp.where(core == 0, jnp.stack([ours, theirs]), jnp.stack([theirs, ours]))
     own = [history]
     if plane:
-        history, tiles[2] = lax.optimization_barrier((history, tiles[2]))
         own += [crossed(history, entry) for entry in near[1:3]]
 
     piece = (lanes, n_block, width, order)

time: 55.1 us -> 55.1 us (level)
    all_to_all x1, waiting for transfers between devices: 4.7 us -> 5.98 us  [per_device(): lax.all_to_all(parts.reshape(n_block * n_col, tall, order), BOTH, 0, 0, a...]
    ppermute x11, waiting for transfers between devices: 7.66 us -> 6.4 us  [swapped(): return lax.ppermute(value, BOTH, pairs)]
  transfers between devices with their start and end apart: 22 -> 22, of which waited for: 11 -> 10; matrix products, arithmetic and copies ran while one was open for 0% -> 0% of each run, Pallas kernels for 3% -> 4%
where the time goes in v8:
time: 55.1 us; the launch traced here: 54.8 us
  starting transfers between devices  30.6 us (56%)
  waiting for transfers between devices  18.3 us (33%)
  Pallas kernels  4.25 us (8%)
  between operations  0.79 us (1%)
  local copies, waits for them, and re-layouts  0.77 us (1%)
    ppermute x9, starting transfers between devices, crossed(): return lax.ppermute(value, BOTH, pairs)  13.6 us
    ppermute x11, starting transfers between devices, swapped(): return lax.ppermute(value, BOTH, pairs)  8.77 us
    ppermute x11, waiting for transfers between devices, swapped(): return lax.ppermute(value, BOTH, pairs)  6.4 us
    all_to_all x1, waiting for transfers between devices, per_device(): lax.all_to_all(parts.reshape(n_block * n_col, tall, order), BOTH, 0, 0, a...  5.98 us
    ppermute x9, waiting for transfers between devices, crossed(): return lax.ppermute(value, BOTH, pairs)  5.95 us
    all_to_all x1, starting transfers between devices, per_device(): lax.all_to_all(parts.reshape(n_block * n_col, tall, order), BOTH, 0, 0, a...  5.11 us
    pallas_call x8, Pallas kernels, call(): pl.pallas_call(kernel, out_shape=out, in_specs=[VMEM] * len(args), out_sp...  4.25 us
    all_to_all x1, starting transfers between devices, per_device(): squares = lax.all_to_all(squares, BOTH, 0, 0)  3.14 us
  transfers between devices with their start and end apart: 22, of which 10 were waited for; matrix products, arithmetic and copies ran while one was open for 0% of the time, Pallas kernels for 4%

profile of v8, /device:TPU:0, one launch (start us, length us, event | category | flops | bytes accessed | tf_op | source)
XLA Modules:
  0.0 54.8 jit_solution(8565218376827756673)
XLA Ops:
  0.6 3.0 %collective-permute-start = (bf16[1024,128]{1,0:T(8,128)(2,1)}, bf16[1024,128]{1,0:T(8,128)(2,1)S(1)}, u32[]{:S(2)}, u32[]{:S(2)}) collective-permute-start(bf16[1024,128]{1,0:T(8,128)(2,1)} %bitcast.11), channel_id=1, source_target_pairs={{0,1},{1,0},{2,3},{3,2},{4,5},{5,4},{6,7},{7,6},{8,24},{9,25},{10,... | collective-permute-start | bytes 786440 | tf_op jit(solution)/shard_map/ppermute | solution.py:254
  3.6 1.5 %collective-permute-start.1 = (bf16[1024,128]{1,0:T(8,128)(2,1)}, bf16[1024,128]{1,0:T(8,128)(2,1)S(1)}, u32[]{:S(2)}, u32[]{:S(2)}) collective-permute-start(bf16[1024,128]{1,0:T(8,128)(2,1)} %bitcast.12), channel_id=1, source_target_pairs={{0,16},{1,17},{2,18},{3,19},{4,20},{5,21},{6,22},{7,23},{8,9},{9,8... | collective-permute-start | bytes 786440 | tf_op jit(solution)/shard_map/ppermute | solution.py:254
  5.2 0.8 %copy-done.1 = bf16[128,128]{1,0:T(8,128)(2,1)S(1)} copy-done((bf16[128,128]{1,0:T(8,128)(2,1)S(1)}, bf16[128,128]{1,0:T(8,128)(2,1)}, u32[]{:S(2)}) %copy-start.1) | copy-done | bytes 32792
  5.9 0.8 %shard_map.59 = bf16[2,8,48,128]{3,2,1,0:T(8,128)(2,1)} custom-call(s32[2,4]{1,0:T(2,128)S(1)} %bitcast.15, bf16[128,128]{1,0:T(8,128)(2,1)S(1)} %copy-done.1), custom_call_target="tpu_custom_call" | custom-call | tf_op jit(solution)/shard_map/pallas_call | solution.py:25
  6.7 5.1 %all-to-all-start = ((bf16[16,48,128]{2,1,0:T(8,128)(2,1)}), bf16[16,48,128]{2,1,0:T(8,128)(2,1)S(1)}, u32[]{:S(2)}, u32[]{:S(2)}) async-start(bf16[16,48,128]{2,1,0:T(8,128)(2,1)} %bitcast.2), calls=%async_computation | async-start | bytes 393216 | tf_op jit(solution)/shard_map/all_to_all | solution.py:305
  11.9 2.0 %collective-permute-start.2 = (bf16[1024,128]{1,0:T(8,128)(2,1)S(1)}, bf16[1024,128]{1,0:T(8,128)(2,1)S(1)}, u32[]{:S(2)}, u32[]{:S(2)}) collective-permute-start(bf16[1024,128]{1,0:T(8,128)(2,1)S(1)} %collective-permute-done.refs_1_.refs_5_), channel_id=1, source_target_pairs={{0,16},{1,17},{2,18},{3,19},{4,20},{5,21},{6,22},{7,23},{8,9},{9,8... | collective-permute-start | bytes 786440 | tf_op jit(solution)/shard_map/ppermute | solution.py:254
  14.0 6.0 %all-to-all-done = bf16[16,48,128]{2,1,0:T(8,128)(2,1)S(1)} async-done(((bf16[16,48,128]{2,1,0:T(8,128)(2,1)}), bf16[16,48,128]{2,1,0:T(8,128)(2,1)S(1)}, u32[]{:S(2)}, u32[]{:S(2)}) %all-to-all-start) | async-done | bytes 196640 | tf_op jit(solution)/shard_map/all_to_all | solution.py:305
  19.9 0.5 shard_map.60
  20.7 1.5 %collective-permute-start.9 = (bf16[2,128,256]{2,1,0:T(8,128)(2,1)S(1)}, bf16[2,128,256]{2,1,0:T(8,128)(2,1)S(1)}, u32[]{:S(2)}, u32[]{:S(2)}) collective-permute-start(bf16[2,128,256]{2,1,0:T(8,128)(2,1)S(1)} %maximum_select_fusion.refs_0_), channel_id=1, source_target_pairs={{0,1},{1,0},{2,3},{3,2},{4,5},{5,4},{6,7},{7,6},{8,24},{9,25},{10,... | collective-permute-start | bytes 393224 | tf_op jit(solution)/shard_map/ppermute | solution.py:254
  22.3 0.8 %collective-permute-start.4 = (bf16[2,2,32,128]{3,2,1,0:T(8,128)(2,1)S(1)}, bf16[2,2,32,128]{3,2,1,0:T(8,128)(2,1)S(1)}, u32[]{:S(2)}, u32[]{:S(2)}) collective-permute-start(bf16[2,2,32,128]{3,2,1,0:T(8,128)(2,1)S(1)} %add_convert_fusion.refs_0_), channel_id=1, source_target_pairs={{0,2},{1,3},{2,0},{3,1},{4,6},{5,7},{6,4},{7,5},{8,10},{9,11},{10,... | collective-permute-start | bytes 98312 | tf_op jit(solution)/shard_map/ppermute | solution.py:266
  23.1 2.2 %collective-permute-start.5 = (bf16[2,2,32,128]{3,2,1,0:T(8,128)(2,1)S(1)}, bf16[2,2,32,128]{3,2,1,0:T(8,128)(2,1)S(1)}, u32[]{:S(2)}, u32[]{:S(2)}) collective-permute-start(bf16[2,2,32,128]{3,2,1,0:T(8,128)(2,1)S(1)} %add_convert_fusion.refs_0_), channel_id=1, source_target_pairs={{0,4},{1,5},{2,6},{3,7},{4,0},{5,1},{6,2},{7,3},{8,12},{9,13},{10,... | collective-permute-start | bytes 98312 | tf_op jit(solution)/shard_map/ppermute | solution.py:266
  25.3 1.4 %collective-permute-start.6 = (bf16[2,2,32,128]{3,2,1,0:T(8,128)(2,1)S(1)}, bf16[2,2,32,128]{3,2,1,0:T(8,128)(2,1)S(1)}, u32[]{:S(2)}, u32[]{:S(2)}) collective-permute-start(bf16[2,2,32,128]{3,2,1,0:T(8,128)(2,1)S(1)} %add_convert_fusion.refs_0_), channel_id=1, source_target_pairs={{0,6},{1,7},{2,4},{3,5},{4,2},{5,3},{6,0},{7,1},{8,14},{9,15},{10,... | collective-permute-start | bytes 98312 | tf_op jit(solution)/shard_map/ppermute | solution.py:266
  26.7 0.8 %collective-permute-start.10 = (bf16[2,128,256]{2,1,0:T(8,128)(2,1)S(1)}, bf16[2,128,256]{2,1,0:T(8,128)(2,1)S(1)}, u32[]{:S(2)}, u32[]{:S(2)}) collective-permute-start(bf16[2,128,256]{2,1,0:T(8,128)(2,1)S(1)} %maximum_select_fusion.refs_0_), channel_id=1, source_target_pairs={{0,16},{1,17},{2,18},{3,19},{4,20},{5,21},{6,22},{7,23},{8,9},{9,8... | collective-permute-start | bytes 393224 | tf_op jit(solution)/shard_map/ppermute | solution.py:254
  27.5 1.2 %collective-permute-start.11 = (bf16[2,128,256]{2,1,0:T(8,128)(2,1)S(1)}, bf16[2,128,256]{2,1,0:T(8,128)(2,1)S(1)}, u32[]{:S(2)}, u32[]{:S(2)}) collective-permute-start(bf16[2,128,256]{2,1,0:T(8,128)(2,1)S(1)} %collective-permute-done.9.refs_1_), channel_id=1, source_target_pairs={{0,16},{1,17},{2,18},{3,19},{4,20},{5,21},{6,22},{7,23},{8,9},{9,8... | collective-permute-start | bytes 393224 | tf_op jit(solution)/shard_map/ppermute | solution.py:254
  28.8 2.3 %collective-permute-done.6.refs_3_ = bf16[2,2,32,128]{3,2,1,0:T(8,128)(2,1)S(1)} collective-permute-done((bf16[2,2,32,128]{3,2,1,0:T(8,128)(2,1)S(1)}, bf16[2,2,32,128]{3,2,1,0:T(8,128)(2,1)S(1)}, u32[]{:S(2)}, u32[]{:S(2)}) %collective-permute-start.6) | collective-permute-done | bytes 32800 | tf_op jit(solution)/shard_map/ppermute | solution.py:266
  31.0 0.5 shard_map.62.ours_ref
  31.7 1.4 %collective-permute-done.11.refs_3_ = bf16[2,128,256]{2,1,0:T(8,128)(2,1)S(1)} collective-permute-done((bf16[2,128,256]{2,1,0:T(8,128)(2,1)S(1)}, bf16[2,128,256]{2,1,0:T(8,128)(2,1)S(1)}, u32[]{:S(2)}, u32[]{:S(2)}) %collective-permute-start.11) | collective-permute-done | bytes 131104 | tf_op jit(solution)/shard_map/ppermute | solution.py:254
  33.4 0.8 %collective-permute-start.13 = (f32[32,256]{1,0:T(8,128)S(1)}, f32[32,256]{1,0:T(8,128)S(1)}, u32[]{:S(2)}, u32[]{:S(2)}) collective-permute-start(f32[32,256]{1,0:T(8,128)S(1)} %get-tuple-element.25), channel_id=1, source_target_pairs={{0,4},{1,5},{2,6},{3,7},{4,0},{5,1},{6,2},{7,3},{8,12},{9,13},{10,... | collective-permute-start | bytes 98312 | tf_op jit(solution)/shard_map/ppermute | solution.py:266
  34.2 1.8 %collective-permute-start.14 = (f32[32,256]{1,0:T(8,128)S(1)}, f32[32,256]{1,0:T(8,128)S(1)}, u32[]{:S(2)}, u32[]{:S(2)}) collective-permute-start(f32[32,256]{1,0:T(8,128)S(1)} %get-tuple-element.25), channel_id=1, source_target_pairs={{0,6},{1,7},{2,4},{3,5},{4,2},{5,3},{6,0},{7,1},{8,14},{9,15},{10,... | collective-permute-start | bytes 98312 | tf_op jit(solution)/shard_map/ppermute | solution.py:266
  35.9 1.0 %collective-permute-start.12 = (f32[32,256]{1,0:T(8,128)S(1)}, f32[32,256]{1,0:T(8,128)S(1)}, u32[]{:S(2)}, u32[]{:S(2)}) collective-permute-start(f32[32,256]{1,0:T(8,128)S(1)} %get-tuple-element.25), channel_id=1, source_target_pairs={{0,2},{1,3},{2,0},{3,1},{4,6},{5,7},{6,4},{7,5},{8,10},{9,11},{10,... | collective-permute-start | bytes 98312 | tf_op jit(solution)/shard_map/ppermute | solution.py:266
  36.9 1.7 %collective-permute-done.13 = f32[32,256]{1,0:T(8,128)S(1)} collective-permute-done((f32[32,256]{1,0:T(8,128)S(1)}, f32[32,256]{1,0:T(8,128)S(1)}, u32[]{:S(2)}, u32[]{:S(2)}) %collective-permute-start.13) | collective-permute-done | bytes 32800 | tf_op jit(solution)/shard_map/ppermute | solution.py:266
  38.6 1.4 %collective-permute-done.14 = f32[32,256]{1,0:T(8,128)S(1)} collective-permute-done((f32[32,256]{1,0:T(8,128)S(1)}, f32[32,256]{1,0:T(8,128)S(1)}, u32[]{:S(2)}, u32[]{:S(2)}) %collective-permute-start.14) | collective-permute-done | bytes 32800 | tf_op jit(solution)/shard_map/ppermute | solution.py:266
  40.2 0.3 shard_map.64
  40.6 0.5 collective-permute-start.15
  41.1 0.9 %collective-permute-done.15.mate_ref = f32[32,256]{1,0:T(8,128)S(1)} collective-permute-done((f32[32,256]{1,0:T(8,128)S(1)}, f32[32,256]{1,0:T(8,128)S(1)}, u32[]{:S(2)}, u32[]{:S(2)}) %collective-permute-start.15) | collective-permute-done | bytes 32800 | tf_op jit(solution)/shard_map/ppermute | solution.py:266
  41.9 0.9 %shard_map.65 = (f32[32,640]{1,0:T(8,128)S(1)}, f32[32,640]{1,0:T(8,128)S(1)}, f32[32,640]{1,0:T(8,128)S(1)}, f32[32,640]{1,0:T(8,128)S(1)}, f32[32,4,128]{2,1,0:T(4,128)}) custom-call(f32[32,256]{1,0:T(8,128)S(1)} %add_add_fusion.coeffs_ref.mine_ref, f32[32,256]{1,0:T(8,128)S(1)} %collective-permute-done.15.mate_ref, ...), custom_call_target="tpu_custom_call" | custom-call | tf_op jit(solution)/shard_map/pallas_call | solution.py:25
  42.8 3.1 %all-to-all-start.1 = ((f32[32,4,128]{2,1,0:T(4,128)}), f32[32,4,128]{2,1,0:T(4,128)S(1)}, u32[]{:S(2)}, u32[]{:S(2)}) async-start(f32[32,4,128]{2,1,0:T(4,128)} %get-tuple-element.29), calls=%async_computation.1 | async-start | bytes 131072 | tf_op jit(solution)/shard_map/all_to_all | solution.py:382
  45.9 2.7 %collective-permute-start.17 = (f32[32,640]{1,0:T(8,128)S(1)}, f32[32,640]{1,0:T(8,128)S(1)}, u32[]{:S(2)}, u32[]{:S(2)}) collective-permute-start(f32[32,640]{1,0:T(8,128)S(1)} %get-tuple-element.30), channel_id=1, source_target_pairs={{0,17},{1,16},{2,19},{3,18},{4,21},{5,20},{6,23},{7,22},{8,25},{9,... | collective-permute-start | bytes 245768 | tf_op jit(solution)/shard_map/ppermute | solution.py:254
  48.7 0.6 %collective-permute-start.18 = (f32[32,640]{1,0:T(8,128)S(1)}, f32[32,640]{1,0:T(8,128)S(1)}, u32[]{:S(2)}, u32[]{:S(2)}) collective-permute-start(f32[32,640]{1,0:T(8,128)S(1)} %get-tuple-element.31), channel_id=1, source_target_pairs={{0,16},{1,17},{2,18},{3,19},{4,20},{5,21},{6,22},{7,23},{8,9},{9,8... | collective-permute-start | bytes 245768 | tf_op jit(solution)/shard_map/ppermute | solution.py:254
  49.5 3.0 %collective-permute-done.17.refs_0_ = f32[32,640]{1,0:T(8,128)S(1)} collective-permute-done((f32[32,640]{1,0:T(8,128)S(1)}, f32[32,640]{1,0:T(8,128)S(1)}, u32[]{:S(2)}, u32[]{:S(2)}) %collective-permute-start.17) | collective-permute-done | bytes 81952 | tf_op jit(solution)/shard_map/ppermute | solution.py:254
  52.5 1.4 %collective-permute-done.18.refs_1_ = f32[32,640]{1,0:T(8,128)S(1)} collective-permute-done((f32[32,640]{1,0:T(8,128)S(1)}, f32[32,640]{1,0:T(8,128)S(1)}, u32[]{:S(2)}, u32[]{:S(2)}) %collective-permute-start.18) | collective-permute-done | bytes 81952 | tf_op jit(solution)/shard_map/ppermute | solution.py:254
  53.9 0.9 %shard_map.66 = (f32[128,128]{1,0:T(8,128)}, f32[512,128]{1,0:T(8,128)}) custom-call(f32[32,4,128]{2,1,0:T(4,128)S(1)} %all-to-all-done.1.squares_ref, f32[32,640]{1,0:T(8,128)S(1)} %collective-permute-done.17.refs_0_, f32[32,640]{1,0:T(8,128)S(1)} %collective-permute-done.18.refs_1_, f32[32,640]{1,0:T(8,128)S(1)} %collective-permute-done.19.refs_2_, ...), custom_call_target="tpu_custom_call" | custom-call | tf_op jit(solution)/shard_map/pallas_call | solution.py:25
  (32 shorter events, 1.4 us)
Async XLA Ops:
  0.6 4.5 %copy-start.2 = (s32[1,4,1,2]{1,3,2,0:T(2,128)S(1)}, s32[1,4,1,2]{1,3,2,0:T(2,128)}, u32[]{:S(2)}) copy-start(s32[1,4,1,2]{1,3,2,0:T(2,128)} %param.6) | copy-start | bytes 100
  0.6 11.2 %collective-permute-start = (bf16[1024,128]{1,0:T(8,128)(2,1)}, bf16[1024,128]{1,0:T(8,128)(2,1)S(1)}, u32[]{:S(2)}, u32[]{:S(2)}) collective-permute-start(bf16[1024,128]{1,0:T(8,128)(2,1)} %bitcast.11), channel_id=1, source_target_pairs={{0,1},{1,0},{2,3},{3,2},{4,5},{5,4},{6,7},{7,6},{8,24},{9,25},{10,... | collective-permute-start | bytes 786440 | tf_op jit(solution)/shard_map/ppermute | solution.py:254
  3.6 8.2 %collective-permute-start.1 = (bf16[1024,128]{1,0:T(8,128)(2,1)}, bf16[1024,128]{1,0:T(8,128)(2,1)S(1)}, u32[]{:S(2)}, u32[]{:S(2)}) collective-permute-start(bf16[1024,128]{1,0:T(8,128)(2,1)} %bitcast.12), channel_id=1, source_target_pairs={{0,16},{1,17},{2,18},{3,19},{4,20},{5,21},{6,22},{7,23},{8,9},{9,8... | collective-permute-start | bytes 786440 | tf_op jit(solution)/shard_map/ppermute | solution.py:254
  5.2 0.8 %copy-start.1 = (bf16[128,128]{1,0:T(8,128)(2,1)S(1)}, bf16[128,128]{1,0:T(8,128)(2,1)}, u32[]{:S(2)}) copy-start(bf16[128,128]{1,0:T(8,128)(2,1)} %start_ref.1) | copy-start | bytes 98308
  6.7 7.1 %copy-start.3 = (bf16[128,512]{1,0:T(8,128)(2,1)S(1)}, bf16[128,512]{1,0:T(8,128)(2,1)}, u32[]{:S(2)}) copy-start(bf16[128,512]{1,0:T(8,128)(2,1)} %param.7) | copy-start | bytes 393220
  6.7 13.2 %copy-start = (bf16[1,4,1,2,128,128]{5,4,3,2,1,0:T(8,128)(2,1)S(1)}, bf16[1,4,1,2,128,128]{5,4,3,2,1,0:T(8,128)(2,1)}, u32[]{:S(2)}) copy-start(bf16[1,4,1,2,128,128]{5,4,3,2,1,0:T(8,128)(2,1)} %param.5) | copy-start | bytes 786436
  6.7 13.2 %all-to-all-start = ((bf16[16,48,128]{2,1,0:T(8,128)(2,1)}), bf16[16,48,128]{2,1,0:T(8,128)(2,1)S(1)}, u32[]{:S(2)}, u32[]{:S(2)}) async-start(bf16[16,48,128]{2,1,0:T(8,128)(2,1)} %bitcast.2), calls=%async_computation | async-start | bytes 393216 | tf_op jit(solution)/shard_map/all_to_all | solution.py:305
  11.9 8.5 %collective-permute-start.2 = (bf16[1024,128]{1,0:T(8,128)(2,1)S(1)}, bf16[1024,128]{1,0:T(8,128)(2,1)S(1)}, u32[]{:S(2)}, u32[]{:S(2)}) collective-permute-start(bf16[1024,128]{1,0:T(8,128)(2,1)S(1)} %collective-permute-done.refs_1_.refs_5_), channel_id=1, source_target_pairs={{0,16},{1,17},{2,18},{3,19},{4,20},{5,21},{6,22},{7,23},{8,9},{9,8... | collective-permute-start | bytes 786440 | tf_op jit(solution)/shard_map/ppermute | solution.py:254
  13.9 6.8 %collective-permute-start.8 = (bf16[128,256]{1,0:T(8,128)(2,1)S(1)}, bf16[128,256]{1,0:T(8,128)(2,1)S(1)}, u32[]{:S(2)}, u32[]{:S(2)}) collective-permute-start(bf16[128,256]{1,0:T(8,128)(2,1)S(1)} %get-tuple-element.35), channel_id=1, source_target_pairs={{0,8},{1,9},{2,10},{3,11},{4,12},{5,13},{6,14},{7,15},{8,0},{9,1},... | collective-permute-start | bytes 196616 | tf_op jit(solution)/shard_map/ppermute | solution.py:266
  20.6 1.6 %collective-permute-start.3 = (f32[2,2,32,128]{3,2,1,0:T(8,128)S(1)}, f32[2,2,32,128]{3,2,1,0:T(8,128)S(1)}, u32[]{:S(2)}, u32[]{:S(2)}) collective-permute-start(f32[2,2,32,128]{3,2,1,0:T(8,128)S(1)} %get-tuple-element.24), channel_id=1, source_target_pairs={{0,8},{1,9},{2,10},{3,11},{4,12},{5,13},{6,14},{7,15},{8,0},{9,1},... | collective-permute-start | bytes 196616 | tf_op jit(solution)/shard_map/ppermute | solution.py:266
  20.7 6.8 %collective-permute-start.9 = (bf16[2,128,256]{2,1,0:T(8,128)(2,1)S(1)}, bf16[2,128,256]{2,1,0:T(8,128)(2,1)S(1)}, u32[]{:S(2)}, u32[]{:S(2)}) collective-permute-start(bf16[2,128,256]{2,1,0:T(8,128)(2,1)S(1)} %maximum_select_fusion.refs_0_), channel_id=1, source_target_pairs={{0,1},{1,0},{2,3},{3,2},{4,5},{5,4},{6,7},{7,6},{8,24},{9,25},{10,... | collective-permute-start | bytes 393224 | tf_op jit(solution)/shard_map/ppermute | solution.py:254
  22.3 6.5 %collective-permute-start.4 = (bf16[2,2,32,128]{3,2,1,0:T(8,128)(2,1)S(1)}, bf16[2,2,32,128]{3,2,1,0:T(8,128)(2,1)S(1)}, u32[]{:S(2)}, u32[]{:S(2)}) collective-permute-start(bf16[2,2,32,128]{3,2,1,0:T(8,128)(2,1)S(1)} %add_convert_fusion.refs_0_), channel_id=1, source_target_pairs={{0,2},{1,3},{2,0},{3,1},{4,6},{5,7},{6,4},{7,5},{8,10},{9,11},{10,... | collective-permute-start | bytes 98312 | tf_op jit(solution)/shard_map/ppermute | solution.py:266
  23.1 5.7 %collective-permute-start.5 = (bf16[2,2,32,128]{3,2,1,0:T(8,128)(2,1)S(1)}, bf16[2,2,32,128]{3,2,1,0:T(8,128)(2,1)S(1)}, u32[]{:S(2)}, u32[]{:S(2)}) collective-permute-start(bf16[2,2,32,128]{3,2,1,0:T(8,128)(2,1)S(1)} %add_convert_fusion.refs_0_), channel_id=1, source_target_pairs={{0,4},{1,5},{2,6},{3,7},{4,0},{5,1},{6,2},{7,3},{8,12},{9,13},{10,... | collective-permute-start | bytes 98312 | tf_op jit(solution)/shard_map/ppermute | solution.py:266
  25.3 5.7 %collective-permute-start.6 = (bf16[2,2,32,128]{3,2,1,0:T(8,128)(2,1)S(1)}, bf16[2,2,32,128]{3,2,1,0:T(8,128)(2,1)S(1)}, u32[]{:S(2)}, u32[]{:S(2)}) collective-permute-start(bf16[2,2,32,128]{3,2,1,0:T(8,128)(2,1)S(1)} %add_convert_fusion.refs_0_), channel_id=1, source_target_pairs={{0,6},{1,7},{2,4},{3,5},{4,2},{5,3},{6,0},{7,1},{8,14},{9,15},{10,... | collective-permute-start | bytes 98312 | tf_op jit(solution)/shard_map/ppermute | solution.py:266
  26.7 5.0 %collective-permute-start.10 = (bf16[2,128,256]{2,1,0:T(8,128)(2,1)S(1)}, bf16[2,128,256]{2,1,0:T(8,128)(2,1)S(1)}, u32[]{:S(2)}, u32[]{:S(2)}) collective-permute-start(bf16[2,128,256]{2,1,0:T(8,128)(2,1)S(1)} %maximum_select_fusion.refs_0_), channel_id=1, source_target_pairs={{0,16},{1,17},{2,18},{3,19},{4,20},{5,21},{6,22},{7,23},{8,9},{9,8... | collective-permute-start | bytes 393224 | tf_op jit(solution)/shard_map/ppermute | solution.py:254
  27.5 5.6 %collective-permute-start.11 = (bf16[2,128,256]{2,1,0:T(8,128)(2,1)S(1)}, bf16[2,128,256]{2,1,0:T(8,128)(2,1)S(1)}, u32[]{:S(2)}, u32[]{:S(2)}) collective-permute-start(bf16[2,128,256]{2,1,0:T(8,128)(2,1)S(1)} %collective-permute-done.9.refs_1_), channel_id=1, source_target_pairs={{0,16},{1,17},{2,18},{3,19},{4,20},{5,21},{6,22},{7,23},{8,9},{9,8... | collective-permute-start | bytes 393224 | tf_op jit(solution)/shard_map/ppermute | solution.py:254
  31.5 1.6 %collective-permute-start.7 = (f32[2,4,32,128]{3,2,1,0:T(8,128)S(1)}, f32[2,4,32,128]{3,2,1,0:T(8,128)S(1)}, u32[]{:S(2)}, u32[]{:S(2)}) collective-permute-start(f32[2,4,32,128]{3,2,1,0:T(8,128)S(1)} %shard_map.62.ours_ref), channel_id=1, source_target_pairs={{0,8},{1,9},{2,10},{3,11},{4,12},{5,13},{6,14},{7,15},{8,0},{9,1},... | collective-permute-start | bytes 393224 | tf_op jit(solution)/shard_map/ppermute | solution.py:266
  33.4 5.3 %collective-permute-start.13 = (f32[32,256]{1,0:T(8,128)S(1)}, f32[32,256]{1,0:T(8,128)S(1)}, u32[]{:S(2)}, u32[]{:S(2)}) collective-permute-start(f32[32,256]{1,0:T(8,128)S(1)} %get-tuple-element.25), channel_id=1, source_target_pairs={{0,4},{1,5},{2,6},{3,7},{4,0},{5,1},{6,2},{7,3},{8,12},{9,13},{10,... | collective-permute-start | bytes 98312 | tf_op jit(solution)/shard_map/ppermute | solution.py:266
  34.2 5.8 %collective-permute-start.14 = (f32[32,256]{1,0:T(8,128)S(1)}, f32[32,256]{1,0:T(8,128)S(1)}, u32[]{:S(2)}, u32[]{:S(2)}) collective-permute-start(f32[32,256]{1,0:T(8,128)S(1)} %get-tuple-element.25), channel_id=1, source_target_pairs={{0,6},{1,7},{2,4},{3,5},{4,2},{5,3},{6,0},{7,1},{8,14},{9,15},{10,... | collective-permute-start | bytes 98312 | tf_op jit(solution)/shard_map/ppermute | solution.py:266
  35.9 4.3 %collective-permute-start.12 = (f32[32,256]{1,0:T(8,128)S(1)}, f32[32,256]{1,0:T(8,128)S(1)}, u32[]{:S(2)}, u32[]{:S(2)}) collective-permute-start(f32[32,256]{1,0:T(8,128)S(1)} %get-tuple-element.25), channel_id=1, source_target_pairs={{0,2},{1,3},{2,0},{3,1},{4,6},{5,7},{6,4},{7,5},{8,10},{9,11},{10,... | collective-permute-start | bytes 98312 | tf_op jit(solution)/shard_map/ppermute | solution.py:266
  40.5 1.4 %collective-permute-start.16 = (f32[2,2,32,128]{3,2,1,0:T(8,128)S(1)}, f32[2,2,32,128]{3,2,1,0:T(8,128)S(1)}, u32[]{:S(2)}, u32[]{:S(2)}) collective-permute-start(f32[2,2,32,128]{3,2,1,0:T(8,128)S(1)} %get-tuple-element.28), channel_id=1, source_target_pairs={{0,8},{1,9},{2,10},{3,11},{4,12},{5,13},{6,14},{7,15},{8,0},{9,1},... | collective-permute-start | bytes 196616 | tf_op jit(solution)/shard_map/ppermute | solution.py:266
  40.6 1.4 %collective-permute-start.15 = (f32[32,256]{1,0:T(8,128)S(1)}, f32[32,256]{1,0:T(8,128)S(1)}, u32[]{:S(2)}, u32[]{:S(2)}) collective-permute-start(f32[32,256]{1,0:T(8,128)S(1)} %add_add_fusion.coeffs_ref.mine_ref), channel_id=1, source_target_pairs={{0,8},{1,9},{2,10},{3,11},{4,12},{5,13},{6,14},{7,15},{8,0},{9,1},... | collective-permute-start | bytes 98312 | tf_op jit(solution)/shard_map/ppermute | solution.py:266
  42.8 11.1 %all-to-all-start.1 = ((f32[32,4,128]{2,1,0:T(4,128)}), f32[32,4,128]{2,1,0:T(4,128)S(1)}, u32[]{:S(2)}, u32[]{:S(2)}) async-start(f32[32,4,128]{2,1,0:T(4,128)} %get-tuple-element.29), calls=%async_computation.1 | async-start | bytes 131072 | tf_op jit(solution)/shard_map/all_to_all | solution.py:382
  45.9 6.6 %collective-permute-start.17 = (f32[32,640]{1,0:T(8,128)S(1)}, f32[32,640]{1,0:T(8,128)S(1)}, u32[]{:S(2)}, u32[]{:S(2)}) collective-permute-start(f32[32,640]{1,0:T(8,128)S(1)} %get-tuple-element.30), channel_id=1, source_target_pairs={{0,17},{1,16},{2,19},{3,18},{4,21},{5,20},{6,23},{7,22},{8,25},{9,... | collective-permute-start | bytes 245768 | tf_op jit(solution)/shard_map/ppermute | solution.py:254
  48.7 5.2 %collective-permute-start.18 = (f32[32,640]{1,0:T(8,128)S(1)}, f32[32,640]{1,0:T(8,128)S(1)}, u32[]{:S(2)}, u32[]{:S(2)}) collective-permute-start(f32[32,640]{1,0:T(8,128)S(1)} %get-tuple-element.31), channel_id=1, source_target_pairs={{0,16},{1,17},{2,18},{3,19},{4,20},{5,21},{6,22},{7,23},{8,9},{9,8... | collective-permute-start | bytes 245768 | tf_op jit(solution)/shard_map/ppermute | solution.py:254
  49.2 4.7 %collective-permute-start.19 = (f32[32,640]{1,0:T(8,128)S(1)}, f32[32,640]{1,0:T(8,128)S(1)}, u32[]{:S(2)}, u32[]{:S(2)}) collective-permute-start(f32[32,640]{1,0:T(8,128)S(1)} %get-tuple-element.32), channel_id=1, source_target_pairs={{0,1},{1,0},{2,3},{3,2},{4,5},{5,4},{6,7},{7,6},{8,24},{9,25},{10,... | collective-permute-start | bytes 245768 | tf_op jit(solution)/shard_map/ppermute | solution.py:254
